TPU v7x, 128 devices: a whole 4x4x4 slice. The times are simulated.
128 devices in a mesh: row: 8 (over x_lo, z), col: 16 (over y, x_hi, core).
Axes of the slice: x: 4 (x_hi: 2, x_lo: 2; x = x_hi * 2 + x_lo), y: 4, z: 4, core: 2. Of those that a mesh axis runs over, the one named last changes fastest.
Arguments:
- pair_act: bfloat16 [2048, 2048, 128], P('row', 'col'), may hold values from -6 to 6
- atom_act: bfloat16 [16384, 128], P(('row', 'col')), may hold values from -6 to 6
- atom_token: int32 [16384], P(('row', 'col')), may hold values from 0 to 2047, as said below
- atom_gain: float32 [128], replicated, may hold values from 0.1 to 1.9
- w_attn: bfloat16 [128, 512], replicated, may hold values from -0.5 to 0.5
- w_out: bfloat16 [128, 128], replicated, may hold values from -0.5 to 0.5
- w_bias: bfloat16 [128, 4], replicated, may hold values from -9.722718 to 9.722718
- w_trans_in: bfloat16 [128, 1024], replicated, may hold values from -0.5 to 0.5
- w_trans_out: bfloat16 [512, 128], replicated, may hold values from -0.25 to 0.25
- w_agg: bfloat16 [128, 384], replicated, may hold values from -0.5 to 0.5
- w_single: bfloat16 [384, 256], replicated, may hold values from -0.3125 to 0.3125
Outputs:
- atom_out: bfloat16 [16384, 128], P(('row', 'col'))
- token_single: bfloat16 [2048, 384], P(('row', 'col'))
- pair_out: bfloat16 [2048, 2048, 128], P('row', 'col')
Inputs may be any that keep to these rules, and one draw needn't show every extreme that they name: `atom_token`: non-decreasing; token 0 begins at atom 0, and the first atom of every other token t lies between atoms 8 t and 8 t + 4, and between 8 t + 1 and 8 t + 4 where t is a positive multiple of 16; so every token has 4 to 12 atoms, atom i belongs to a token from 16 * (i // 128) - 1 to 16 * (i // 128) + 15, and a query atom and each of its keys belong to tokens at most 10 apart.
All inputs are finite; a program needn't handle non-finite values.
Results may differ from a plain program's by a relative error of at most 0.0075.
Values may be sent and summed in bfloat16 or wider, within the bound.
No kernel may reach another device: no remote copies, remote signals or barrier semaphores. Data moves between devices by JAX's collectives and lax.ppermute only.
A program may use at most 128 MiB of HBM per device.

v0:
```python
import math

import jax
import jax.numpy as jnp
from jax import lax
from jax.sharding import PartitionSpec as P

QB = 32
KW = 128
SPAN = 10


def passed_along(value, axis, steps):
    count = lax.axis_size(axis)
    initial, last = (max(0, -steps), min(count, count - steps))
    return lax.ppermute(value, axis, [(source, source + steps) for source in range(initial, last)])


def with_halo(cells, sides, width):
    for axis, dim in sides:
        count = lax.axis_size(axis)
        ends = count - 1
        head = lax.slice_in_dim(cells, 0, width, axis=dim)
        tail = lax.slice_in_dim(cells, cells.shape[dim] - width, cells.shape[dim], axis=dim)
        cells = jnp.concatenate(
            [
                lax.ppermute(tail, axis, [(i, (i + 1) % count) for i in range(ends)]),
                cells,
                lax.ppermute(head, axis, [((i + 1) % count, i) for i in range(ends)]),
            ],
            axis=dim,
        )
    return cells


def normalize(values):
    centre = values - jnp.mean(values, axis=-1, keepdims=True)
    spread = jnp.mean(centre * centre, axis=-1, keepdims=True)
    return centre * lax.rsqrt(spread + 1e-05)


def band_slice(pair_line, offset):
    return lax.dynamic_slice_in_dim(pair_line, offset, 2 * SPAN + 1, 0)


def on_device(
    pair_act,
    atom_act,
    atom_token,
    atom_gain,
    w_attn,
    w_out,
    w_bias,
    w_trans_in,
    w_trans_out,
    w_agg,
    w_single,
):
    rows_n, cols_n, pair_width = pair_act.shape
    atom_n, atom_width = atom_act.shape
    heads = w_bias.shape[1]
    head_dim = atom_width // heads
    trans_width = w_trans_out.shape[0]
    tok_dev = atom_n // 8
    n_col = lax.axis_size("col")
    row_index = lax.axis_index("row")
    col_index = lax.axis_index("col")
    flat_index = row_index * n_col + col_index
    total_atoms = atom_n * lax.axis_size("row") * n_col
    base_token = flat_index * tok_dev - 1
    band_cols = 2 * SPAN + 1
    normed_pair = normalize(
        pair_act.reshape(rows_n * cols_n, pair_width).astype(jnp.float32)
    ).astype(jnp.bfloat16)
    block_rows = math.gcd(rows_n, max(1, 2048 // cols_n))
    steps_n = rows_n // block_rows
    pair_blocks = pair_act.reshape(steps_n, block_rows * cols_n, pair_width)
    normed_blocks = normed_pair.reshape(steps_n, block_rows * cols_n, pair_width)

    def transition(pieces):
        pair_rows, normed_rows = pieces
        hidden_pre = jnp.dot(normed_rows, w_trans_in, preferred_element_type=jnp.float32)
        hidden = (jax.nn.silu(hidden_pre[:, :trans_width]) * hidden_pre[:, trans_width:]).astype(
            jnp.bfloat16
        )
        return pair_rows.astype(jnp.float32) + jnp.dot(
            hidden, w_trans_out, preferred_element_type=jnp.float32
        )

    tile_bias = jnp.dot(normed_pair, w_bias, preferred_element_type=jnp.float32).astype(
        jnp.bfloat16
    )
    tile_bias = tile_bias.reshape(rows_n, cols_n, heads)
    padded = jnp.pad(tile_bias, ((0, 0), (band_cols, band_cols), (0, 0)))
    starts = (
        row_index * rows_n
        + jnp.arange(rows_n, dtype=jnp.int32)
        - SPAN
        - col_index * cols_n
        + band_cols
    )
    starts = jnp.clip(starts, 0, cols_n + band_cols)
    pair_band = jax.vmap(band_slice)(padded, starts)
    pair_band = jnp.transpose(pair_band, (0, 2, 1)).reshape(rows_n, heads * band_cols)
    own_band = lax.psum_scatter(
        pair_band.astype(jnp.float32).astype(jnp.bfloat16), "col", scatter_dimension=0, tiled=True
    )
    lower_band = passed_along(own_band[-1:], ("row", "col"), 1)
    near_band = jnp.concatenate([lower_band, own_band], axis=0).reshape(
        tok_dev + 1, heads, band_cols
    )
    atom_float = atom_act.astype(jnp.float32)
    normed_atoms = (normalize(atom_float) * atom_gain).astype(jnp.bfloat16)
    queries = jnp.dot(
        normed_atoms, w_attn[:, :atom_width], preferred_element_type=jnp.float32
    ).astype(jnp.bfloat16)
    gating = jax.nn.sigmoid(
        jnp.dot(normed_atoms, w_attn[:, 3 * atom_width :], preferred_element_type=jnp.float32)
    )
    query_rel = atom_token - base_token
    token_rel = query_rel.astype(jnp.bfloat16)
    key_margin = (KW - QB) // 2
    pair_kv = jnp.dot(
        normed_atoms, w_attn[:, atom_width : 3 * atom_width], preferred_element_type=jnp.float32
    ).astype(jnp.bfloat16)
    wide_kv, wide_rel = (
        with_halo(pair_kv, ((("row", "col"), 0),), key_margin),
        with_halo(token_rel, ((("row", "col"), 0),), key_margin),
    )
    rel_shift = jnp.concatenate(
        [
            jnp.full((key_margin,), -tok_dev, jnp.float32),
            jnp.zeros((atom_n,), jnp.float32),
            jnp.full((key_margin,), tok_dev, jnp.float32),
        ]
    )
    key_rel = (wide_rel.astype(jnp.float32) + rel_shift).astype(jnp.int32)
    blocks = atom_n // QB
    window = (jnp.arange(blocks, dtype=jnp.int32) * QB)[:, None] + jnp.arange(KW, dtype=jnp.int32)[
        None, :
    ]
    global_key = flat_index * atom_n - key_margin + window
    usable = (global_key >= 0) & (global_key < total_atoms)
    key_window = wide_kv[window]
    key_heads = key_window[:, :, :atom_width].reshape(blocks, KW, heads, head_dim)
    value_heads = key_window[:, :, atom_width:].reshape(blocks, KW, heads, head_dim)
    query_heads = queries.reshape(blocks, QB, heads, head_dim)
    scores = jnp.einsum(
        "bqhd,bkhd->bhqk", query_heads, key_heads, preferred_element_type=jnp.float32
    ) * (1.0 / math.sqrt(head_dim))
    query_slot = query_rel.reshape(blocks, QB)
    band_offset = key_rel[window][:, None, :] - query_slot[:, :, None] + SPAN
    key_bias = near_band[query_slot[:, :, None], :, band_offset].astype(jnp.float32)
    scores = scores + jnp.transpose(key_bias, (0, 3, 1, 2))
    scores = jnp.where(usable[:, None, None, :], scores, -jnp.inf)
    row_max = jnp.max(scores, axis=-1, keepdims=True)
    exponent = jnp.exp(scores - row_max)
    weights = (exponent / jnp.sum(exponent, axis=-1, keepdims=True)).astype(jnp.bfloat16)
    attended = jnp.einsum(
        "bhqk,bkhd->bqhd", weights, value_heads, preferred_element_type=jnp.float32
    ).reshape(atom_n, atom_width)
    attended = (gating * attended).astype(jnp.bfloat16)
    atom_out = (atom_float + jnp.dot(attended, w_out, preferred_element_type=jnp.float32)).astype(
        jnp.bfloat16
    )
    features = jax.nn.relu(jnp.dot(atom_out, w_agg, preferred_element_type=jnp.float32))
    token_slots = jnp.arange(tok_dev + 1, dtype=jnp.int32)
    member = (query_rel[:, None] == token_slots[None, :]).astype(jnp.float32)
    local_totals = jnp.dot(
        member.T, features, precision=lax.Precision.HIGHEST, preferred_element_type=jnp.float32
    )
    local_counts = jnp.sum(member, axis=0)
    upper_totals, upper_counts = passed_along(
        (local_totals[:1], local_counts[:1]), ("row", "col"), -1
    )
    totals = local_totals[1:].at[-1].add(upper_totals[0])
    counts = local_counts[1:].at[-1].add(upper_counts[0])
    token_single = (totals / counts[:, None]).astype(jnp.bfloat16)
    singles = jnp.dot(token_single, w_single, preferred_element_type=jnp.float32)
    row_part = singles[:, :pair_width].astype(jnp.bfloat16)
    col_part = singles[:, pair_width:].astype(jnp.bfloat16)
    row_all = lax.all_gather(row_part, "col", axis=0, tiled=True)
    col_all = lax.all_gather(col_part, ("row", "col"), axis=0, tiled=True)
    col_tile = lax.dynamic_slice_in_dim(col_all, col_index * cols_n, cols_n, 0)
    row_blocks = row_all.reshape(steps_n, block_rows, pair_width)

    def finish(pieces):
        pair_rows, normed_rows, row_extra = pieces
        moved = transition((pair_rows, normed_rows)).reshape(block_rows, cols_n, pair_width)
        moved = moved + row_extra.astype(jnp.float32)[:, None, :]
        return (moved + col_tile.astype(jnp.float32)[None, :, :]).astype(jnp.bfloat16)

    pair_out = lax.map(finish, (pair_blocks, normed_blocks, row_blocks)).reshape(
        rows_n, cols_n, pair_width
    )
    return (atom_out, token_single, pair_out)


def solution(mesh):
    return jax.shard_map(
        on_device,
        mesh=mesh,
        in_specs=(
            P("row", "col", None),
            P(("row", "col"), None),
            P(("row", "col")),
            P(),
            P(),
            P(),
            P(),
            P(),
            P(),
            P(),
            P(),
        ),
        out_specs=(P(("row", "col"), None), P(("row", "col"), None), P("row", "col", None)),
        check_vma=False,
    )
```

profile of v0, /device:TPU:1, one launch (start us, length us, event | category | flops | bytes accessed | tf_op | source)
XLA Modules:
  0.0 605.6 jit_solution(4856616157540320213)
XLA Ops:
  8.0 6.0 collective-permute-start.3
  14.0 1.9 collective-permute-start.4
  16.0 5.8 convert_reduce_fusion
  21.8 10.9 %multiply_reduce_fusion = f32[256,128]{1,0:T(8,128)S(1)} fusion(bf16[256,128,128]{2,1,0:T(8,128)(2,1)} %param.17, f32[256,128]{1,0:T(8,128)S(1)} %get-tuple-element.93), kind=kLoop, calls=%fused_computation.21 | loop fusion | flops 16744448 | bytes 8650752 | tf_op jit(solution)/shard_map/reduce_sum | solution.py:38
  32.8 9.9 %fusion.10 = bf16[32768,128]{1,0:T(8,128)(2,1)S(1)} fusion(bf16[256,128,128]{2,1,0:T(8,128)(2,1)S(1)} %bitcast.84, f32[32768]{0:T(1024)S(1)} %get-tuple-element.91, f32[32768]{0:T(1024)S(1)} %get-tuple-element.92), kind=kLoop, calls=%fused_computation.19 | loop fusion | flops 16777216 | bytes 17039360 | tf_op jit(solution)/shard_map/convert_element_type | solution.py:74
  42.7 2.3 fusion.15
  45.0 6.5 %copy.53 = bf16[256,128,4]{2,0,1:T(8,128)(2,1)} copy(bf16[256,128,4]{1,0,2:T(8,128)(2,1)S(1)} %bitcast.88) | data formatting | bytes 524288 | tf_op jit(solution)/shard_map/reshape | solution.py:93
  51.5 9.9 %pad.9 = bf16[256,170,4]{2,0,1:T(8,128)(2,1)} pad(bf16[256,128,4]{2,0,1:T(8,128)(2,1)} %copy.53, bf16[]{:T(256)} %constant.129.clone.1), padding=0_0x21_21x0_0 | pad | bytes 610306 | tf_op jit(solution)/shard_map/jit(_pad)/pad | solution.py:94
  61.4 6.0 gather_fusion.3
  69.4 5.2 collective-permute-start
  74.5 1.9 collective-permute-start.1
  76.6 2.1 collective-permute-start.6
  79.4 12.1 %multiply_convert_fusion = bf16[16,2048,128]{2,1,0:T(8,128)(2,1)} fusion(f32[16,2048]{1,0:T(8,128)S(1)} %rsqrt.26, f32[16,2048]{1,0:T(8,128)S(1)} %div.49, bf16[16,2048,128]{2,1,0:T(8,128)(2,1)} %bitcast.81), kind=kLoop, calls=%fused_computation.20 | loop fusion | flops 16777216 | bytes 17039360 | tf_op jit(solution)/shard_map/convert_element_type | solution.py:74
  91.7 3.5 gather_fusion.1
  95.3 2.0 gather_fusion
  97.3 33.7 %reduce-scatter.4.cloned.1.call-done = bf16[16,84]{1,0:T(8,128)(2,1)} async-done(((bf16[256,84]{1,0:T(8,128)(2,1)}), bf16[16,84]{1,0:T(8,128)(2,1)}) %reduce-scatter.4.cloned.1.call-update) | async-done | bytes 2704 | tf_op jit(solution)/shard_map/reduce_scatter | solution.py:105
  131.8 6.5 %collective-permute-start.2 = (bf16[1,84]{0,1:T(8,128)(2,1)S(1)}, bf16[1,84]{0,1:T(8,128)(2,1)S(1)}, u32[]{:S(2)}, u32[]{:S(2)}) collective-permute-start(bf16[1,84]{0,1:T(8,128)(2,1)S(1)} %copy.65), channel_id=1, source_target_pairs={{0,1},{1,2},{2,3},{3,4},{4,5},{5,6},{6,7},{7,8},{8,9},{9,10},{10,1... | collective-permute-start | bytes 512 | tf_op jit(solution)/shard_map/ppermute | solution.py:16
  140.3 160.6 %gather_fusion.2 = bf16[16384,4]{1,0:T(8,128)(2,1)} fusion(bf16[17,4,21]{1,2,0:T(8,128)(2,1)S(1)} %copy.57, s32[16384]{0:T(1024)S(1)} %bitcast.80), kind=kCustom, calls=%fused_computation.2 | custom fusion | bytes 393216 | tf_op jit(solution)/shard_map/gather | solution.py:153
  301.0 3.9 copy.68
  307.4 1.9 collective-permute-start.5
  310.1 4.2 collective-permute-done.5
  314.6 174.8 %all_gather.7 = bf16[2048,128]{1,0:T(8,128)(2,1)S(1)} all-gather(bf16[16,128]{1,0:T(8,128)(2,1)S(1)} %get-tuple-element.96), channel_id=1, replica_groups=mesh['row'=8,'col'=16] {'row','col'}, dimensions={0}, use_global_device_ids=true | all-gather | bytes 528384 | tf_op jit(solution)/shard_map/all_gather | solution.py:183
  489.4 19.5 %all_gather.6 = bf16[256,128]{1,0:T(8,128)(2,1)S(1)} all-gather(bf16[16,128]{1,0:T(8,128)(2,1)S(1)} %get-tuple-element.97), channel_id=1, replica_groups=mesh['row'=8,'col'=16] {'col'}, dimensions={0}, use_global_device_ids=true | all-gather | bytes 69632 | tf_op jit(solution)/shard_map/all_gather | solution.py:182
  509.0 88.8 %while.12 = (s32[]{:T(128)}, bf16[16,16,128,128]{3,2,1,0:T(8,128)(2,1)}, bf16[16,2048,128]{2,1,0:T(8,128)(2,1)}, bf16[16,2048,128]{2,1,0:T(8,128)(2,1)}, bf16[12...) while((s32[]{:T(128)}, ...), condition=%wide.region_9.10_spmd, body=%wide.region_8.9_spmd.sunk | while | flops 812926976 | bytes 21025892 | solution.py:193
  509.0 2.3 fusion.86
  511.3 2.3 convolution_add_fusion.3
  513.6 1.0 fusion.87
  514.5 2.3 fusion.86
  516.8 2.3 convolution_add_fusion.3
  519.1 1.0 fusion.87
  520.1 2.3 fusion.86
  522.4 2.3 convolution_add_fusion.3
  524.7 1.0 fusion.87
  525.6 2.3 fusion.86
  527.9 2.3 convolution_add_fusion.3
  530.2 1.0 fusion.87
  531.2 2.3 fusion.86
  533.5 2.3 convolution_add_fusion.3
  535.8 1.0 fusion.87
  536.7 2.3 fusion.86
  539.0 2.3 convolution_add_fusion.3
  541.3 1.0 fusion.87
  542.3 2.3 fusion.86
  544.6 2.3 convolution_add_fusion.3
  546.9 1.0 fusion.87
  547.8 2.3 fusion.86
  550.1 2.3 convolution_add_fusion.3
  553.4 2.3 fusion.86
  555.7 2.3 convolution_add_fusion.3
  558.9 2.3 fusion.86
  561.2 2.3 convolution_add_fusion.3
  564.5 2.3 fusion.86
  566.8 2.3 convolution_add_fusion.3
  570.0 2.3 fusion.86
  572.3 2.3 convolution_add_fusion.3
  575.6 2.3 fusion.86
  577.9 2.3 convolution_add_fusion.3
  581.1 2.3 fusion.86
  583.4 2.3 convolution_add_fusion.3
  585.7 1.0 fusion.87
  586.7 2.3 fusion.86
  589.0 2.3 convolution_add_fusion.3
  592.2 2.3 fusion.86
  594.5 2.3 convolution_add_fusion.3
  (137 shorter events, 19.0 us)
Async XLA Ops:
  7.2 307.3 %copy-start = (bf16[384,256]{1,0:T(8,128)(2,1)S(1)}, bf16[384,256]{1,0:T(8,128)(2,1)}, u32[]{:S(2)}) copy-start(bf16[384,256]{1,0:T(8,128)(2,1)} %param.27) | copy-start | bytes 589828
  7.2 123.9 %reduce-scatter.4.cloned.1.call-start = ((), (), s32[]{:S(2)}) async-start(), calls=%async_computation.1 | async-start | bytes 69632 | tf_op jit(solution)/shard_map/reduce_scatter | solution.py:105
  8.0 83.6 %collective-permute-start.3 = (bf16[48]{0:T(256)(128)(2,1)S(1)}, bf16[48]{0:T(256)(128)(2,1)S(1)}, u32[]{:S(2)}, u32[]{:S(2)}) collective-permute-start(bf16[48]{0:T(256)(128)(2,1)S(1)} %get-tuple-element.98), channel_id=1, source_target_pairs={{0,1},{1,2},{2,3},{3,4},{4,5},{5,6},{6,7},{7,8},{8,9},{9,10},{10,1... | collective-permute-start | bytes 296 | tf_op jit(solution)/shard_map/ppermute | solution.py:27
  14.0 77.5 %collective-permute-start.4 = (bf16[48]{0:T(256)(128)(2,1)S(1)}, bf16[48]{0:T(256)(128)(2,1)S(1)}, u32[]{:S(2)}, u32[]{:S(2)}) collective-permute-start(bf16[48]{0:T(256)(128)(2,1)S(1)} %get-tuple-element.99), channel_id=1, source_target_pairs={{1,0},{2,1},{3,2},{4,3},{5,4},{6,5},{7,6},{8,7},{9,8},{10,9},{11,1... | collective-permute-start | bytes 296 | tf_op jit(solution)/shard_map/ppermute | solution.py:29
  16.0 16.8 %slice-start = ((s8[8388608]{0:T(1024)(128)(4,1)}), s8[4194304]{0:T(1024)(128)(4,1)S(1)}, s32[]{:S(2)}) async-start(s8[8388608]{0:T(1024)(128)(4,1)} %bitcast.83), calls=%async_computation.2 | async-start | bytes 8388608
  21.8 10.9 %slice-start.1 = ((s8[8388608]{0:T(1024)(128)(4,1)}), s8[4194304]{0:T(1024)(128)(4,1)S(1)}, s32[]{:S(2)}) async-start(s8[8388608]{0:T(1024)(128)(4,1)} %bitcast.83), calls=%async_computation.3 | async-start | bytes 8388608
  32.8 9.9 %copy-start.7 = (bf16[128,4]{0,1:T(4,128)(2,1)S(1)}, bf16[128,4]{0,1:T(4,128)(2,1)}, u32[]{:S(2)}) copy-start(bf16[128,4]{0,1:T(4,128)(2,1)} %param.23) | copy-start | bytes 3076
  61.4 7.4 %copy-start.3 = (bf16[128,128]{1,0:T(8,128)(2,1)S(1)}, bf16[128,128]{1,0:T(8,128)(2,1)}, u32[]{:S(2)}) copy-start(bf16[128,128]{1,0:T(8,128)(2,1)} %param.18) | copy-start | bytes 98308
  61.4 7.7 %copy-start.9 = (bf16[128,512]{1,0:T(8,128)(2,1)S(1)}, bf16[128,512]{1,0:T(8,128)(2,1)}, u32[]{:S(2)}) copy-start(bf16[128,512]{1,0:T(8,128)(2,1)} %param.21) | copy-start | bytes 393220
  61.4 7.7 %copy-start.12 = (f32[128]{0:T(128)S(1)}, f32[128]{0:T(128)}, u32[]{:S(2)}) copy-start(f32[128]{0:T(128)} %param.20) | copy-start | bytes 1540
  69.4 25.9 %collective-permute-start = (bf16[48,256]{1,0:T(8,128)(2,1)S(1)}, bf16[48,256]{1,0:T(8,128)(2,1)S(1)}, u32[]{:S(2)}, u32[]{:S(2)}) collective-permute-start(bf16[48,256]{1,0:T(8,128)(2,1)S(1)} %get-tuple-element.94), channel_id=1, source_target_pairs={{0,1},{1,2},{2,3},{3,4},{4,5},{5,6},{6,7},{7,8},{8,9},{9,10},{10,1... | collective-permute-start | bytes 73736 | tf_op jit(solution)/shard_map/ppermute | solution.py:27
  74.5 20.8 %collective-permute-start.1 = (bf16[48,256]{1,0:T(8,128)(2,1)S(1)}, bf16[48,256]{1,0:T(8,128)(2,1)S(1)}, u32[]{:S(2)}, u32[]{:S(2)}) collective-permute-start(bf16[48,256]{1,0:T(8,128)(2,1)S(1)} %get-tuple-element.95), channel_id=1, source_target_pairs={{1,0},{2,1},{3,2},{4,3},{5,4},{6,5},{7,6},{8,7},{9,8},{10,9},{11,1... | collective-permute-start | bytes 73736 | tf_op jit(solution)/shard_map/ppermute | solution.py:29
  76.6 232.7 %collective-permute-start.6 = (f32[1]{0:T(128)S(1)}, f32[1]{0:T(128)}, u32[]{:S(2)}, u32[]{:S(2)}) collective-permute-start(f32[1]{0:T(128)S(1)} %bitcast.96), channel_id=1, source_target_pairs={{1,0},{2,1},{3,2},{4,3},{5,4},{6,5},{7,6},{8,7},{9,8},{10,9},{11,1... | collective-permute-start | bytes 20 | tf_op jit(solution)/shard_map/ppermute | solution.py:16
  79.4 12.2 %copy-start.8 = (f32[224]{0:T(256)S(1)}, f32[224]{0:T(256)}, u32[]{:S(2)}) copy-start(f32[224]{0:T(256)} %constant.137.clone.1) | copy-start | bytes 2692
  131.8 7.4 %collective-permute-start.2 = (bf16[1,84]{0,1:T(8,128)(2,1)S(1)}, bf16[1,84]{0,1:T(8,128)(2,1)S(1)}, u32[]{:S(2)}, u32[]{:S(2)}) collective-permute-start(bf16[1,84]{0,1:T(8,128)(2,1)S(1)} %copy.65), channel_id=1, source_target_pairs={{0,1},{1,2},{2,3},{3,4},{4,5},{5,6},{6,7},{7,8},{8,9},{9,10},{10,1... | collective-permute-start | bytes 512 | tf_op jit(solution)/shard_map/ppermute | solution.py:16
  140.3 166.3 %copy-start.11 = (bf16[128,128]{1,0:T(8,128)(2,1)S(1)}, bf16[128,128]{1,0:T(8,128)(2,1)}, u32[]{:S(2)}) copy-start(bf16[128,128]{1,0:T(8,128)(2,1)} %param.22) | copy-start | bytes 98308
  301.0 6.0 copy-start.4
  301.0 208.0 %copy-start.2 = (bf16[128,1024]{1,0:T(8,128)(2,1)S(1)}, bf16[128,1024]{1,0:T(8,128)(2,1)}, u32[]{:S(2)}) copy-start(bf16[128,1024]{1,0:T(8,128)(2,1)} %param.24) | copy-start | bytes 786436
  301.0 208.0 %copy-start.10 = (bf16[512,128]{1,0:T(8,128)(2,1)S(1)}, bf16[512,128]{1,0:T(8,128)(2,1)}, u32[]{:S(2)}) copy-start(bf16[512,128]{1,0:T(8,128)(2,1)} %param.25) | copy-start | bytes 393220
  307.0 201.9 %copy-start.6 = (bf16[128,128]{1,0:T(8,128)(2,1)}, bf16[128,128]{1,0:T(8,128)(2,1)S(1)}, u32[]{:S(2)}) copy-start(bf16[128,128]{1,0:T(8,128)(2,1)S(1)} %fusion.21) | copy-start | bytes 98308
  307.4 7.0 %collective-permute-start.5 = (f32[1,384]{1,0:T(1,128)S(1)}, f32[1,384]{1,0:T(1,128)S(1)}, u32[]{:S(2)}, u32[]{:S(2)}) collective-permute-start(f32[1,384]{1,0:T(1,128)S(1)} %slice.125), channel_id=1, source_target_pairs={{1,0},{2,1},{3,2},{4,3},{5,4},{6,5},{7,6},{8,7},{9,8},{10,9},{11,1... | collective-permute-start | bytes 4616 | tf_op jit(solution)/shard_map/ppermute | solution.py:16
  314.5 194.5 %copy-start.5 = (bf16[16,384]{1,0:T(8,128)(2,1)}, bf16[16,384]{1,0:T(8,128)(2,1)S(1)}, u32[]{:S(2)}) copy-start(bf16[16,384]{1,0:T(8,128)(2,1)S(1)} %divide_convert_fusion.2) | copy-start | bytes 36868
  597.8 0.9 copy-start.1
Sparse Core Ops, SparseCore 0:
  68.9 62.0 reduce-scatter.3
where the time goes:
time: 608 us; the launch traced here: 606 us
  local copies, waits for them, and re-layouts  197 us (32%)
  blocking collectives  194 us (32%)
  matrix products  77.5 us (13%)
  other arithmetic  57.5 us (9%)
  waiting for transfers between devices  38.6 us (6%)
  starting transfers between devices  25.6 us (4%)
  between operations  14.6 us (2%)
    all_gather x1, blocking collectives, on_device(): col_all = lax.all_gather(col_part, ('row', 'col'), axis=0, tiled=True)  175 us
    gather x1, local copies, waits for them, and re-layouts, on_device(): near_band[query_slot[:, :, None], :, band_offset].astype(jnp.float32)  161 us
    dot_general x16, matrix products, transition(): jnp.dot(hidden, w_trans_out, preferred_element_type=jnp.float32)  36.5 us
    dot_general x16, matrix products, transition(): jnp.dot(normed_rows, w_trans_in, preferred_element_type=jnp.float32)  36.4 us
    reduce_scatter x1, waiting for transfers between devices, on_device(): lax.psum_scatter(pair_band.astype(jnp.float32).astype(jnp.bfloat16), 'col...  33.7 us
    convert_element_type x2, other arithmetic, on_device(): normed_pair = normalize(pair_act.reshape(rows_n * cols_n, pair_width).ast...  22 us
    all_gather x1, blocking collectives, on_device(): row_all = lax.all_gather(row_part, 'col', axis=0, tiled=True)  19.5 us
    dynamic_update_slice x16, other arithmetic, on_device(): lax.map(finish, (pair_blocks, normed_blocks, row_blocks))  15.3 us
  transfers between devices with their start and end apart: 8, of which 3 were waited for; matrix products, arithmetic and copies ran while one was open for 40% of the time, Pallas kernels for 0%

commit v1 on v0

v1 whole, which is shorter than its diff:
```python
import functools
import math

import jax
import jax.numpy as jnp
from jax import lax
from jax.experimental import pallas as pl
from jax.experimental.pallas import tpu as pltpu
from jax.sharding import PartitionSpec as P

SPAN = 10
QB = 32
KW = 128
TOK_DEV = 16
BELOW = (KW - QB) // 2
ABOVE = KW - BELOW
WINDOW = 64
GROUPS = 9
BAND_ROWS = 32
VMEM_BYTES = 56 * 1024 * 1024


def normalize(values):
    centre = values - jnp.mean(values, axis=-1, keepdims=True)
    spread = jnp.mean(centre * centre, axis=-1, keepdims=True)
    return centre * lax.rsqrt(spread + 1e-05)


def dot(a, b, **kw):
    return jnp.dot(a, b, preferred_element_type=jnp.float32, **kw)


def dot_nt(a, b):
    return lax.dot_general(a, b, (((1,), (1,)), ((), ())), preferred_element_type=jnp.float32)


def band_kernel(place_ref, pair_ref, weight_ref, out_ref, cells, rows_scr, sems):
    row, col = place_ref[0], place_ref[1]
    shift = col - 2 * row
    first = jnp.clip(8 * shift - 1, 0, 7)
    pieces = WINDOW // 16
    copies = []
    for j in range(GROUPS):
        group = first + j
        start = group - 8 * shift - 1
        mine = []
        for t in range(pieces):
            piece = jnp.clip(start + t, 0, 7)
            copy = pltpu.make_async_copy(
                pair_ref.at[
                    pl.ds(pl.multiple_of(group * 16, 16), 16),
                    pl.ds(pl.multiple_of(piece * 16, 16), 16),
                    :,
                ],
                cells.at[j, :, pl.ds(16 * t, 16), :],
                sems.at[j, t],
            )
            copy.start()
            mine.append(copy)
        copies.append(mine)
    out_ref[...] = jnp.zeros_like(out_ref)
    lane_piece = (lax.broadcasted_iota(jnp.int32, (BAND_ROWS, 128), 1) % WINDOW) // 16
    for j in range(GROUPS):
        group = first + j
        start = group - 8 * shift - 1
        for copy in copies[j]:
            copy.wait()
        flat = cells[j].reshape(16 * WINDOW, 128)
        normed = normalize(flat.astype(jnp.float32)).astype(jnp.bfloat16)
        biases = dot_nt(weight_ref[...], normed)
        for i in range(8):
            rows_scr[j, 4 * i : 4 * i + 4, :] = biases[0:4, 128 * i : 128 * (i + 1)]
        at = start + lane_piece
        kept = jnp.where((at >= 0) & (at <= 7), rows_scr[j], 0.0)
        out_ref[pl.ds(group, 1)] = kept.astype(jnp.bfloat16)[None]


def band_biases(place, pair_act, w_bias):
    n_col = 16
    weight = jnp.zeros((16, 128), jnp.bfloat16).at[:4].set(w_bias.T)
    return pl.pallas_call(
        band_kernel,
        in_specs=[
            pl.BlockSpec(memory_space=pltpu.SMEM),
            pl.BlockSpec(memory_space=pl.ANY),
            pl.BlockSpec(memory_space=pltpu.VMEM),
        ],
        out_specs=pl.BlockSpec(memory_space=pltpu.VMEM),
        out_shape=jax.ShapeDtypeStruct((n_col, BAND_ROWS, 128), jnp.bfloat16),
        scratch_shapes=[
            pltpu.VMEM((GROUPS, 16, WINDOW, 128), jnp.bfloat16),
            pltpu.VMEM((GROUPS, BAND_ROWS, 128), jnp.float32),
            pltpu.SemaphoreType.DMA((GROUPS, WINDOW // 16)),
        ],
        cost_estimate=pl.CostEstimate(flops=10**9, bytes_accessed=3 * 10**6, transcendentals=0),
        compiler_params=pltpu.CompilerParams(vmem_limit_bytes=VMEM_BYTES),
        name="band",
    )(place, pair_act, weight)


def atom_kernel(
    place_ref, below_ref, own_ref, above_ref, tok_ref, band_ref, gain_ref, wattn_ref, wout_ref,
    wagg_ref, wsingle_ref, atom_out_ref, next_out_ref, token_ref, singles_ref,
    wide, q_scr, k_scr, v_scr, gate_scr,
):
    flat = place_ref[2]
    atoms = own_ref.shape[0]
    heads = 4
    n_query = atoms + QB
    total = place_ref[3]
    wide[0:BELOW, :] = below_ref[0:BELOW, :].astype(jnp.float32)
    wide[BELOW : BELOW + atoms, :] = own_ref[...].astype(jnp.float32)
    wide[BELOW + atoms :, :] = above_ref[0:ABOVE, :].astype(jnp.float32)
    normed = (normalize(wide[...]) * gain_ref[...]).astype(jnp.bfloat16)
    projected = dot(normed, wattn_ref[...])
    q_scr[...] = projected[BELOW : BELOW + n_query, 0:128].astype(jnp.bfloat16)
    k_scr[...] = projected[:, 128:256].astype(jnp.bfloat16)
    v_scr[...] = projected[:, 256:384].astype(jnp.bfloat16)
    gate_scr[...] = jax.nn.sigmoid(projected[BELOW : BELOW + n_query, 384:512])

    tok_own = tok_ref[0:1, :].astype(jnp.float32)
    tok_below = below_ref[BELOW : BELOW + 16, :].astype(jnp.float32)[0:1] - TOK_DEV
    tok_above = above_ref[ABOVE : ABOVE + 16, :].astype(jnp.float32)[0:1] + TOK_DEV
    lane = lax.broadcasted_iota(jnp.int32, (8, 128), 1)
    rolled_own = pltpu.roll(jnp.broadcast_to(tok_own, (8, 128)), BELOW, 1)
    rolled_below = pltpu.roll(jnp.broadcast_to(tok_below, (8, 128)), BELOW, 1)
    rolled_above = pltpu.roll(jnp.broadcast_to(tok_above, (8, 128)), BELOW, 1)
    key_tok = jnp.concatenate(
        [
            jnp.where(lane < BELOW, rolled_below, rolled_own)[0:1],
            jnp.where(lane < BELOW, rolled_own, rolled_above)[0:1],
        ],
        axis=1,
    )
    col_own = jnp.transpose(jnp.broadcast_to(tok_own, (128, 128)))
    col_above = jnp.transpose(jnp.broadcast_to(tok_above, (128, 128)))

    band = jnp.sum(band_ref[...].astype(jnp.float32), axis=0)
    half = lax.broadcasted_iota(jnp.int32, (BAND_ROWS, 128), 1) < WINDOW
    band = jnp.concatenate([jnp.where(half, band, 0.0), jnp.where(half, 0.0, band)], axis=0)
    slot = (lax.broadcasted_iota(jnp.int32, (128, 256), 0) % WINDOW - 16).astype(jnp.float32)
    pick_key = (slot == key_tok).astype(jnp.bfloat16)
    spread = dot(band.astype(jnp.bfloat16), pick_key).astype(jnp.bfloat16)

    row_head = lax.broadcasted_iota(jnp.int32, (128, 128), 0) // QB
    lane_head = lax.broadcasted_iota(jnp.int32, (128, 128), 1) // 32
    own_head = row_head == lane_head
    entry = lax.broadcasted_iota(jnp.int32, (128, WINDOW), 1)
    entry_tok = (2 * ((entry % 32) // 4) + entry // 32).astype(jnp.float32)
    entry_head = entry % 4 == lax.broadcasted_iota(jnp.int32, (128, WINDOW), 0) // QB
    key_lane = lax.broadcasted_iota(jnp.int32, (128, KW), 1)
    for b in range(n_query // QB):
        at = b * QB
        queries = q_scr[at : at + QB, :]
        stacked = jnp.where(own_head, jnp.concatenate([queries] * heads, axis=0), 0)
        keys = k_scr[at : at + KW, :]
        tok_col = col_own[at : at + QB, 0:WINDOW] if at < atoms else col_above[0:QB, 0:WINDOW]
        pick = (jnp.concatenate([tok_col] * heads, axis=0) == entry_tok) & entry_head
        bias = dot(pick.astype(jnp.bfloat16), spread[:, at : at + KW])
        scores = dot_nt(stacked, keys) * (1.0 / math.sqrt(32)) + bias
        key_index = flat * atoms - BELOW + at + key_lane
        scores = jnp.where((key_index >= 0) & (key_index < total), scores, -jnp.inf)
        exponent = jnp.exp(scores - jnp.max(scores, axis=-1, keepdims=True))
        weights = (exponent / jnp.sum(exponent, axis=-1, keepdims=True)).astype(jnp.bfloat16)
        mixed = jnp.where(own_head, dot(weights, v_scr[at : at + KW, :]), 0.0)
        mixed = (mixed[0:32] + mixed[32:64]) + (mixed[64:96] + mixed[96:128])
        gate_scr[at : at + QB, :] = gate_scr[at : at + QB, :] * mixed
    attended = gate_scr[...].astype(jnp.bfloat16)
    atom_out = (wide[BELOW : BELOW + n_query, :] + dot(attended, wout_ref[...])).astype(
        jnp.bfloat16
    )
    atom_out_ref[...] = atom_out[0:atoms]
    next_out_ref[...] = atom_out[atoms : atoms + 16]
    features = jnp.maximum(dot(atom_out, wagg_ref[...]), 0.0)
    tokens = lax.broadcasted_iota(jnp.int32, (TOK_DEV, 128), 0).astype(jnp.float32)
    member = (tok_own == tokens).astype(jnp.float32)
    member_next = ((tok_above == tokens) & (key_lane[0:TOK_DEV] < QB)).astype(jnp.float32)[:, 0:QB]
    counts = jnp.sum(member, axis=1, keepdims=True) + jnp.sum(member_next, axis=1, keepdims=True)
    totals = dot(member, features[0:atoms], precision=lax.Precision.HIGHEST) + dot(
        member_next, features[atoms:], precision=lax.Precision.HIGHEST
    )
    token_single = (totals / counts).astype(jnp.bfloat16)
    token_ref[...] = token_single
    singles_ref[...] = dot(token_single, wsingle_ref[...]).astype(jnp.bfloat16)


def atom_part(place, below, own, above, tok_rows, band, atom_gain, w_attn, w_out, w_agg, w_single):
    atoms = own.shape[0]
    vmem = pl.BlockSpec(memory_space=pltpu.VMEM)
    return pl.pallas_call(
        atom_kernel,
        in_specs=[pl.BlockSpec(memory_space=pltpu.SMEM)] + [vmem] * 10,
        out_specs=[vmem] * 4,
        out_shape=[
            jax.ShapeDtypeStruct((atoms, 128), jnp.bfloat16),
            jax.ShapeDtypeStruct((16, 128), jnp.bfloat16),
            jax.ShapeDtypeStruct((TOK_DEV, 384), jnp.bfloat16),
            jax.ShapeDtypeStruct((TOK_DEV, 256), jnp.bfloat16),
        ],
        scratch_shapes=[
            pltpu.VMEM((atoms + KW, 128), jnp.float32),
            pltpu.VMEM((atoms + QB, 128), jnp.bfloat16),
            pltpu.VMEM((atoms + KW, 128), jnp.bfloat16),
            pltpu.VMEM((atoms + KW, 128), jnp.bfloat16),
            pltpu.VMEM((atoms + QB, 128), jnp.float32),
        ],
        cost_estimate=pl.CostEstimate(flops=10**9, bytes_accessed=10**6, transcendentals=10**5),
        compiler_params=pltpu.CompilerParams(vmem_limit_bytes=VMEM_BYTES),
        name="atoms",
    )(place, below, own, above, tok_rows, band, atom_gain, w_attn, w_out, w_agg, w_single)


def transition(cells, w_in, w_out):
    width = w_out.shape[0]
    wide = cells.astype(jnp.float32)
    hidden = dot(normalize(wide).astype(jnp.bfloat16), w_in)
    gate = hidden[:, :width].astype(jnp.bfloat16)
    up = hidden[:, width:].astype(jnp.bfloat16)
    return wide + dot((gate + gate * jnp.tanh(gate)) * up, w_out)


ROWS = 16
SUB = 512
PARTS = 4


def part_kernel(rows_n, pair_ref, w_in_ref, w_out_ref, *refs):
    out_ref = refs[-1]
    cols = pair_ref.shape[1]
    step = SUB // cols
    for i in range(rows_n // step):
        cells = pair_ref[i * step : (i + 1) * step].reshape(SUB, 128)
        moved = transition(cells, w_in_ref[...], w_out_ref[...])
        out_ref[i * step : (i + 1) * step] = moved.astype(jnp.bfloat16).reshape(step, cols, 128)


def pair_part(pair_act, w_in, w_out, part, first, count, earlier, after):
    rows, cols, width = pair_act.shape
    block = (ROWS, cols, width)
    whole = pl.BlockSpec(memory_space=pltpu.VMEM)
    anywhere = pl.BlockSpec(memory_space=pl.ANY)
    args = [pair_act, w_in, w_out]
    specs = [pl.BlockSpec(block, lambda i: (PARTS * (first + i) + part, 0, 0)), whole, whole]
    aliases = {}
    if earlier is not None:
        aliases = {len(args): 0}
        args.append(earlier)
        specs.append(anywhere)
    for value in after:
        args.append(value)
        specs.append(anywhere)
    cells = count * ROWS * cols
    return pl.pallas_call(
        functools.partial(part_kernel, ROWS),
        grid=(count,),
        in_specs=specs,
        out_specs=pl.BlockSpec(block, lambda i: (PARTS * (first + i) + part, 0, 0)),
        out_shape=jax.ShapeDtypeStruct(pair_act.shape, jnp.bfloat16),
        input_output_aliases=aliases,
        cost_estimate=pl.CostEstimate(
            flops=cells * 196608 * 4, bytes_accessed=cells * 512, transcendentals=cells * 512
        ),
        compiler_params=pltpu.CompilerParams(vmem_limit_bytes=VMEM_BYTES),
        name="pair_part",
    )(*args)


def last_kernel(
    place_ref, pair_ref, done_ref, w_in_ref, w_out_ref, own_ref, other_ref, col_ref, out_ref,
    row_scr, col_scr,
):
    i = pl.program_id(0)
    cols = pair_ref.shape[1]

    @pl.when(i == 0)
    def _():
        row, col = place_ref[0], place_ref[1]
        for block in range(8):
            at = pl.ds(block * 16, 16)
            mine = pl.multiple_of((block ^ (col & 7)) * 16, 16)
            col_at = pl.multiple_of((block ^ row) * 16, 16)
            col_scr[at, :] = col_ref[pl.ds(col_at, 16), :].astype(jnp.float32)
            own_half = pl.multiple_of((col >> 3) * 128 + block * 16, 16)
            other_half = pl.multiple_of((1 - (col >> 3)) * 128 + block * 16, 16)
            row_scr[pl.ds(own_half, 16), :] = own_ref[pl.ds(mine, 16), :].astype(jnp.float32)
            row_scr[pl.ds(other_half, 16), :] = other_ref[pl.ds(mine, 16), :].astype(jnp.float32)

    size = PARTS * ROWS
    base = pl.multiple_of(i * size, size)
    col_add = col_scr[...]
    for r in range((PARTS - 1) * ROWS):
        extra = row_scr[pl.ds(base + r, 1), :] + col_add
        out_ref[r] = (done_ref[r].astype(jnp.float32) + extra).astype(jnp.bfloat16)
    step = SUB // cols
    for k in range(ROWS // step):
        cells = pair_ref[k * step : (k + 1) * step].reshape(SUB, 128)
        moved = transition(cells, w_in_ref[...], w_out_ref[...])
        for s in range(step):
            r = (PARTS - 1) * ROWS + k * step + s
            extra = row_scr[pl.ds(base + r, 1), :] + col_add
            out_ref[r] = (moved[s * cols : (s + 1) * cols] + extra).astype(jnp.bfloat16)


def last_part(place, pair_act, done, w_in, w_out, own, other, col):
    rows, cols, width = pair_act.shape
    count = rows // (PARTS * ROWS)
    big = (PARTS * ROWS, cols, width)
    whole = pl.BlockSpec(memory_space=pltpu.VMEM)
    return pl.pallas_call(
        last_kernel,
        grid=(count,),
        in_specs=[
            pl.BlockSpec(memory_space=pltpu.SMEM),
            pl.BlockSpec((ROWS, cols, width), lambda i: (PARTS * i + PARTS - 1, 0, 0)),
            pl.BlockSpec(big, lambda i: (i, 0, 0)),
            whole,
            whole,
            whole,
            whole,
            whole,
        ],
        out_specs=pl.BlockSpec(big, lambda i: (i, 0, 0)),
        out_shape=jax.ShapeDtypeStruct(pair_act.shape, jnp.bfloat16),
        scratch_shapes=[
            pltpu.VMEM((rows, width), jnp.float32),
            pltpu.VMEM((cols, width), jnp.float32),
        ],
        input_output_aliases={2: 0},
        cost_estimate=pl.CostEstimate(
            flops=rows * cols * 196608, bytes_accessed=rows * cols * 512, transcendentals=0
        ),
        compiler_params=pltpu.CompilerParams(vmem_limit_bytes=VMEM_BYTES),
        name="pair_last",
    )(place, pair_act, done, w_in, w_out, own, other, col)


def after(value, *others):
    return lax.optimization_barrier((value, *others))[0]


def on_device(
    pair_act, atom_act, atom_token, atom_gain, w_attn, w_out, w_bias, w_trans_in, w_trans_out,
    w_agg, w_single,
):
    atom_n, atom_width = atom_act.shape
    n_row, n_col = lax.axis_size("row"), lax.axis_size("col")
    devices = n_row * n_col
    row_index, col_index = lax.axis_index("row"), lax.axis_index("col")
    flat = row_index * n_col + col_index
    place = jnp.stack([row_index, col_index, flat, jnp.int32(devices * atom_n)]).astype(jnp.int32)
    both = ("row", "col")
    up = [(i, i + 1) for i in range(devices - 1)]
    down = [(i + 1, i) for i in range(devices - 1)]

    token_rel = (atom_token - flat * TOK_DEV).astype(jnp.bfloat16)
    tok_rows = jnp.broadcast_to(token_rel[None, :], (16, atom_n))
    below = lax.ppermute(jnp.concatenate([atom_act[-BELOW:], tok_rows]), both, up)
    above = lax.ppermute(jnp.concatenate([atom_act[:ABOVE], tok_rows]), both, down)

    width = w_trans_out.shape[0]
    scale = jnp.where(jnp.arange(2 * width) < width, 0.5, 1.0).astype(jnp.bfloat16)
    w_in = w_trans_in * scale[None, :]

    band = band_biases(place, pair_act, w_bias)
    near = lax.all_to_all(band, "col", 0, 0, tiled=True)
    moved = pair_part(pair_act, w_in, w_trans_out, 0, 0, 4, None, (band,))
    near, below, above = lax.optimization_barrier((near, below, above, moved))[:3]
    atom_out, next_out, token_single, singles = atom_part(
        place, below, atom_act, above, tok_rows, near, atom_gain[None, :], w_attn, w_out, w_agg,
        w_single,
    )

    held = singles
    from_below = lax.ppermute(next_out, both, up)
    for k in range(3):
        arrived = lax.ppermute(held, "col", [(i, i ^ (1 << k)) for i in range(n_col)])
        moved = pair_part(pair_act, w_in, w_trans_out, 1 + k // 2, 2 * (k % 2), 2, moved, (held,))
        arrived = after(arrived, moved)
        held = jnp.concatenate([held, arrived])
    row_own, col_own = held[:, :atom_width], held[:, atom_width:]
    row_other = lax.ppermute(row_own, "col", [(i, i ^ 8) for i in range(n_col)])
    turn = [(16 * a + 8 * h + k, 16 * k + 2 * a + h) for a in range(8) for h in range(2) for k in range(8)]
    col_tile = lax.ppermute(col_own, both, turn)
    moved = pair_part(pair_act, w_in, w_trans_out, 2, 2, 2, moved, (row_own, col_own))
    row_other, col_tile, from_below = lax.optimization_barrier(
        (row_other, col_tile, from_below, moved)
    )[:3]
    pair_out = last_part(
        place, pair_act, moved, w_in, w_trans_out, row_own, row_other, col_tile
    )
    shared = (atom_token < flat * TOK_DEV)[:16, None]
    atom_out = atom_out.at[:16].set(jnp.where(shared, from_below, atom_out[:16]))
    return (atom_out, token_single, pair_out)


def solution(mesh):
    both = P(("row", "col"), None)
    return jax.shard_map(
        on_device,
        mesh=mesh,
        in_specs=(P("row", "col", None), both, P(("row", "col"))) + (P(),) * 8,
        out_specs=(both, both, P("row", "col", None)),
        check_vma=False,
    )
```

time: 608 us -> 101 us (0.17)
  the two profiles are of different devices: /device:TPU:1 before, /device:TPU:6 now
where the time goes in v1:
time: 101 us; the launch traced here: 99.5 us
  Pallas kernels  60.2 us (60%)
  starting transfers between devices  30.3 us (30%)
  local copies, waits for them, and re-layouts  4.78 us (5%)
  other arithmetic  3.38 us (3%)
    pallas_call x5, Pallas kernels, pair_part(): pl.pallas_call(functools.partial(part_kernel, ROWS), grid=(count,), in_sp...  35.4 us
    pallas_call x1, Pallas kernels, last_part(): pl.pallas_call(last_kernel, grid=(count,), in_specs=[pl.BlockSpec(memory_...  13.1 us
    ppermute x1, starting transfers between devices, on_device(): col_tile = lax.ppermute(col_own, both, turn)  9.37 us
    all_to_all x1, starting transfers between devices, on_device(): near = lax.all_to_all(band, 'col', 0, 0, tiled=True)  8.34 us
    pallas_call x1, Pallas kernels, band_biases(): pl.pallas_call(band_kernel, in_specs=[pl.BlockSpec(memory_space=pltpu.SME...  7.11 us
    ppermute x1, starting transfers between devices, on_device(): lax.ppermute(jnp.concatenate([atom_act[:ABOVE], tok_rows]), both, down)  5.13 us
    pallas_call x1, Pallas kernels, atom_part(): pl.pallas_call(atom_kernel, in_specs=[pl.BlockSpec(memory_space=pltpu.SME...  4.6 us
    ppermute x3, starting transfers between devices, on_device(): arrived = lax.ppermute(held, 'col', [(i, i ^ 1 << k) for i in range(n_col)])  2.41 us
  transfers between devices with their start and end apart: 9, of which 0 were waited for; matrix products, arithmetic and copies ran while one was open for 3% of the time, Pallas kernels for 36%

profile of v1, /device:TPU:6, one launch (start us, length us, event | category | flops | bytes accessed | tf_op | source)
XLA Modules:
  0.0 99.5 jit_solution(10057544767888050326)
XLA Ops:
  0.6 0.0 copy-start.1
  0.6 0.8 slice.51
  1.4 0.7 subtract_convert_fusion
  2.1 0.0 copy-start.5
  2.1 1.9 %collective-permute-start = (bf16[64,128]{1,0:T(8,128)(2,1)S(1)}, bf16[64,128]{1,0:T(8,128)(2,1)S(1)}, u32[]{:S(2)}, u32[]{:S(2)}) collective-permute-start(bf16[64,128]{1,0:T(8,128)(2,1)S(1)} %pad_maximum_fusion.1), channel_id=1, source_target_pairs={{0,1},{1,2},{2,3},{3,4},{4,5},{5,6},{6,7},{7,8},{8,9},{9,10},{10,1... | collective-permute-start | bytes 49160 | tf_op jit(solution)/shard_map/ppermute | solution.py:357
  4.0 0.7 slice.52
  4.7 5.1 %collective-permute-start.1 = (bf16[96,128]{1,0:T(8,128)(2,1)S(1)}, bf16[96,128]{1,0:T(8,128)(2,1)S(1)}, u32[]{:S(2)}, u32[]{:S(2)}) collective-permute-start(bf16[96,128]{1,0:T(8,128)(2,1)S(1)} %pad_maximum_fusion), channel_id=1, source_target_pairs={{1,0},{2,1},{3,2},{4,3},{5,4},{6,5},{7,6},{8,7},{9,8},{10,9},{11,1... | collective-permute-start | bytes 73736 | tf_op jit(solution)/shard_map/ppermute | solution.py:358
  9.9 1.3 %scatter.6.weight_ref = bf16[16,128]{1,0:T(8,128)(2,1)} pad(bf16[4,128]{1,0:T(4,128)(2,1)} %bitcast.6, bf16[]{:T(256)} %constant.66.clone.1), padding=0_12x0_0 | pad | bytes 5122 | tf_op jit(solution)/shard_map/scatter | solution.py:80
  11.2 0.6 pad_add_fusion.place_ref
  11.8 7.1 %band.1.refs_0_ = bf16[16,32,128]{2,1,0:T(8,128)(2,1)} custom-call(s32[4]{0:T(128)} %pad_add_fusion.place_ref, bf16[256,128,128]{2,1,0:T(8,128)(2,1)} %pair_ref.13, bf16[16,128]{1,0:T(8,128)(2,1)} %scatter.6.weight_ref), custom_call_target="tpu_custom_call" | custom-call | flops 1000000000 | bytes 3000000 | tf_op jit(solution)/shard_map/band/pallas_call | solution.py:81
  18.9 8.3 %all-to-all-start = ((bf16[16,32,128]{2,1,0:T(8,128)(2,1)}), bf16[16,32,128]{2,1,0:T(8,128)(2,1)S(1)}, u32[]{:S(2)}, u32[]{:S(2)}) async-start(bf16[16,32,128]{2,1,0:T(8,128)(2,1)} %band.1.refs_0_), calls=%async_computation | async-start | bytes 262144 | tf_op jit(solution)/shard_map/all_to_all | solution.py:365
  27.2 0.0 copy-done.1
  27.3 0.7 broadcast_multiply_fusion.w_in_ref
  28.0 0.0 copy-start.13
  28.0 10.5 %pair_part.5.refs_0_ = bf16[256,128,128]{2,1,0:T(8,128)(2,1)} custom-call(bf16[256,128,128]{2,1,0:T(8,128)(2,1)} %pair_ref.13, bf16[128,1024]{1,0:T(8,128)(2,1)} %broadcast_multiply_fusion.w_in_ref, bf16[512,128]{1,0:T(8,128)(2,1)} %w_out_ref.11, bf16[16,32,128]{2,1,0:T(8,128)(2,1)} %band.1.refs_0_), custom_call_target="tpu_custom_call" | custom-call | flops 6442450944 | bytes 4194304 | tf_op jit(solution)/shard_map/pair_part/pallas_call | solution.py:253
  38.5 0.0 copy-done.5
  38.5 0.0 copy-done.13
  38.5 0.0 collective-permute-done.below_ref
  38.5 0.0 copy-start.11
  38.5 0.0 collective-permute-done.1.above_ref
  38.6 0.0 copy-start.10
  38.6 0.0 all-to-all-done.band_ref
  38.6 0.0 copy-start.3
  38.6 0.6 copy-done.11
  39.1 0.0 copy-done.10
  39.2 0.1 copy-done.3
  39.2 4.6 %atoms.1 = (bf16[128,128]{1,0:T(8,128)(2,1)}, bf16[16,128]{1,0:T(8,128)(2,1)}, bf16[16,384]{1,0:T(8,128)(2,1)}, bf16[16,256]{1,0:T(8,128)(2,1)}) custom-call(s32[4]{0:T(128)} %pad_add_fusion.place_ref, bf16[64,128]{1,0:T(8,128)(2,1)} %copy-done.11, bf16[128,128]{1,0:T(8,128)(2,1)} %own_ref.1, bf16[96,128]{1,0:T(8,128)(2,1)} %copy-done.10, ...), custom_call_target="tpu_custom_call" | custom-call | flops 1000000000 | bytes 1000000 | tf_op jit(solution)/shard_map/atoms/pallas_call | solution.py:190
  43.8 0.0 copy-start.9
  43.8 0.0 copy-start.12
  43.8 6.2 %pair_part.6.refs_0_ = bf16[256,128,128]{2,1,0:T(8,128)(2,1)} custom-call(bf16[256,128,128]{2,1,0:T(8,128)(2,1)} %pair_ref.13, bf16[128,1024]{1,0:T(8,128)(2,1)} %broadcast_multiply_fusion.w_in_ref, bf16[512,128]{1,0:T(8,128)(2,1)} %w_out_ref.11, bf16[256,128,128]{2,1,0:T(8,128)(2,1)} %pair_part.5.refs_0_, ...), custom_call_target="tpu_custom_call", output_to_operand_aliasing={{}: (3, {})} | custom-call | flops 3221225472 | bytes 2097152 | tf_op jit(solution)/shard_map/pair_part/pallas_call | solution.py:253
  50.1 0.0 copy-done.9
  50.1 0.1 collective-permute-start.2
  50.2 0.0 copy-done.12
  50.2 2.3 %collective-permute-start.7 = (bf16[16,128]{1,0:T(8,128)(2,1)S(1)}, bf16[16,128]{1,0:T(8,128)(2,1)S(1)}, u32[]{:S(2)}, u32[]{:S(2)}) collective-permute-start(bf16[16,128]{1,0:T(8,128)(2,1)S(1)} %copy-done.12), channel_id=1, source_target_pairs={{0,1},{1,2},{2,3},{3,4},{4,5},{5,6},{6,7},{7,8},{8,9},{9,10},{10,1... | collective-permute-start | bytes 12296 | tf_op jit(solution)/shard_map/ppermute | solution.py:374
  52.5 0.0 collective-permute-done.2
  52.5 0.0 copy-start.6
  52.5 0.5 collective-permute-start.3
  53.0 0.1 copy-done.6
  53.1 6.2 %pair_part.7.refs_0_ = bf16[256,128,128]{2,1,0:T(8,128)(2,1)} custom-call(bf16[256,128,128]{2,1,0:T(8,128)(2,1)} %pair_ref.13, bf16[128,1024]{1,0:T(8,128)(2,1)} %broadcast_multiply_fusion.w_in_ref, bf16[512,128]{1,0:T(8,128)(2,1)} %w_out_ref.11, bf16[256,128,128]{2,1,0:T(8,128)(2,1)} %pair_part.6.refs_0_, ...), custom_call_target="tpu_custom_call", output_to_operand_aliasing={{}: (3, {})} | custom-call | flops 3221225472 | bytes 2097152 | tf_op jit(solution)/shard_map/pair_part/pallas_call | solution.py:253
  59.3 0.0 collective-permute-done.3
  59.3 0.0 copy-start.4
  59.3 1.8 %collective-permute-start.4 = (bf16[64,256]{1,0:T(8,128)(2,1)S(1)}, bf16[64,256]{1,0:T(8,128)(2,1)S(1)}, u32[]{:S(2)}, u32[]{:S(2)}) collective-permute-start(bf16[64,256]{1,0:T(8,128)(2,1)S(1)} %get-tuple-element.55.refs_1_), channel_id=1, source_target_pairs={{0,4},{1,5},{2,6},{3,7},{4,0},{5,1},{6,2},{7,3},{8,12},{9,13},{10,... | collective-permute-start | bytes 98312 | tf_op jit(solution)/shard_map/ppermute | solution.py:376
  61.1 0.0 copy-done.4
  61.1 6.2 %pair_part.8.refs_0_ = bf16[256,128,128]{2,1,0:T(8,128)(2,1)} custom-call(bf16[256,128,128]{2,1,0:T(8,128)(2,1)} %pair_ref.13, bf16[128,1024]{1,0:T(8,128)(2,1)} %broadcast_multiply_fusion.w_in_ref, bf16[512,128]{1,0:T(8,128)(2,1)} %w_out_ref.11, bf16[256,128,128]{2,1,0:T(8,128)(2,1)} %pair_part.7.refs_0_, ...), custom_call_target="tpu_custom_call", output_to_operand_aliasing={{}: (3, {})} | custom-call | flops 3221225472 | bytes 2097152 | tf_op jit(solution)/shard_map/pair_part/pallas_call | solution.py:253
  67.4 0.0 collective-permute-done.4
  67.4 0.0 copy-start
  67.4 0.0 copy-start.2
  67.4 9.4 %collective-permute-start.6 = (bf16[128,128]{1,0:T(8,128)(2,1)S(1)}, bf16[128,128]{1,0:T(8,128)(2,1)S(1)}, u32[]{:S(2)}, u32[]{:S(2)}) collective-permute-start(bf16[128,128]{1,0:T(8,128)(2,1)S(1)} %get-tuple-element.53.refs_2_), channel_id=1, source_target_pairs={{0,0},{1,16},{2,32},{3,48},{4,64},{5,80},{6,96},{7,112},{8,1},{9,1... | collective-permute-start | bytes 98312 | tf_op jit(solution)/shard_map/ppermute | solution.py:383
  76.8 0.9 collective-permute-start.5
  77.6 0.0 copy-done
  77.6 0.0 copy-done.2
  77.6 6.2 %pair_part.9.done_ref = bf16[256,128,128]{2,1,0:T(8,128)(2,1)} custom-call(bf16[256,128,128]{2,1,0:T(8,128)(2,1)} %pair_ref.13, bf16[128,1024]{1,0:T(8,128)(2,1)} %broadcast_multiply_fusion.w_in_ref, bf16[512,128]{1,0:T(8,128)(2,1)} %w_out_ref.11, bf16[256,128,128]{2,1,0:T(8,128)(2,1)} %pair_part.8.refs_0_, ...), custom_call_target="tpu_custom_call", output_to_operand_aliasing={{}: (3, {})} | custom-call | flops 3221225472 | bytes 2097152 | tf_op jit(solution)/shard_map/pair_part/pallas_call | solution.py:253
  83.9 0.0 collective-permute-done.7
  83.9 0.0 collective-permute-done.6.col_ref
  83.9 0.0 copy-start.7
  83.9 0.0 collective-permute-done.5.other_ref
  83.9 0.6 copy-done.7
  84.5 0.0 copy-start.8
  84.5 0.6 copy-done.8
  85.1 13.1 %pair_last.1 = bf16[256,128,128]{2,1,0:T(8,128)(2,1)} custom-call(s32[4]{0:T(128)} %pad_add_fusion.place_ref, bf16[256,128,128]{2,1,0:T(8,128)(2,1)} %pair_ref.13, bf16[256,128,128]{2,1,0:T(8,128)(2,1)} %pair_part.9.done_ref, bf16[128,1024]{1,0:T(8,128)(2,1)} %broadcast_multiply_fusion.w_in_ref, ...), custom_call_target="tpu_custom_call", output_to_operand_aliasing={{}: (2, {})} | custom-call | flops 6442450944 | bytes 16777216 | tf_op jit(solution)/shard_map/pair_last/pallas_call | solution.py:309
  98.2 1.4 %select_dynamic-update-slice_fusion = bf16[128,128]{1,0:T(8,128)(2,1)} fusion(bf16[128,128]{1,0:T(8,128)(2,1)} %get-tuple-element.43, bf16[16,128]{1,0:T(8,128)(2,1)S(1)} %collective-permute-done.7, pred[16]{0:T(512)(128)(4,1)S(1)} %bitcast.7), kind=kLoop, calls=%fused_computation.12 | loop fusion | flops 2048 | bytes 12304 | tf_op jit(solution)/shard_map/scatter | solution.py:392
  (10 shorter events, 0.0 us)
Async XLA Ops:
  0.6 26.6 %copy-start.1 = (bf16[128,1024]{1,0:T(8,128)(2,1)S(1)}, bf16[128,1024]{1,0:T(8,128)(2,1)}, u32[]{:S(2)}) copy-start(bf16[128,1024]{1,0:T(8,128)(2,1)} %param.22) | copy-start | bytes 786436
  2.1 36.4 %copy-start.5 = (bf16[16,128]{1,0:T(8,128)(2,1)}, bf16[16,128]{1,0:T(8,128)(2,1)S(1)}, u32[]{:S(2)}) copy-start(bf16[16,128]{1,0:T(8,128)(2,1)S(1)} %broadcast_in_dim.28.tok_ref) | copy-start | bytes 12292
  2.1 36.5 %collective-permute-start = (bf16[64,128]{1,0:T(8,128)(2,1)S(1)}, bf16[64,128]{1,0:T(8,128)(2,1)S(1)}, u32[]{:S(2)}, u32[]{:S(2)}) collective-permute-start(bf16[64,128]{1,0:T(8,128)(2,1)S(1)} %pad_maximum_fusion.1), channel_id=1, source_target_pairs={{0,1},{1,2},{2,3},{3,4},{4,5},{5,6},{6,7},{7,8},{8,9},{9,10},{10,1... | collective-permute-start | bytes 49160 | tf_op jit(solution)/shard_map/ppermute | solution.py:357
  4.7 33.8 %collective-permute-start.1 = (bf16[96,128]{1,0:T(8,128)(2,1)S(1)}, bf16[96,128]{1,0:T(8,128)(2,1)S(1)}, u32[]{:S(2)}, u32[]{:S(2)}) collective-permute-start(bf16[96,128]{1,0:T(8,128)(2,1)S(1)} %pad_maximum_fusion), channel_id=1, source_target_pairs={{1,0},{2,1},{3,2},{4,3},{5,4},{6,5},{7,6},{8,7},{9,8},{10,9},{11,1... | collective-permute-start | bytes 73736 | tf_op jit(solution)/shard_map/ppermute | solution.py:358
  18.9 19.7 %all-to-all-start = ((bf16[16,32,128]{2,1,0:T(8,128)(2,1)}), bf16[16,32,128]{2,1,0:T(8,128)(2,1)S(1)}, u32[]{:S(2)}, u32[]{:S(2)}) async-start(bf16[16,32,128]{2,1,0:T(8,128)(2,1)} %band.1.refs_0_), calls=%async_computation | async-start | bytes 262144 | tf_op jit(solution)/shard_map/all_to_all | solution.py:365
  28.0 10.5 %copy-start.13 = (s32[128]{0:T(128)S(1)}, s32[128]{0:T(128)}, u32[]{:S(2)}) copy-start(s32[128]{0:T(128)} %param.17) | copy-start | bytes 1540
  38.5 0.6 copy-start.11
  38.6 0.6 copy-start.10
  38.6 0.7 copy-start.3
  43.8 6.2 %copy-start.9 = (bf16[16,256]{1,0:T(8,128)(2,1)S(1)}, bf16[16,256]{1,0:T(8,128)(2,1)}, u32[]{:S(2)}) copy-start(bf16[16,256]{1,0:T(8,128)(2,1)} %get-tuple-element.44.refs_1_) | copy-start | bytes 24580
  43.8 6.4 %copy-start.12 = (bf16[16,128]{1,0:T(8,128)(2,1)S(1)}, bf16[16,128]{1,0:T(8,128)(2,1)}, u32[]{:S(2)}) copy-start(bf16[16,128]{1,0:T(8,128)(2,1)} %get-tuple-element.48) | copy-start | bytes 12292
  50.1 2.4 %collective-permute-start.2 = (bf16[16,256]{1,0:T(8,128)(2,1)S(1)}, bf16[16,256]{1,0:T(8,128)(2,1)S(1)}, u32[]{:S(2)}, u32[]{:S(2)}) collective-permute-start(bf16[16,256]{1,0:T(8,128)(2,1)S(1)} %copy-done.9), channel_id=1, source_target_pairs={{0,1},{1,0},{2,3},{3,2},{4,5},{5,4},{6,7},{7,6},{8,9},{9,8},{10,11... | collective-permute-start | bytes 24584 | tf_op jit(solution)/shard_map/ppermute | solution.py:376
  50.2 33.7 %collective-permute-start.7 = (bf16[16,128]{1,0:T(8,128)(2,1)S(1)}, bf16[16,128]{1,0:T(8,128)(2,1)S(1)}, u32[]{:S(2)}, u32[]{:S(2)}) collective-permute-start(bf16[16,128]{1,0:T(8,128)(2,1)S(1)} %copy-done.12), channel_id=1, source_target_pairs={{0,1},{1,2},{2,3},{3,4},{4,5},{5,6},{6,7},{7,8},{8,9},{9,10},{10,1... | collective-permute-start | bytes 12296 | tf_op jit(solution)/shard_map/ppermute | solution.py:374
  52.5 0.6 copy-start.6
  52.5 6.8 %collective-permute-start.3 = (bf16[32,256]{1,0:T(8,128)(2,1)S(1)}, bf16[32,256]{1,0:T(8,128)(2,1)S(1)}, u32[]{:S(2)}, u32[]{:S(2)}) collective-permute-start(bf16[32,256]{1,0:T(8,128)(2,1)S(1)} %get-tuple-element.59.refs_1_), channel_id=1, source_target_pairs={{0,2},{1,3},{2,0},{3,1},{4,6},{5,7},{6,4},{7,5},{8,10},{9,11},{10,... | collective-permute-start | bytes 49160 | tf_op jit(solution)/shard_map/ppermute | solution.py:376
  59.3 1.8 %copy-start.4 = (bf16[64,256]{1,0:T(8,128)(2,1)}, bf16[64,256]{1,0:T(8,128)(2,1)S(1)}, u32[]{:S(2)}) copy-start(bf16[64,256]{1,0:T(8,128)(2,1)S(1)} %get-tuple-element.55.refs_1_) | copy-start | bytes 98308
  59.3 8.0 %collective-permute-start.4 = (bf16[64,256]{1,0:T(8,128)(2,1)S(1)}, bf16[64,256]{1,0:T(8,128)(2,1)S(1)}, u32[]{:S(2)}, u32[]{:S(2)}) collective-permute-start(bf16[64,256]{1,0:T(8,128)(2,1)S(1)} %get-tuple-element.55.refs_1_), channel_id=1, source_target_pairs={{0,4},{1,5},{2,6},{3,7},{4,0},{5,1},{6,2},{7,3},{8,12},{9,13},{10,... | collective-permute-start | bytes 98312 | tf_op jit(solution)/shard_map/ppermute | solution.py:376
  67.4 10.3 %copy-start = (bf16[128,128]{1,0:T(8,128)(2,1)}, bf16[128,128]{1,0:T(8,128)(2,1)S(1)}, u32[]{:S(2)}) copy-start(bf16[128,128]{1,0:T(8,128)(2,1)S(1)} %get-tuple-element.54.refs_1_.own_ref) | copy-start | bytes 98308
  67.4 10.3 %copy-start.2 = (bf16[128,128]{1,0:T(8,128)(2,1)}, bf16[128,128]{1,0:T(8,128)(2,1)S(1)}, u32[]{:S(2)}) copy-start(bf16[128,128]{1,0:T(8,128)(2,1)S(1)} %get-tuple-element.53.refs_2_) | copy-start | bytes 98308
  67.4 16.5 %collective-permute-start.6 = (bf16[128,128]{1,0:T(8,128)(2,1)S(1)}, bf16[128,128]{1,0:T(8,128)(2,1)S(1)}, u32[]{:S(2)}, u32[]{:S(2)}) collective-permute-start(bf16[128,128]{1,0:T(8,128)(2,1)S(1)} %get-tuple-element.53.refs_2_), channel_id=1, source_target_pairs={{0,0},{1,16},{2,32},{3,48},{4,64},{5,80},{6,96},{7,112},{8,1},{9,1... | collective-permute-start | bytes 98312 | tf_op jit(solution)/shard_map/ppermute | solution.py:383
  76.8 7.1 %collective-permute-start.5 = (bf16[128,128]{1,0:T(8,128)(2,1)S(1)}, bf16[128,128]{1,0:T(8,128)(2,1)S(1)}, u32[]{:S(2)}, u32[]{:S(2)}) collective-permute-start(bf16[128,128]{1,0:T(8,128)(2,1)S(1)} %get-tuple-element.54.refs_1_.own_ref), channel_id=1, source_target_pairs={{0,8},{1,9},{2,10},{3,11},{4,12},{5,13},{6,14},{7,15},{8,0},{9,1},... | collective-permute-start | bytes 98312 | tf_op jit(solution)/shard_map/ppermute | solution.py:381
  83.9 0.6 copy-start.7
  84.5 0.6 copy-start.8

commit v2 on v1

v2 whole, which is shorter than its diff:
```python
import functools
import math

import jax
import jax.numpy as jnp
from jax import lax
from jax.experimental import pallas as pl
from jax.experimental.pallas import tpu as pltpu
from jax.sharding import PartitionSpec as P

SPAN = 10
QB = 32
KW = 128
TOK_DEV = 16
BELOW = (KW - QB) // 2
ABOVE = KW - BELOW
WINDOW = 64
GROUPS = 9
BAND_ROWS = 32
EDGE = 48
BLOCK_ROWS = BAND_ROWS + 16 + ABOVE
BATCH = 3
VMEM_BYTES = 56 * 1024 * 1024
ROWS = 64
EARLY = 16
SUB = 512


def normalize(values):
    centre = values - jnp.mean(values, axis=-1, keepdims=True)
    spread = jnp.mean(centre * centre, axis=-1, keepdims=True)
    return centre * lax.rsqrt(spread + 1e-05)


def dot(a, b, **kw):
    return jnp.dot(a, b, preferred_element_type=jnp.float32, **kw)


def dot_nt(a, b):
    return lax.dot_general(a, b, (((1,), (1,)), ((), ())), preferred_element_type=jnp.float32)


def band_kernel(
    place_ref, pair_ref, weight_ref, atom_ref, token_ref, out_ref, cross_ref, tok_ref, cells, sems
):
    row, col = place_ref[0], place_ref[1]
    shift = col - 2 * row
    first = jnp.clip(8 * shift - 1, 0, 7)
    copies = []
    for j in range(GROUPS):
        group = first + j
        start = group - 8 * shift - 1
        begin = jnp.clip(start, 0, 4)
        at = jnp.clip(EDGE // 16 + begin - start, 0, 2 * EDGE // 16)
        copy = pltpu.make_async_copy(
            pair_ref.at[
                pl.ds(pl.multiple_of(group * 16, 16), 16),
                pl.ds(pl.multiple_of(begin * 16, 16), WINDOW),
                :,
            ],
            cells.at[j, :, pl.ds(pl.multiple_of(at * 16, 16), WINDOW), :],
            sems.at[j],
        )
        copy.start()
        copies.append(copy)
    out_ref[:, 0:BAND_ROWS, :] = jnp.zeros((out_ref.shape[0], BAND_ROWS, 128), jnp.bfloat16)
    atoms = atom_ref.shape[0]
    token_rel = (token_ref[...] - place_ref[2] * TOK_DEV).astype(jnp.float32)
    tok_rows = jnp.broadcast_to(token_rel, (16, 128)).astype(jnp.bfloat16)
    tok_ref[...] = tok_rows
    low = BAND_ROWS
    last = out_ref.shape[0] - 1

    def to_above(ref, at):
        ref[at : at + 16, :] = tok_rows
        ref[at + 16 : at + 16 + BELOW, :] = atom_ref[atoms - BELOW :, :]

    def to_below(ref, at):
        ref[at : at + 16, :] = tok_rows
        ref[at + 16 : at + 16 + ABOVE, :] = atom_ref[0:ABOVE, :]

    to_above(out_ref.at[jnp.minimum(col + 1, last)], low)
    to_below(out_ref.at[jnp.maximum(col - 1, 0)], low)

    @pl.when(col == last)
    def _():
        to_above(cross_ref, 0)
        to_below(out_ref.at[last - 1], low)

    @pl.when(col == 0)
    def _():
        to_below(cross_ref, 0)
        to_above(out_ref.at[1], low)

    weight = jnp.concatenate(
        [weight_ref[...].astype(jnp.float32), jnp.zeros((12, 128), jnp.float32)], axis=0
    ).astype(jnp.bfloat16)
    lane_piece = (lax.broadcasted_iota(jnp.int32, (BAND_ROWS, 128), 1) % WINDOW) // 16
    for j0 in range(0, GROUPS, BATCH):
        for j in range(j0, j0 + BATCH):
            copies[j].wait()
        flat = cells[j0 : j0 + BATCH, :, EDGE : EDGE + WINDOW, :].reshape(-1, 128)
        normed = normalize(flat.astype(jnp.float32)).astype(jnp.bfloat16)
        biases = dot_nt(weight, normed)
        for j in range(j0, j0 + BATCH):
            off = (j - j0) * 8
            rows = jnp.concatenate(
                [biases[0:4, 128 * (off + i) : 128 * (off + i + 1)] for i in range(8)], axis=0
            )
            at = first + j - 8 * shift - 1 + lane_piece
            kept = jnp.where((at >= 0) & (at <= 7), rows, 0.0)
            out_ref[pl.ds(first + j, 1), 0:BAND_ROWS, :] = kept.astype(jnp.bfloat16)[None]


def band_biases(place, pair_act, w_bias, atom_act, atom_token):
    vmem = pl.BlockSpec(memory_space=pltpu.VMEM)
    return pl.pallas_call(
        band_kernel,
        in_specs=[
            pl.BlockSpec(memory_space=pltpu.SMEM),
            pl.BlockSpec(memory_space=pl.ANY),
            vmem,
            vmem,
            vmem,
        ],
        out_specs=[vmem] * 3,
        out_shape=[
            jax.ShapeDtypeStruct((16, BLOCK_ROWS, 128), jnp.bfloat16),
            jax.ShapeDtypeStruct((16 + ABOVE, 128), jnp.bfloat16),
            jax.ShapeDtypeStruct((16, 128), jnp.bfloat16),
        ],
        scratch_shapes=[
            pltpu.VMEM((GROUPS, 16, WINDOW + 2 * EDGE, 128), jnp.bfloat16),
            pltpu.SemaphoreType.DMA((GROUPS,)),
        ],
        cost_estimate=pl.CostEstimate(flops=10**9, bytes_accessed=3 * 10**6, transcendentals=0),
        compiler_params=pltpu.CompilerParams(vmem_limit_bytes=VMEM_BYTES),
        name="band",
    )(place, pair_act, w_bias.T, atom_act, atom_token[None, :])


def atom_kernel(
    place_ref, cross_ref, own_ref, tok_ref, near_ref, gain_ref, wattn_ref, wout_ref,
    wagg_ref, wsingle_ref, atom_out_ref, next_out_ref, shared_ref, token_ref, singles_ref,
    wide, q_scr, k_scr, v_scr, gate_scr,
):
    flat = place_ref[2]
    atoms = own_ref.shape[0]
    heads = 4
    n_query = atoms + QB
    total = place_ref[3]
    col = place_ref[1]
    last = near_ref.shape[0] - 1
    low = BAND_ROWS
    from_below = near_ref[jnp.maximum(col - 1, 0), low : low + 16 + BELOW, :].astype(jnp.float32)
    from_above = near_ref[jnp.minimum(col + 1, last), low:, :].astype(jnp.float32)
    cross = cross_ref[...].astype(jnp.float32)
    from_below = jnp.where(col == 0, cross[0 : 16 + BELOW], from_below)
    from_above = jnp.where(col == last, cross, from_above)
    wide[0:BELOW, :] = from_below[16:]
    wide[BELOW : BELOW + atoms, :] = own_ref[...].astype(jnp.float32)
    wide[BELOW + atoms :, :] = from_above[16:]
    normed = (normalize(wide[...]) * gain_ref[...]).astype(jnp.bfloat16)
    projected = dot(normed, wattn_ref[...])
    q_scr[...] = projected[BELOW : BELOW + n_query, 0:128].astype(jnp.bfloat16)
    k_scr[...] = projected[:, 128:256].astype(jnp.bfloat16)
    v_scr[...] = projected[:, 256:384].astype(jnp.bfloat16)
    gate_scr[...] = jax.nn.sigmoid(projected[BELOW : BELOW + n_query, 384:512])

    tok_own = tok_ref[0:1, :].astype(jnp.float32)
    tok_below = from_below[0:1] - TOK_DEV
    tok_above = from_above[0:1] + TOK_DEV
    lane = lax.broadcasted_iota(jnp.int32, (8, 128), 1)
    rolled_own = pltpu.roll(jnp.broadcast_to(tok_own, (8, 128)), BELOW, 1)
    rolled_below = pltpu.roll(jnp.broadcast_to(tok_below, (8, 128)), BELOW, 1)
    rolled_above = pltpu.roll(jnp.broadcast_to(tok_above, (8, 128)), BELOW, 1)
    key_tok = jnp.concatenate(
        [
            jnp.where(lane < BELOW, rolled_below, rolled_own)[0:1],
            jnp.where(lane < BELOW, rolled_own, rolled_above)[0:1],
        ],
        axis=1,
    )
    col_own = jnp.transpose(jnp.broadcast_to(tok_own, (128, 128)))
    col_above = jnp.transpose(jnp.broadcast_to(tok_above, (128, 128)))

    band = jnp.sum(near_ref[:, 0:BAND_ROWS, :].astype(jnp.float32), axis=0)
    half = lax.broadcasted_iota(jnp.int32, (BAND_ROWS, 128), 1) < WINDOW
    band = jnp.concatenate([jnp.where(half, band, 0.0), jnp.where(half, 0.0, band)], axis=0)
    slot = (lax.broadcasted_iota(jnp.int32, (128, 256), 0) % WINDOW - 16).astype(jnp.float32)
    pick_key = (slot == key_tok).astype(jnp.bfloat16)
    spread = dot(band.astype(jnp.bfloat16), pick_key).astype(jnp.bfloat16)

    row_head = lax.broadcasted_iota(jnp.int32, (128, 128), 0) // QB
    lane_head = lax.broadcasted_iota(jnp.int32, (128, 128), 1) // 32
    own_head = row_head == lane_head
    entry = lax.broadcasted_iota(jnp.int32, (128, WINDOW), 1)
    entry_tok = (2 * ((entry % 32) // 4) + entry // 32).astype(jnp.float32)
    entry_head = entry % 4 == lax.broadcasted_iota(jnp.int32, (128, WINDOW), 0) // QB
    key_lane = lax.broadcasted_iota(jnp.int32, (128, KW), 1)
    for b in range(n_query // QB):
        at = b * QB
        queries = q_scr[at : at + QB, :]
        stacked = jnp.where(own_head, jnp.concatenate([queries] * heads, axis=0), 0)
        keys = k_scr[at : at + KW, :]
        tok_col = col_own[at : at + QB, 0:WINDOW] if at < atoms else col_above[0:QB, 0:WINDOW]
        pick = (jnp.concatenate([tok_col] * heads, axis=0) == entry_tok) & entry_head
        bias = dot(pick.astype(jnp.bfloat16), spread[:, at : at + KW])
        scores = dot_nt(stacked, keys) * (1.0 / math.sqrt(32)) + bias
        key_index = flat * atoms - BELOW + at + key_lane
        scores = jnp.where((key_index >= 0) & (key_index < total), scores, -jnp.inf)
        exponent = jnp.exp(scores - jnp.max(scores, axis=-1, keepdims=True))
        weights = (exponent / jnp.sum(exponent, axis=-1, keepdims=True)).astype(jnp.bfloat16)
        mixed = jnp.where(own_head, dot(weights, v_scr[at : at + KW, :]), 0.0)
        mixed = (mixed[0:32] + mixed[32:64]) + (mixed[64:96] + mixed[96:128])
        gate_scr[at : at + QB, :] = gate_scr[at : at + QB, :] * mixed
    attended = gate_scr[...].astype(jnp.bfloat16)
    atom_out = (wide[BELOW : BELOW + n_query, :] + dot(attended, wout_ref[...])).astype(
        jnp.bfloat16
    )
    atom_out_ref[...] = atom_out[0:atoms]
    next_out_ref[0:16, :] = atom_out[atoms : atoms + 16]
    next_out_ref[16:, :] = jnp.zeros((atoms - 16, 128), jnp.bfloat16)
    shared_ref[...] = col_own.astype(jnp.bfloat16)
    features = jnp.maximum(dot(atom_out, wagg_ref[...]), 0.0)
    tokens = lax.broadcasted_iota(jnp.int32, (TOK_DEV, 128), 0).astype(jnp.float32)
    member = (tok_own == tokens).astype(jnp.float32)
    member_next = ((tok_above == tokens) & (key_lane[0:TOK_DEV] < QB)).astype(jnp.float32)[:, 0:QB]
    counts = jnp.sum(member, axis=1, keepdims=True) + jnp.sum(member_next, axis=1, keepdims=True)
    totals = dot(member, features[0:atoms], precision=lax.Precision.HIGHEST) + dot(
        member_next, features[atoms:], precision=lax.Precision.HIGHEST
    )
    token_single = (totals / counts).astype(jnp.bfloat16)
    token_ref[...] = token_single
    singles = dot(token_single, wsingle_ref[...]).astype(jnp.bfloat16)
    singles_ref[...] = singles


def atom_part(place, cross, own, tok_rows, near, atom_gain, w_attn, w_out, w_agg, w_single):
    atoms = own.shape[0]
    vmem = pl.BlockSpec(memory_space=pltpu.VMEM)
    return pl.pallas_call(
        atom_kernel,
        in_specs=[pl.BlockSpec(memory_space=pltpu.SMEM)] + [vmem] * 9,
        out_specs=[vmem] * 5,
        out_shape=[
            jax.ShapeDtypeStruct((atoms, 128), jnp.bfloat16),
            jax.ShapeDtypeStruct((atoms, 128), jnp.bfloat16),
            jax.ShapeDtypeStruct((atoms, 128), jnp.bfloat16),
            jax.ShapeDtypeStruct((TOK_DEV, 384), jnp.bfloat16),
            jax.ShapeDtypeStruct((TOK_DEV, 256), jnp.bfloat16),
        ],
        scratch_shapes=[
            pltpu.VMEM((atoms + KW, 128), jnp.float32),
            pltpu.VMEM((atoms + QB, 128), jnp.bfloat16),
            pltpu.VMEM((atoms + KW, 128), jnp.bfloat16),
            pltpu.VMEM((atoms + KW, 128), jnp.bfloat16),
            pltpu.VMEM((atoms + QB, 128), jnp.float32),
        ],
        cost_estimate=pl.CostEstimate(flops=10**9, bytes_accessed=10**6, transcendentals=10**5),
        compiler_params=pltpu.CompilerParams(vmem_limit_bytes=VMEM_BYTES),
        name="atoms",
    )(place, cross, own, tok_rows, near, atom_gain, w_attn, w_out, w_agg, w_single)


def whole(array):
    return pl.BlockSpec(array.shape, lambda i: (0,) * array.ndim)


def halved_gate(w_in_ref, w_in_scr):
    width = w_in_ref.shape[1] // 2
    w_in_scr[:, :width] = w_in_ref[:, :width] * 0.5
    w_in_scr[:, width:] = w_in_ref[:, width:]


def transition(cells, w_in_scr, w_out_ref):
    width = w_out_ref.shape[0]
    wide = cells.reshape(-1, 128).astype(jnp.float32)
    hidden = dot(normalize(wide).astype(jnp.bfloat16), w_in_scr[...])
    gate = hidden[:, :width].astype(jnp.bfloat16)
    up = hidden[:, width:].astype(jnp.bfloat16)
    return wide + dot((gate + gate * jnp.tanh(gate)) * up, w_out_ref[...])


def early_kernel(pair_ref, w_in_ref, w_out_ref, band_ref, out_ref, w_in_scr):
    rows, cols, _ = pair_ref.shape

    @pl.when(pl.program_id(0) == 0)
    def _():
        halved_gate(w_in_ref, w_in_scr)

    step = SUB // cols
    for k in range(0, rows, step):
        moved = transition(pair_ref[k : k + step], w_in_scr, w_out_ref)
        out_ref[k : k + step] = moved.astype(jnp.bfloat16).reshape(step, cols, 128)


def early_part(pair_act, w_in, w_out, band):
    rows, cols, width = pair_act.shape
    block = pl.BlockSpec((EARLY, cols, width), lambda i: (ROWS // EARLY * i, 0, 0))
    cells = rows // ROWS * EARLY * cols
    return pl.pallas_call(
        early_kernel,
        grid=(rows // ROWS,),
        in_specs=[block, whole(w_in), whole(w_out), pl.BlockSpec(memory_space=pl.ANY)],
        out_specs=block,
        out_shape=jax.ShapeDtypeStruct(pair_act.shape, jnp.bfloat16),
        scratch_shapes=[pltpu.VMEM(w_in.shape, jnp.bfloat16)],
        cost_estimate=pl.CostEstimate(
            flops=cells * 196608 * 2, bytes_accessed=cells * 512, transcendentals=0
        ),
        compiler_params=pltpu.CompilerParams(vmem_limit_bytes=VMEM_BYTES),
        name="pair_early",
    )(pair_act, w_in, w_out, band)


def last_kernel(
    place_ref, pair_ref, done_ref, w_in_ref, w_out_ref, own_ref, other_ref, col_ref,
    out_ref, w_in_scr, row_scr, col_scr,
):
    i = pl.program_id(0)
    rows, cols, _ = pair_ref.shape

    @pl.when(i == 0)
    def _():
        halved_gate(w_in_ref, w_in_scr)
        row, col = place_ref[0], place_ref[1]
        half = col // 8
        for block in range(8):
            at = slice(block * TOK_DEV, (block + 1) * TOK_DEV)
            row_at = pl.ds(pl.multiple_of((block ^ (col % 8)) * 16, 16), 16)
            col_at = pl.ds(pl.multiple_of((block ^ row) * 16, 16), 16)
            own_to = pl.ds(pl.multiple_of(half * 128 + block * 16, 16), 16)
            other_to = pl.ds(pl.multiple_of((1 - half) * 128 + block * 16, 16), 16)
            row_scr[own_to, :] = own_ref[row_at, 0:128].astype(jnp.float32)
            row_scr[other_to, :] = other_ref[row_at, 0:128].astype(jnp.float32)
            col_scr[at, :] = col_ref[col_at, 128:256].astype(jnp.float32)

    base = pl.multiple_of(i * rows, rows)
    col_add = col_scr[...]
    step = SUB // cols
    for k in range(EARLY, rows, step):
        moved = transition(pair_ref[k : k + step], w_in_scr, w_out_ref)
        for s in range(step):
            extra = row_scr[pl.ds(base + k + s, 1), :] + col_add
            out_ref[k + s] = (moved[s * cols : (s + 1) * cols] + extra).astype(jnp.bfloat16)
    for r in range(EARLY):
        extra = row_scr[pl.ds(base + r, 1), :] + col_add
        out_ref[r] = (done_ref[r].astype(jnp.float32) + extra).astype(jnp.bfloat16)


def last_part(place, pair_act, done, w_in, w_out, own, other, col):
    rows, cols, width = pair_act.shape
    block = pl.BlockSpec((ROWS, cols, width), lambda i: (i, 0, 0))
    done_block = pl.BlockSpec((EARLY, cols, width), lambda i: (ROWS // EARLY * i, 0, 0))
    return pl.pallas_call(
        last_kernel,
        grid=(rows // ROWS,),
        in_specs=[pl.BlockSpec(memory_space=pltpu.SMEM), block, done_block]
        + [whole(x) for x in (w_in, w_out, own, other, col)],
        out_specs=block,
        out_shape=jax.ShapeDtypeStruct(pair_act.shape, jnp.bfloat16),
        scratch_shapes=[
            pltpu.VMEM(w_in.shape, jnp.bfloat16),
            pltpu.VMEM((rows, width), jnp.float32),
            pltpu.VMEM((cols, width), jnp.float32),
        ],
        cost_estimate=pl.CostEstimate(
            flops=rows * cols * 196608 * 2, bytes_accessed=rows * cols * 512, transcendentals=0
        ),
        compiler_params=pltpu.CompilerParams(vmem_limit_bytes=VMEM_BYTES),
        name="pair_last",
    )(place, pair_act, done, w_in, w_out, own, other, col)


def on_device(
    pair_act, atom_act, atom_token, atom_gain, w_attn, w_out, w_bias, w_trans_in, w_trans_out,
    w_agg, w_single,
):
    atom_n = atom_act.shape[0]
    n_row, n_col = lax.axis_size("row"), lax.axis_size("col")
    devices = n_row * n_col
    row_index, col_index = lax.axis_index("row"), lax.axis_index("col")
    flat = row_index * n_col + col_index
    place = jnp.stack([row_index, col_index, flat, jnp.int32(devices * atom_n)]).astype(jnp.int32)
    both = ("row", "col")
    up = [(i, i + 1) for i in range(devices - 1)]
    firsts = [n_col * i for i in range(1, n_row)]
    ends = [(i - 1, i) for i in firsts] + [(i, i - 1) for i in firsts]
    turn = [
        (16 * a + 8 * h + k, 16 * k + 2 * a + h)
        for a in range(n_row)
        for h in range(2)
        for k in range(8)
    ]

    band, cross, tok_rows = band_biases(place, pair_act, w_bias, atom_act, atom_token)
    cross = lax.ppermute(cross, both, ends)
    near = lax.all_to_all(band, "col", 0, 0, tiled=True)
    done = early_part(pair_act, w_trans_in, w_trans_out, band)
    near, cross = lax.optimization_barrier((near, cross, done))[:2]
    atom_main, next_out, shared, token_single, singles = atom_part(
        place, cross, atom_act, tok_rows, near, atom_gain[None, :], w_attn, w_out, w_agg, w_single
    )
    held = singles
    for k in range(3):
        pairs = [(i, i ^ (1 << k)) for i in range(n_col)]
        held = jnp.concatenate([held, lax.ppermute(held, "col", pairs)])
    col_all = lax.ppermute(held, both, turn)
    other = lax.ppermute(held, "col", [(i, i ^ 8) for i in range(n_col)])
    from_below = lax.ppermute(next_out, both, up)
    pair_out = last_part(
        place, pair_act, done, w_trans_in, w_trans_out, held, other, col_all
    )
    from_below = lax.optimization_barrier((from_below, pair_out))[0]
    atom_out = jnp.where(shared < 0, from_below, atom_main)
    return (atom_out, token_single, pair_out)


def solution(mesh):
    both = P(("row", "col"), None)
    return jax.shard_map(
        on_device,
        mesh=mesh,
        in_specs=(P("row", "col", None), both, P(("row", "col"))) + (P(),) * 8,
        out_specs=(both, both, P("row", "col", None)),
        check_vma=False,
    )
```

time: 101 us -> 89.1 us (0.88)
  the two profiles are of different devices: /device:TPU:6 before, /device:TPU:1 now
where the time goes in v2:
time: 89.1 us; the launch traced here: 88.6 us
  Pallas kernels  46.3 us (52%)
  starting transfers between devices  30.9 us (35%)
  waiting for transfers between devices  5.3 us (6%)
  local copies, waits for them, and re-layouts  2.72 us (3%)
  other arithmetic  2.61 us (3%)
    pallas_call x1, Pallas kernels, last_part(): pl.pallas_call(last_kernel, grid=(rows // ROWS,), in_specs=[pl.BlockSpec(...  25.2 us
    ppermute x1, starting transfers between devices, on_device(): col_all = lax.ppermute(held, both, turn)  10.7 us
    pallas_call x1, Pallas kernels, early_part(): pl.pallas_call(early_kernel, grid=(rows // ROWS,), in_specs=[block, whole...  10.6 us
    all_to_all x1, starting transfers between devices, on_device(): near = lax.all_to_all(band, 'col', 0, 0, tiled=True)  8.46 us
    ppermute x1, starting transfers between devices, on_device(): from_below = lax.ppermute(next_out, both, up)  7.42 us
    pallas_call x1, Pallas kernels, band_biases(): pl.pallas_call(band_kernel, in_specs=[pl.BlockSpec(memory_space=pltpu.SME...  5.86 us
    ppermute x3, waiting for transfers between devices, on_device(): held = jnp.concatenate([held, lax.ppermute(held, 'col', pairs)])  5.21 us
    pallas_call x1, Pallas kernels, atom_part(): pl.pallas_call(atom_kernel, in_specs=[pl.BlockSpec(memory_space=pltpu.SME...  4.64 us
  transfers between devices with their start and end apart: 8, of which 4 were waited for; matrix products, arithmetic and copies ran while one was open for 1% of the time, Pallas kernels for 40%

profile of v2, /device:TPU:1, one launch (start us, length us, event | category | flops | bytes accessed | tf_op | source)
XLA Modules:
  0.0 88.6 jit_solution(7352263872011444539)
XLA Ops:
  0.6 0.6 pad_add_fusion.place_ref
  1.2 5.9 %band.1 = (bf16[16,128,128]{2,1,0:T(8,128)(2,1)}, bf16[96,128]{1,0:T(8,128)(2,1)}, bf16[16,128]{1,0:T(8,128)(2,1)}) custom-call(s32[4]{0:T(128)} %pad_add_fusion.place_ref, bf16[256,128,128]{2,1,0:T(8,128)(2,1)} %pair_ref.5, bf16[4,128]{1,0:T(4,128)(2,1)} %bitcast.6, bf16[128,128]{1,0:T(8,128)(2,1)} %own_ref.1, s32[1,128]{1,0:T(1,128)} %bitcast.7), custom_call_target="tpu_custom_call" | custom-call | flops 1000000000 | bytes 3000000 | tf_op jit(solution)/shard_map/band/pallas_call | solution.py:117
  7.1 8.5 %all-to-all-start = ((bf16[16,128,128]{2,1,0:T(8,128)(2,1)}), bf16[16,128,128]{2,1,0:T(8,128)(2,1)S(1)}, u32[]{:S(2)}, u32[]{:S(2)}) async-start(bf16[16,128,128]{2,1,0:T(8,128)(2,1)} %get-tuple-element.14.band_ref), calls=%async_computation | async-start | bytes 1048576 | tf_op jit(solution)/shard_map/all_to_all | solution.py:399
  15.6 0.7 collective-permute-start
  16.2 10.6 %pair_early.1.done_ref = bf16[256,128,128]{2,1,0:T(8,128)(2,1)} custom-call(bf16[256,128,128]{2,1,0:T(8,128)(2,1)} %pair_ref.5, bf16[128,1024]{1,0:T(8,128)(2,1)} %w_in_ref.3, bf16[512,128]{1,0:T(8,128)(2,1)} %w_out_ref.3, bf16[16,128,128]{2,1,0:T(8,128)(2,1)} %get-tuple-element.14.band_ref), custom_call_target="tpu_custom_call" | custom-call | flops 3221225472 | bytes 4194304 | tf_op jit(solution)/shard_map/pair_early/pallas_call | solution.py:302
  26.8 0.0 collective-permute-done.cross_ref
  26.8 0.0 copy-start.6
  26.8 0.1 all-to-all-done.near_ref
  26.9 0.0 copy-start
  26.9 0.5 copy-done.6
  27.4 0.3 copy-done
  27.6 4.6 %atoms.1 = (bf16[128,128]{1,0:T(8,128)(2,1)}, bf16[128,128]{1,0:T(8,128)(2,1)}, bf16[128,128]{1,0:T(8,128)(2,1)}, bf16[16,384]{1,0:T(8,128)(2,1)}, bf16[16,256]{1,0:T(8,128)(2,1)}) custom-call(s32[4]{0:T(128)} %pad_add_fusion.place_ref, bf16[96,128]{1,0:T(8,128)(2,1)} %copy-done.6, bf16[128,128]{1,0:T(8,128)(2,1)} %own_ref.1, ...), custom_call_target="tpu_custom_call" | custom-call | flops 1000000000 | bytes 1000000 | tf_op jit(solution)/shard_map/atoms/pallas_call | solution.py:242
  32.3 1.4 %collective-permute-start.2 = (bf16[16,256]{1,0:T(8,128)(2,1)}, bf16[16,256]{1,0:T(8,128)(2,1)S(1)}, u32[]{:S(2)}, u32[]{:S(2)}) collective-permute-start(bf16[16,256]{1,0:T(8,128)(2,1)} %get-tuple-element.21), channel_id=1, source_target_pairs={{0,1},{1,0},{2,3},{3,2},{4,5},{5,4},{6,7},{7,6},{8,9},{9,8},{10,11... | collective-permute-start | bytes 24584 | tf_op jit(solution)/shard_map/ppermute | solution.py:408
  33.7 0.7 constant_dynamic-update-slice_fusion.3
  34.4 0.3 collective-permute-done.2
  34.8 0.7 pad_maximum_fusion.1
  35.5 1.7 %collective-permute-start.3 = (bf16[32,256]{1,0:T(8,128)(2,1)S(1)}, bf16[32,256]{1,0:T(8,128)(2,1)S(1)}, u32[]{:S(2)}, u32[]{:S(2)}) collective-permute-start(bf16[32,256]{1,0:T(8,128)(2,1)S(1)} %pad_maximum_fusion.1), channel_id=1, source_target_pairs={{0,2},{1,3},{2,0},{3,1},{4,6},{5,7},{6,4},{7,5},{8,10},{9,11},{10,... | collective-permute-start | bytes 49160 | tf_op jit(solution)/shard_map/ppermute | solution.py:408
  37.2 2.3 %collective-permute-done.3 = bf16[32,256]{1,0:T(8,128)(2,1)S(1)} collective-permute-done((bf16[32,256]{1,0:T(8,128)(2,1)S(1)}, bf16[32,256]{1,0:T(8,128)(2,1)S(1)}, u32[]{:S(2)}, u32[]{:S(2)}) %collective-permute-start.3) | collective-permute-done | bytes 16416 | tf_op jit(solution)/shard_map/ppermute | solution.py:408
  39.5 0.7 pad_maximum_fusion
  40.2 0.2 collective-permute-start.4
  40.5 2.5 %collective-permute-done.4 = bf16[64,256]{1,0:T(8,128)(2,1)S(1)} collective-permute-done((bf16[64,256]{1,0:T(8,128)(2,1)S(1)}, bf16[64,256]{1,0:T(8,128)(2,1)S(1)}, u32[]{:S(2)}, u32[]{:S(2)}) %collective-permute-start.4) | collective-permute-done | bytes 32800 | tf_op jit(solution)/shard_map/ppermute | solution.py:408
  43.0 0.0 copy-start.3
  43.0 10.7 %collective-permute-start.6 = (bf16[128,256]{1,0:T(8,128)(2,1)S(1)}, bf16[128,256]{1,0:T(8,128)(2,1)S(1)}, u32[]{:S(2)}, u32[]{:S(2)}) collective-permute-start(bf16[128,256]{1,0:T(8,128)(2,1)S(1)} %constant_dynamic-update-slice_fusion.own_ref), channel_id=1, source_target_pairs={{0,0},{1,16},{2,32},{3,48},{4,64},{5,80},{6,96},{7,112},{8,1},{9,1... | collective-permute-start | bytes 196616 | tf_op jit(solution)/shard_map/ppermute | solution.py:409
  53.8 0.2 collective-permute-start.5
  54.0 0.0 copy-start.1
  54.0 0.0 copy-start.2
  54.0 7.4 %collective-permute-start.1 = (bf16[128,128]{1,0:T(8,128)(2,1)}, bf16[128,128]{1,0:T(8,128)(2,1)S(1)}, u32[]{:S(2)}, u32[]{:S(2)}) collective-permute-start(bf16[128,128]{1,0:T(8,128)(2,1)} %get-tuple-element.20), channel_id=1, source_target_pairs={{0,1},{1,2},{2,3},{3,4},{4,5},{5,6},{6,7},{7,8},{8,9},{9,10},{10,1... | collective-permute-start | bytes 98312 | tf_op jit(solution)/shard_map/ppermute | solution.py:411
  61.4 0.0 collective-permute-done.6.col_ref
  61.4 0.0 copy-start.4
  61.5 0.0 collective-permute-done.5.other_ref
  61.5 0.0 copy-done.3
  61.5 0.6 copy-done.4
  62.1 0.0 copy-start.5
  62.1 0.6 copy-done.5
  62.7 25.2 %pair_last.1 = bf16[256,128,128]{2,1,0:T(8,128)(2,1)} custom-call(s32[4]{0:T(128)} %pad_add_fusion.place_ref, bf16[256,128,128]{2,1,0:T(8,128)(2,1)} %pair_ref.5, bf16[256,128,128]{2,1,0:T(8,128)(2,1)} %pair_early.1.done_ref, bf16[128,1024]{1,0:T(8,128)(2,1)} %w_in_ref.3, bf16[512,128]{1,0:T(8,128)(2,1)} %w_out_ref.3, bf16[128,256]{1,0:T(8,128)(2,1)} %copy-done.3, ...), custom_call_target="tpu_custom_call" | custom-call | flops 12884901888 | bytes 16777216 | tf_op jit(solution)/shard_map/pair_last/pallas_call | solution.py:356
  87.9 0.0 collective-permute-done.1
  87.9 0.0 copy-done.1
  87.9 0.0 copy-done.2
  87.9 0.6 compare_select_fusion
  (3 shorter events, 0.0 us)
Async XLA Ops:
  7.1 19.8 %all-to-all-start = ((bf16[16,128,128]{2,1,0:T(8,128)(2,1)}), bf16[16,128,128]{2,1,0:T(8,128)(2,1)S(1)}, u32[]{:S(2)}, u32[]{:S(2)}) async-start(bf16[16,128,128]{2,1,0:T(8,128)(2,1)} %get-tuple-element.14.band_ref), calls=%async_computation | async-start | bytes 1048576 | tf_op jit(solution)/shard_map/all_to_all | solution.py:399
  15.6 11.2 %collective-permute-start = (bf16[96,128]{1,0:T(8,128)(2,1)}, bf16[96,128]{1,0:T(8,128)(2,1)S(1)}, u32[]{:S(2)}, u32[]{:S(2)}) collective-permute-start(bf16[96,128]{1,0:T(8,128)(2,1)} %get-tuple-element.15), channel_id=1, source_target_pairs={{15,16},{31,32},{47,48},{63,64},{79,80},{95,96},{111,112},{16,15},... | collective-permute-start | bytes 73736 | tf_op jit(solution)/shard_map/ppermute | solution.py:398
  26.8 0.6 copy-start.6
  26.9 0.8 copy-start
  32.3 2.5 %collective-permute-start.2 = (bf16[16,256]{1,0:T(8,128)(2,1)}, bf16[16,256]{1,0:T(8,128)(2,1)S(1)}, u32[]{:S(2)}, u32[]{:S(2)}) collective-permute-start(bf16[16,256]{1,0:T(8,128)(2,1)} %get-tuple-element.21), channel_id=1, source_target_pairs={{0,1},{1,0},{2,3},{3,2},{4,5},{5,4},{6,7},{7,6},{8,9},{9,8},{10,11... | collective-permute-start | bytes 24584 | tf_op jit(solution)/shard_map/ppermute | solution.py:408
  35.5 4.1 %collective-permute-start.3 = (bf16[32,256]{1,0:T(8,128)(2,1)S(1)}, bf16[32,256]{1,0:T(8,128)(2,1)S(1)}, u32[]{:S(2)}, u32[]{:S(2)}) collective-permute-start(bf16[32,256]{1,0:T(8,128)(2,1)S(1)} %pad_maximum_fusion.1), channel_id=1, source_target_pairs={{0,2},{1,3},{2,0},{3,1},{4,6},{5,7},{6,4},{7,5},{8,10},{9,11},{10,... | collective-permute-start | bytes 49160 | tf_op jit(solution)/shard_map/ppermute | solution.py:408
  40.2 2.8 %collective-permute-start.4 = (bf16[64,256]{1,0:T(8,128)(2,1)S(1)}, bf16[64,256]{1,0:T(8,128)(2,1)S(1)}, u32[]{:S(2)}, u32[]{:S(2)}) collective-permute-start(bf16[64,256]{1,0:T(8,128)(2,1)S(1)} %pad_maximum_fusion), channel_id=1, source_target_pairs={{0,4},{1,5},{2,6},{3,7},{4,0},{5,1},{6,2},{7,3},{8,12},{9,13},{10,... | collective-permute-start | bytes 98312 | tf_op jit(solution)/shard_map/ppermute | solution.py:408
  43.0 18.5 %copy-start.3 = (bf16[128,256]{1,0:T(8,128)(2,1)}, bf16[128,256]{1,0:T(8,128)(2,1)S(1)}, u32[]{:S(2)}) copy-start(bf16[128,256]{1,0:T(8,128)(2,1)S(1)} %constant_dynamic-update-slice_fusion.own_ref) | copy-start | bytes 196612
  43.0 18.4 %collective-permute-start.6 = (bf16[128,256]{1,0:T(8,128)(2,1)S(1)}, bf16[128,256]{1,0:T(8,128)(2,1)S(1)}, u32[]{:S(2)}, u32[]{:S(2)}) collective-permute-start(bf16[128,256]{1,0:T(8,128)(2,1)S(1)} %constant_dynamic-update-slice_fusion.own_ref), channel_id=1, source_target_pairs={{0,0},{1,16},{2,32},{3,48},{4,64},{5,80},{6,96},{7,112},{8,1},{9,1... | collective-permute-start | bytes 196616 | tf_op jit(solution)/shard_map/ppermute | solution.py:409
  53.8 7.7 %collective-permute-start.5 = (bf16[128,256]{1,0:T(8,128)(2,1)S(1)}, bf16[128,256]{1,0:T(8,128)(2,1)S(1)}, u32[]{:S(2)}, u32[]{:S(2)}) collective-permute-start(bf16[128,256]{1,0:T(8,128)(2,1)S(1)} %constant_dynamic-update-slice_fusion.own_ref), channel_id=1, source_target_pairs={{0,8},{1,9},{2,10},{3,11},{4,12},{5,13},{6,14},{7,15},{8,0},{9,1},... | collective-permute-start | bytes 196616 | tf_op jit(solution)/shard_map/ppermute | solution.py:410
  54.0 33.9 %copy-start.1 = (bf16[128,128]{1,0:T(8,128)(2,1)S(1)}, bf16[128,128]{1,0:T(8,128)(2,1)}, u32[]{:S(2)}) copy-start(bf16[128,128]{1,0:T(8,128)(2,1)} %get-tuple-element.23) | copy-start | bytes 98308
  54.0 33.9 %copy-start.2 = (bf16[128,128]{1,0:T(8,128)(2,1)S(1)}, bf16[128,128]{1,0:T(8,128)(2,1)}, u32[]{:S(2)}) copy-start(bf16[128,128]{1,0:T(8,128)(2,1)} %get-tuple-element.19) | copy-start | bytes 98308
  54.0 33.9 %collective-permute-start.1 = (bf16[128,128]{1,0:T(8,128)(2,1)}, bf16[128,128]{1,0:T(8,128)(2,1)S(1)}, u32[]{:S(2)}, u32[]{:S(2)}) collective-permute-start(bf16[128,128]{1,0:T(8,128)(2,1)} %get-tuple-element.20), channel_id=1, source_target_pairs={{0,1},{1,2},{2,3},{3,4},{4,5},{5,6},{6,7},{7,8},{8,9},{9,10},{10,1... | collective-permute-start | bytes 98312 | tf_op jit(solution)/shard_map/ppermute | solution.py:411
  61.4 0.6 copy-start.4
  62.1 0.6 copy-start.5

commit v3 on v2

--- a/solution.py
+++ b/solution.py
@@ -20,7 +20,8 @@
 EDGE = 48
 BLOCK_ROWS = BAND_ROWS + 16 + ABOVE
 BATCH = 3
-VMEM_BYTES = 56 * 1024 * 1024
+MIB = 1024 * 1024
+WIDE = 50
 ROWS = 64
 EARLY = 16
 SUB = 512
@@ -134,7 +135,7 @@
             pltpu.SemaphoreType.DMA((GROUPS,)),
         ],
         cost_estimate=pl.CostEstimate(flops=10**9, bytes_accessed=3 * 10**6, transcendentals=0),
-        compiler_params=pltpu.CompilerParams(vmem_limit_bytes=VMEM_BYTES),
+        compiler_params=pltpu.CompilerParams(vmem_limit_bytes=56 * MIB),
         name="band",
     )(place, pair_act, w_bias.T, atom_act, atom_token[None, :])
 
@@ -258,7 +259,7 @@
             pltpu.VMEM((atoms + QB, 128), jnp.float32),
         ],
         cost_estimate=pl.CostEstimate(flops=10**9, bytes_accessed=10**6, transcendentals=10**5),
-        compiler_params=pltpu.CompilerParams(vmem_limit_bytes=VMEM_BYTES),
+        compiler_params=pltpu.CompilerParams(vmem_limit_bytes=16 * MIB),
         name="atoms",
     )(place, cross, own, tok_rows, near, atom_gain, w_attn, w_out, w_agg, w_single)
 
@@ -309,7 +310,7 @@
         cost_estimate=pl.CostEstimate(
             flops=cells * 196608 * 2, bytes_accessed=cells * 512, transcendentals=0
         ),
-        compiler_params=pltpu.CompilerParams(vmem_limit_bytes=VMEM_BYTES),
+        compiler_params=pltpu.CompilerParams(vmem_limit_bytes=WIDE * MIB),
         name="pair_early",
     )(pair_act, w_in, w_out, band)
 
@@ -368,7 +369,7 @@
         cost_estimate=pl.CostEstimate(
             flops=rows * cols * 196608 * 2, bytes_accessed=rows * cols * 512, transcendentals=0
         ),
-        compiler_params=pltpu.CompilerParams(vmem_limit_bytes=VMEM_BYTES),
+        compiler_params=pltpu.CompilerParams(vmem_limit_bytes=WIDE * MIB),
         name="pair_last",
     )(place, pair_act, done, w_in, w_out, own, other, col)
 

time: 89.1 us -> 85.5 us (0.960)
  starting transfers between devices: 30.9 us -> 33.1 us
  waiting for transfers between devices: 5.3 us -> 3.49 us
  local copies, waits for them, and re-layouts: 2.72 us -> 1.09 us
  other arithmetic: 2.61 us -> 1.28 us
  Pallas kernels: 46.3 us -> 45.3 us
    ppermute x3, waiting for transfers between devices: 5.21 us -> 3.47 us  [on_device(): held = jnp.concatenate([held, lax.ppermute(held, 'col', pairs)])]
    unnamed x17 -> x25, local copies, waits for them, and re-layouts: 2.72 us -> 1.09 us
    concatenate x2, other arithmetic: 1.4 us -> 0.01 us  [on_device(): held = jnp.concatenate([held, lax.ppermute(held, 'col', pairs)])]
    ppermute x3, starting transfers between devices: 3.42 us -> 4.6 us  [on_device(): held = jnp.concatenate([held, lax.ppermute(held, 'col', pairs)])]
    ppermute x1, starting transfers between devices: 10.7 us -> 11.9 us  [on_device(): col_all = lax.ppermute(held, both, turn)]
  transfers between devices with their start and end apart: 8 -> 8, of which waited for: 4 -> 3; matrix products, arithmetic and copies ran while one was open for 1% -> 0% of each run, Pallas kernels for 40% -> 42%
where the time goes in v3:
time: 85.5 us; the launch traced here: 85.1 us
  Pallas kernels  45.3 us (53%)
  starting transfers between devices  33.1 us (39%)
  waiting for transfers between devices  3.49 us (4%)
  other arithmetic  1.28 us (1%)
  local copies, waits for them, and re-layouts  1.09 us (1%)
    pallas_call x1, Pallas kernels, last_part(): pl.pallas_call(last_kernel, grid=(rows // ROWS,), in_specs=[pl.BlockSpec(...  25.1 us
    ppermute x1, starting transfers between devices, on_device(): col_all = lax.ppermute(held, both, turn)  11.9 us
    pallas_call x1, Pallas kernels, early_part(): pl.pallas_call(early_kernel, grid=(rows // ROWS,), in_specs=[block, whole...  10.5 us
    all_to_all x1, starting transfers between devices, on_device(): near = lax.all_to_all(band, 'col', 0, 0, tiled=True)  8.46 us
    ppermute x1, starting transfers between devices, on_device(): from_below = lax.ppermute(next_out, both, up)  7.28 us
    pallas_call x1, Pallas kernels, band_biases(): pl.pallas_call(band_kernel, in_specs=[pl.BlockSpec(memory_space=pltpu.SME...  5.86 us
    ppermute x3, starting transfers between devices, on_device(): held = jnp.concatenate([held, lax.ppermute(held, 'col', pairs)])  4.6 us
    pallas_call x1, Pallas kernels, atom_part(): pl.pallas_call(atom_kernel, in_specs=[pl.BlockSpec(memory_space=pltpu.SME...  3.82 us
  transfers between devices with their start and end apart: 8, of which 3 were waited for; matrix products, arithmetic and copies ran while one was open for 0% of the time, Pallas kernels for 42%

profile of v3, /device:TPU:1, one launch (start us, length us, event | category | flops | bytes accessed | tf_op | source)
XLA Modules:
  0.0 85.1 jit_solution(3802806361628990819)
XLA Ops:
  0.6 0.0 copy-start.2
  0.6 0.0 copy-start.1
  0.7 0.7 pad_add_fusion.place_ref
  1.3 5.9 %band.1 = (bf16[16,128,128]{2,1,0:T(8,128)(2,1)}, bf16[96,128]{1,0:T(8,128)(2,1)}, bf16[16,128]{1,0:T(8,128)(2,1)}) custom-call(s32[4]{0:T(128)} %pad_add_fusion.place_ref, bf16[256,128,128]{2,1,0:T(8,128)(2,1)} %pair_ref.5, bf16[4,128]{1,0:T(4,128)(2,1)} %bitcast.7, bf16[128,128]{1,0:T(8,128)(2,1)} %own_ref.1, s32[1,128]{1,0:T(1,128)} %bitcast.8), custom_call_target="tpu_custom_call" | custom-call | flops 1000000000 | bytes 3000000 | tf_op jit(solution)/shard_map/band/pallas_call | solution.py:118
  7.2 8.5 %all-to-all-start = ((bf16[16,128,128]{2,1,0:T(8,128)(2,1)}), bf16[16,128,128]{2,1,0:T(8,128)(2,1)S(1)}, u32[]{:S(2)}, u32[]{:S(2)}) async-start(bf16[16,128,128]{2,1,0:T(8,128)(2,1)} %get-tuple-element.14.band_ref), calls=%async_computation | async-start | bytes 1048576 | tf_op jit(solution)/shard_map/all_to_all | solution.py:400
  15.6 0.7 collective-permute-start
  16.3 0.0 copy-done.2
  16.3 0.0 copy-done.1
  16.3 0.0 copy-start
  16.3 1.0 %copy-done = bf16[16,128,128]{2,1,0:T(8,128)(2,1)S(1)} copy-done((bf16[16,128,128]{2,1,0:T(8,128)(2,1)S(1)}, bf16[16,128,128]{2,1,0:T(8,128)(2,1)}, u32[]{:S(2)}) %copy-start) | copy-done | bytes 524312
  17.4 0.0 copy-start.3
  17.4 0.0 copy-start.4
  17.4 0.0 copy-start.5
  17.4 0.0 copy-start.6
  17.4 0.0 copy-start.7
  17.4 0.0 copy-start.8
  17.4 0.0 copy-start.9
  17.4 0.0 copy-start.10
  17.4 10.5 %pair_early.1.done_ref = bf16[256,128,128]{2,1,0:T(8,128)(2,1)} custom-call(bf16[256,128,128]{2,1,0:T(8,128)(2,1)} %pair_ref.5, bf16[128,1024]{1,0:T(8,128)(2,1)S(1)} %copy-done.1, bf16[512,128]{1,0:T(8,128)(2,1)S(1)} %copy-done.2, bf16[16,128,128]{2,1,0:T(8,128)(2,1)S(1)} %copy-done), custom_call_target="tpu_custom_call" | custom-call | flops 3221225472 | bytes 4194304 | tf_op jit(solution)/shard_map/pair_early/pallas_call | solution.py:303
  27.9 0.0 collective-permute-done.cross_ref
  27.9 0.0 all-to-all-done.near_ref
  28.0 0.0 copy-done.3
  28.0 0.0 copy-done.4
  28.0 0.0 copy-done.5
  28.0 0.0 copy-done.6
  28.0 0.0 copy-done.7
  28.0 0.0 copy-done.8
  28.0 0.0 copy-done.9
  28.0 0.0 copy-done.10
  28.0 3.8 %atoms.1 = (bf16[128,128]{1,0:T(8,128)(2,1)S(1)}, bf16[128,128]{1,0:T(8,128)(2,1)S(1)}, bf16[128,128]{1,0:T(8,128)(2,1)S(1)}, bf16[16,384]{1,0:T(8,128)(2,1)}, bf16[16,256]{1,0:T(8,128)(2,1)S(1)}) custom-call(s32[4]{0:T(128)S(1)} %copy-done.4, bf16[96,128]{1,0:T(8,128)(2,1)S(1)} %collective-permute-done.cross_ref, bf16[128,128]{1,0:T(8,128)(2,1)S(1)} %copy-done.3, ...), custom_call_target="tpu_custom_call" | custom-call | flops 1000000000 | bytes 1000000 | tf_op jit(solution)/shard_map/atoms/pallas_call | solution.py:243
  31.8 0.4 collective-permute-start.2
  32.2 0.8 collective-permute-done.2
  33.1 2.9 %collective-permute-start.3 = (bf16[32,256]{1,0:T(8,128)(2,1)S(1)}, bf16[32,256]{1,0:T(8,128)(2,1)S(1)}, u32[]{:S(2)}, u32[]{:S(2)}) collective-permute-start(bf16[32,256]{1,0:T(8,128)(2,1)S(1)} %pad_maximum_fusion.1), channel_id=1, source_target_pairs={{0,2},{1,3},{2,0},{3,1},{4,6},{5,7},{6,4},{7,5},{8,10},{9,11},{10,... | collective-permute-start | bytes 49160 | tf_op jit(solution)/shard_map/ppermute | solution.py:409
  35.9 1.2 %collective-permute-done.3 = bf16[32,256]{1,0:T(8,128)(2,1)S(1)} collective-permute-done((bf16[32,256]{1,0:T(8,128)(2,1)S(1)}, bf16[32,256]{1,0:T(8,128)(2,1)S(1)}, u32[]{:S(2)}, u32[]{:S(2)}) %collective-permute-start.3) | collective-permute-done | bytes 16416 | tf_op jit(solution)/shard_map/ppermute | solution.py:409
  37.2 1.3 %collective-permute-start.4 = (bf16[64,256]{1,0:T(8,128)(2,1)S(1)}, bf16[64,256]{1,0:T(8,128)(2,1)S(1)}, u32[]{:S(2)}, u32[]{:S(2)}) collective-permute-start(bf16[64,256]{1,0:T(8,128)(2,1)S(1)} %pad_maximum_fusion), channel_id=1, source_target_pairs={{0,4},{1,5},{2,6},{3,7},{4,0},{5,1},{6,2},{7,3},{8,12},{9,13},{10,... | collective-permute-start | bytes 98312 | tf_op jit(solution)/shard_map/ppermute | solution.py:409
  38.5 1.4 %collective-permute-done.4 = bf16[64,256]{1,0:T(8,128)(2,1)S(1)} collective-permute-done((bf16[64,256]{1,0:T(8,128)(2,1)S(1)}, bf16[64,256]{1,0:T(8,128)(2,1)S(1)}, u32[]{:S(2)}, u32[]{:S(2)}) %collective-permute-start.4) | collective-permute-done | bytes 32800 | tf_op jit(solution)/shard_map/ppermute | solution.py:409
  39.9 11.9 %collective-permute-start.6 = (bf16[128,256]{1,0:T(8,128)(2,1)S(1)}, bf16[128,256]{1,0:T(8,128)(2,1)S(1)}, u32[]{:S(2)}, u32[]{:S(2)}) collective-permute-start(bf16[128,256]{1,0:T(8,128)(2,1)S(1)} %constant_dynamic-update-slice_fusion.own_ref), channel_id=1, source_target_pairs={{0,0},{1,16},{2,32},{3,48},{4,64},{5,80},{6,96},{7,112},{8,1},{9,1... | collective-permute-start | bytes 196616 | tf_op jit(solution)/shard_map/ppermute | solution.py:410
  51.8 0.2 collective-permute-start.5
  52.0 7.3 %collective-permute-start.1 = (bf16[128,128]{1,0:T(8,128)(2,1)S(1)}, bf16[128,128]{1,0:T(8,128)(2,1)S(1)}, u32[]{:S(2)}, u32[]{:S(2)}) collective-permute-start(bf16[128,128]{1,0:T(8,128)(2,1)S(1)} %get-tuple-element.20), channel_id=1, source_target_pairs={{0,1},{1,2},{2,3},{3,4},{4,5},{5,6},{6,7},{7,8},{8,9},{9,10},{10,1... | collective-permute-start | bytes 98312 | tf_op jit(solution)/shard_map/ppermute | solution.py:412
  59.3 0.0 collective-permute-done.6.col_ref
  59.3 0.0 collective-permute-done.5.other_ref
  59.4 25.1 %pair_last.1 = bf16[256,128,128]{2,1,0:T(8,128)(2,1)} custom-call(s32[4]{0:T(128)S(1)} %copy-done.4, bf16[256,128,128]{2,1,0:T(8,128)(2,1)} %pair_ref.5, bf16[256,128,128]{2,1,0:T(8,128)(2,1)} %pair_early.1.done_ref, bf16[128,1024]{1,0:T(8,128)(2,1)S(1)} %copy-done.1, bf16[512,128]{1,0:T(8,128)(2,1)S(1)} %copy-done.2, ...), custom_call_target="tpu_custom_call" | custom-call | flops 12884901888 | bytes 16777216 | tf_op jit(solution)/shard_map/pair_last/pallas_call | solution.py:357
  84.4 0.0 collective-permute-done.1
  84.5 0.6 compare_select_fusion
  (6 shorter events, 0.0 us)
Async XLA Ops:
  0.6 15.7 %copy-start.2 = (bf16[512,128]{1,0:T(8,128)(2,1)S(1)}, bf16[512,128]{1,0:T(8,128)(2,1)}, u32[]{:S(2)}) copy-start(bf16[512,128]{1,0:T(8,128)(2,1)} %w_out_ref.3) | copy-start | bytes 393220
  0.6 15.7 %copy-start.1 = (bf16[128,1024]{1,0:T(8,128)(2,1)S(1)}, bf16[128,1024]{1,0:T(8,128)(2,1)}, u32[]{:S(2)}) copy-start(bf16[128,1024]{1,0:T(8,128)(2,1)} %w_in_ref.3) | copy-start | bytes 786436
  7.2 20.8 %all-to-all-start = ((bf16[16,128,128]{2,1,0:T(8,128)(2,1)}), bf16[16,128,128]{2,1,0:T(8,128)(2,1)S(1)}, u32[]{:S(2)}, u32[]{:S(2)}) async-start(bf16[16,128,128]{2,1,0:T(8,128)(2,1)} %get-tuple-element.14.band_ref), calls=%async_computation | async-start | bytes 1048576 | tf_op jit(solution)/shard_map/all_to_all | solution.py:400
  15.6 12.3 %collective-permute-start = (bf16[96,128]{1,0:T(8,128)(2,1)}, bf16[96,128]{1,0:T(8,128)(2,1)S(1)}, u32[]{:S(2)}, u32[]{:S(2)}) collective-permute-start(bf16[96,128]{1,0:T(8,128)(2,1)} %get-tuple-element.15), channel_id=1, source_target_pairs={{15,16},{31,32},{47,48},{63,64},{79,80},{95,96},{111,112},{16,15},... | collective-permute-start | bytes 73736 | tf_op jit(solution)/shard_map/ppermute | solution.py:399
  16.3 1.0 %copy-start = (bf16[16,128,128]{2,1,0:T(8,128)(2,1)S(1)}, bf16[16,128,128]{2,1,0:T(8,128)(2,1)}, u32[]{:S(2)}) copy-start(bf16[16,128,128]{2,1,0:T(8,128)(2,1)} %get-tuple-element.14.band_ref) | copy-start | bytes 1572868
  17.4 10.6 %copy-start.3 = (bf16[128,128]{1,0:T(8,128)(2,1)S(1)}, bf16[128,128]{1,0:T(8,128)(2,1)}, u32[]{:S(2)}) copy-start(bf16[128,128]{1,0:T(8,128)(2,1)} %own_ref.1) | copy-start | bytes 98308
  17.4 10.6 %copy-start.4 = (s32[4]{0:T(128)S(1)}, s32[4]{0:T(128)}, u32[]{:S(2)}) copy-start(s32[4]{0:T(128)} %pad_add_fusion.place_ref) | copy-start | bytes 52
  17.4 10.6 %copy-start.5 = (bf16[384,256]{1,0:T(8,128)(2,1)S(1)}, bf16[384,256]{1,0:T(8,128)(2,1)}, u32[]{:S(2)}) copy-start(bf16[384,256]{1,0:T(8,128)(2,1)} %wsingle_ref.1) | copy-start | bytes 589828
  17.4 10.6 %copy-start.6 = (bf16[128,512]{1,0:T(8,128)(2,1)S(1)}, bf16[128,512]{1,0:T(8,128)(2,1)}, u32[]{:S(2)}) copy-start(bf16[128,512]{1,0:T(8,128)(2,1)} %wattn_ref.1) | copy-start | bytes 393220
  17.4 10.6 %copy-start.7 = (bf16[128,384]{1,0:T(8,128)(2,1)S(1)}, bf16[128,384]{1,0:T(8,128)(2,1)}, u32[]{:S(2)}) copy-start(bf16[128,384]{1,0:T(8,128)(2,1)} %wagg_ref.1) | copy-start | bytes 294916
  17.4 10.6 %copy-start.8 = (bf16[128,128]{1,0:T(8,128)(2,1)S(1)}, bf16[128,128]{1,0:T(8,128)(2,1)}, u32[]{:S(2)}) copy-start(bf16[128,128]{1,0:T(8,128)(2,1)} %wout_ref.1) | copy-start | bytes 98308
  17.4 10.6 %copy-start.9 = (bf16[16,128]{1,0:T(8,128)(2,1)S(1)}, bf16[16,128]{1,0:T(8,128)(2,1)}, u32[]{:S(2)}) copy-start(bf16[16,128]{1,0:T(8,128)(2,1)} %get-tuple-element.17.tok_ref) | copy-start | bytes 12292
  17.4 10.6 %copy-start.10 = (f32[128]{0:T(128)S(1)}, f32[128]{0:T(128)}, u32[]{:S(2)}) copy-start(f32[128]{0:T(128)} %param.14) | copy-start | bytes 1540
  31.8 1.2 %collective-permute-start.2 = (bf16[16,256]{1,0:T(8,128)(2,1)S(1)}, bf16[16,256]{1,0:T(8,128)(2,1)S(1)}, u32[]{:S(2)}, u32[]{:S(2)}) collective-permute-start(bf16[16,256]{1,0:T(8,128)(2,1)S(1)} %get-tuple-element.21), channel_id=1, source_target_pairs={{0,1},{1,0},{2,3},{3,2},{4,5},{5,4},{6,7},{7,6},{8,9},{9,8},{10,11... | collective-permute-start | bytes 24584 | tf_op jit(solution)/shard_map/ppermute | solution.py:409
  33.1 4.1 %collective-permute-start.3 = (bf16[32,256]{1,0:T(8,128)(2,1)S(1)}, bf16[32,256]{1,0:T(8,128)(2,1)S(1)}, u32[]{:S(2)}, u32[]{:S(2)}) collective-permute-start(bf16[32,256]{1,0:T(8,128)(2,1)S(1)} %pad_maximum_fusion.1), channel_id=1, source_target_pairs={{0,2},{1,3},{2,0},{3,1},{4,6},{5,7},{6,4},{7,5},{8,10},{9,11},{10,... | collective-permute-start | bytes 49160 | tf_op jit(solution)/shard_map/ppermute | solution.py:409
  37.2 2.8 %collective-permute-start.4 = (bf16[64,256]{1,0:T(8,128)(2,1)S(1)}, bf16[64,256]{1,0:T(8,128)(2,1)S(1)}, u32[]{:S(2)}, u32[]{:S(2)}) collective-permute-start(bf16[64,256]{1,0:T(8,128)(2,1)S(1)} %pad_maximum_fusion), channel_id=1, source_target_pairs={{0,4},{1,5},{2,6},{3,7},{4,0},{5,1},{6,2},{7,3},{8,12},{9,13},{10,... | collective-permute-start | bytes 98312 | tf_op jit(solution)/shard_map/ppermute | solution.py:409
  39.9 19.4 %collective-permute-start.6 = (bf16[128,256]{1,0:T(8,128)(2,1)S(1)}, bf16[128,256]{1,0:T(8,128)(2,1)S(1)}, u32[]{:S(2)}, u32[]{:S(2)}) collective-permute-start(bf16[128,256]{1,0:T(8,128)(2,1)S(1)} %constant_dynamic-update-slice_fusion.own_ref), channel_id=1, source_target_pairs={{0,0},{1,16},{2,32},{3,48},{4,64},{5,80},{6,96},{7,112},{8,1},{9,1... | collective-permute-start | bytes 196616 | tf_op jit(solution)/shard_map/ppermute | solution.py:410
  51.8 7.5 %collective-permute-start.5 = (bf16[128,256]{1,0:T(8,128)(2,1)S(1)}, bf16[128,256]{1,0:T(8,128)(2,1)S(1)}, u32[]{:S(2)}, u32[]{:S(2)}) collective-permute-start(bf16[128,256]{1,0:T(8,128)(2,1)S(1)} %constant_dynamic-update-slice_fusion.own_ref), channel_id=1, source_target_pairs={{0,8},{1,9},{2,10},{3,11},{4,12},{5,13},{6,14},{7,15},{8,0},{9,1},... | collective-permute-start | bytes 196616 | tf_op jit(solution)/shard_map/ppermute | solution.py:411
  52.0 32.4 %collective-permute-start.1 = (bf16[128,128]{1,0:T(8,128)(2,1)S(1)}, bf16[128,128]{1,0:T(8,128)(2,1)S(1)}, u32[]{:S(2)}, u32[]{:S(2)}) collective-permute-start(bf16[128,128]{1,0:T(8,128)(2,1)S(1)} %get-tuple-element.20), channel_id=1, source_target_pairs={{0,1},{1,2},{2,3},{3,4},{4,5},{5,6},{6,7},{7,8},{8,9},{9,10},{10,1... | collective-permute-start | bytes 98312 | tf_op jit(solution)/shard_map/ppermute | solution.py:412

commit v4 on v3

--- a/solution.py
+++ b/solution.py
@@ -3,6 +3,7 @@
 
 import jax
 import jax.numpy as jnp
+import numpy as np
 from jax import lax
 from jax.experimental import pallas as pl
 from jax.experimental.pallas import tpu as pltpu
@@ -42,7 +43,8 @@
 
 
 def band_kernel(
-    place_ref, pair_ref, weight_ref, atom_ref, token_ref, out_ref, cross_ref, tok_ref, cells, sems
+    place_ref, pair_ref, weight_ref, atom_ref, token_ref, far_atom_ref, far_token_ref, out_ref,
+    tok_ref, cells, sems,
 ):
     row, col = place_ref[0], place_ref[1]
     shift = col - 2 * row
@@ -72,26 +74,35 @@
     low = BAND_ROWS
     last = out_ref.shape[0] - 1
 
-    def to_above(ref, at):
-        ref[at : at + 16, :] = tok_rows
-        ref[at + 16 : at + 16 + BELOW, :] = atom_ref[atoms - BELOW :, :]
-
-    def to_below(ref, at):
-        ref[at : at + 16, :] = tok_rows
-        ref[at + 16 : at + 16 + ABOVE, :] = atom_ref[0:ABOVE, :]
-
-    to_above(out_ref.at[jnp.minimum(col + 1, last)], low)
-    to_below(out_ref.at[jnp.maximum(col - 1, 0)], low)
+    def to_above(ref, rows, source):
+        ref[low : low + 16, :] = rows
+        ref[low + 16 : low + 16 + BELOW, :] = source[atoms - BELOW :, :]
+
+    def to_below(ref, rows, source):
+        ref[low : low + 16, :] = rows
+        ref[low + 16 : low + 16 + ABOVE, :] = source[0:ABOVE, :]
+
+    @pl.when(col < last)
+    def _():
+        to_above(out_ref.at[col + 1], tok_rows, atom_ref)
+
+    @pl.when(col > 0)
+    def _():
+        to_below(out_ref.at[col - 1], tok_rows, atom_ref)
+
+    def far_rows(first_token):
+        far = (far_token_ref[...] - first_token).astype(jnp.float32)
+        return jnp.broadcast_to(far, (16, 128)).astype(jnp.bfloat16)
+
+    wide_row = TOK_DEV * (last + 1)
 
     @pl.when(col == last)
     def _():
-        to_above(cross_ref, 0)
-        to_below(out_ref.at[last - 1], low)
+        to_above(out_ref.at[0], far_rows(place_ref[2] * TOK_DEV - wide_row), far_atom_ref)
 
     @pl.when(col == 0)
     def _():
-        to_below(cross_ref, 0)
-        to_above(out_ref.at[1], low)
+        to_below(out_ref.at[last], far_rows(place_ref[2] * TOK_DEV + wide_row), far_atom_ref)
 
     weight = jnp.concatenate(
         [weight_ref[...].astype(jnp.float32), jnp.zeros((12, 128), jnp.float32)], axis=0
@@ -113,21 +124,18 @@
             out_ref[pl.ds(first + j, 1), 0:BAND_ROWS, :] = kept.astype(jnp.bfloat16)[None]
 
 
-def band_biases(place, pair_act, w_bias, atom_act, atom_token):
+def band_biases(place, pair_act, w_bias, atom_act, atom_token, far_atoms, far_tokens):
     vmem = pl.BlockSpec(memory_space=pltpu.VMEM)
     return pl.pallas_call(
         band_kernel,
         in_specs=[
             pl.BlockSpec(memory_space=pltpu.SMEM),
             pl.BlockSpec(memory_space=pl.ANY),
-            vmem,
-            vmem,
-            vmem,
-        ],
-        out_specs=[vmem] * 3,
+        ]
+        + [vmem] * 5,
+        out_specs=[vmem] * 2,
         out_shape=[
             jax.ShapeDtypeStruct((16, BLOCK_ROWS, 128), jnp.bfloat16),
-            jax.ShapeDtypeStruct((16 + ABOVE, 128), jnp.bfloat16),
             jax.ShapeDtypeStruct((16, 128), jnp.bfloat16),
         ],
         scratch_shapes=[
@@ -137,11 +145,13 @@
         cost_estimate=pl.CostEstimate(flops=10**9, bytes_accessed=3 * 10**6, transcendentals=0),
         compiler_params=pltpu.CompilerParams(vmem_limit_bytes=56 * MIB),
         name="band",
-    )(place, pair_act, w_bias.T, atom_act, atom_token[None, :])
+    )(
+        place, pair_act, w_bias.T, atom_act, atom_token[None, :], far_atoms, far_tokens[None, :]
+    )
 
 
 def atom_kernel(
-    place_ref, cross_ref, own_ref, tok_ref, near_ref, gain_ref, wattn_ref, wout_ref,
+    place_ref, own_ref, tok_ref, near_ref, gain_ref, wattn_ref, wout_ref,
     wagg_ref, wsingle_ref, atom_out_ref, next_out_ref, shared_ref, token_ref, singles_ref,
     wide, q_scr, k_scr, v_scr, gate_scr,
 ):
@@ -153,11 +163,10 @@
     col = place_ref[1]
     last = near_ref.shape[0] - 1
     low = BAND_ROWS
-    from_below = near_ref[jnp.maximum(col - 1, 0), low : low + 16 + BELOW, :].astype(jnp.float32)
-    from_above = near_ref[jnp.minimum(col + 1, last), low:, :].astype(jnp.float32)
-    cross = cross_ref[...].astype(jnp.float32)
-    from_below = jnp.where(col == 0, cross[0 : 16 + BELOW], from_below)
-    from_above = jnp.where(col == last, cross, from_above)
+    below = jnp.where(col == 0, last, col - 1)
+    above = jnp.where(col == last, 0, col + 1)
+    from_below = near_ref[below, low : low + 16 + BELOW, :].astype(jnp.float32)
+    from_above = near_ref[above, low:, :].astype(jnp.float32)
     wide[0:BELOW, :] = from_below[16:]
     wide[BELOW : BELOW + atoms, :] = own_ref[...].astype(jnp.float32)
     wide[BELOW + atoms :, :] = from_above[16:]
@@ -237,12 +246,12 @@
     singles_ref[...] = singles
 
 
-def atom_part(place, cross, own, tok_rows, near, atom_gain, w_attn, w_out, w_agg, w_single):
+def atom_part(place, own, tok_rows, near, atom_gain, w_attn, w_out, w_agg, w_single):
     atoms = own.shape[0]
     vmem = pl.BlockSpec(memory_space=pltpu.VMEM)
     return pl.pallas_call(
         atom_kernel,
-        in_specs=[pl.BlockSpec(memory_space=pltpu.SMEM)] + [vmem] * 9,
+        in_specs=[pl.BlockSpec(memory_space=pltpu.SMEM)] + [vmem] * 8,
         out_specs=[vmem] * 5,
         out_shape=[
             jax.ShapeDtypeStruct((atoms, 128), jnp.bfloat16),
@@ -261,7 +270,7 @@
         cost_estimate=pl.CostEstimate(flops=10**9, bytes_accessed=10**6, transcendentals=10**5),
         compiler_params=pltpu.CompilerParams(vmem_limit_bytes=16 * MIB),
         name="atoms",
-    )(place, cross, own, tok_rows, near, atom_gain, w_attn, w_out, w_agg, w_single)
+    )(place, own, tok_rows, near, atom_gain, w_attn, w_out, w_agg, w_single)
 
 
 def whole(array):
@@ -325,12 +334,12 @@
     @pl.when(i == 0)
     def _():
         halved_gate(w_in_ref, w_in_scr)
-        row, col = place_ref[0], place_ref[1]
+        col, sender = place_ref[1], place_ref[4]
         half = col // 8
         for block in range(8):
             at = slice(block * TOK_DEV, (block + 1) * TOK_DEV)
             row_at = pl.ds(pl.multiple_of((block ^ (col % 8)) * 16, 16), 16)
-            col_at = pl.ds(pl.multiple_of((block ^ row) * 16, 16), 16)
+            col_at = pl.ds(pl.multiple_of((block ^ sender) * 16, 16), 16)
             own_to = pl.ds(pl.multiple_of(half * 128 + block * 16, 16), 16)
             other_to = pl.ds(pl.multiple_of((1 - half) * 128 + block * 16, 16), 16)
             row_scr[own_to, :] = own_ref[row_at, 0:128].astype(jnp.float32)
@@ -374,6 +383,51 @@
     )(place, pair_act, done, w_in, w_out, own, other, col)
 
 
+def chip_of(row, col):
+    x_lo, z = divmod(row, 4)
+    y, rest = divmod(col, 4)
+    return (2 * (rest // 2) + x_lo, y, z)
+
+
+def hops(one, other):
+    return sum(min((a - b) % 4, (b - a) % 4) for a, b in zip(one, other))
+
+
+def assigned(costs, most):
+    owner = {}
+
+    def place(source, seen):
+        for target in sorted(range(len(costs)), key=lambda t: costs[source][t]):
+            if costs[source][target] <= most and target not in seen:
+                seen.add(target)
+                if target not in owner or place(owner[target], seen):
+                    owner[target] = source
+                    return True
+        return False
+
+    for source in range(len(costs)):
+        if not place(source, set()):
+            return None
+    return {source: target for target, source in owner.items()}
+
+
+def column_turn():
+    pairs = []
+    for row in range(8):
+        for half in range(2):
+            column = 2 * row + half
+            costs = [
+                [hops(chip_of(row, 8 * half + k), chip_of(target, column)) for target in range(8)]
+                for k in range(8)
+            ]
+            most = 0
+            while assigned(costs, most) is None:
+                most += 1
+            found = assigned(costs, most)
+            pairs += [(16 * row + 8 * half + k, 16 * found[k] + column) for k in range(8)]
+    return pairs
+
+
 def on_device(
     pair_act, atom_act, atom_token, atom_gain, w_attn, w_out, w_bias, w_trans_in, w_trans_out,
     w_agg, w_single,
@@ -383,25 +437,28 @@
     devices = n_row * n_col
     row_index, col_index = lax.axis_index("row"), lax.axis_index("col")
     flat = row_index * n_col + col_index
-    place = jnp.stack([row_index, col_index, flat, jnp.int32(devices * atom_n)]).astype(jnp.int32)
     both = ("row", "col")
     up = [(i, i + 1) for i in range(devices - 1)]
-    firsts = [n_col * i for i in range(1, n_row)]
-    ends = [(i - 1, i) for i in firsts] + [(i, i - 1) for i in firsts]
-    turn = [
-        (16 * a + 8 * h + k, 16 * k + 2 * a + h)
-        for a in range(n_row)
-        for h in range(2)
-        for k in range(8)
-    ]
-
-    band, cross, tok_rows = band_biases(place, pair_act, w_bias, atom_act, atom_token)
-    cross = lax.ppermute(cross, both, ends)
+    turn = column_turn()
+    senders = np.zeros(devices, np.int32)
+    for source, target in turn:
+        senders[target] = source % 8
+    place = jnp.stack(
+        [row_index, col_index, flat, jnp.int32(devices * atom_n), jnp.asarray(senders)[flat]]
+    ).astype(jnp.int32)
+    ends = [(n_col * (i + 1) - 1, n_col * (i + 2) - 1) for i in range(n_row - 1)]
+    ends += [(n_col * (i + 1), n_col * i) for i in range(n_row - 1)]
+
+    far_atoms = lax.ppermute(atom_act, both, ends)
+    far_tokens = lax.ppermute(atom_token, both, ends)
+    band, tok_rows = band_biases(
+        place, pair_act, w_bias, atom_act, atom_token, far_atoms, far_tokens
+    )
     near = lax.all_to_all(band, "col", 0, 0, tiled=True)
     done = early_part(pair_act, w_trans_in, w_trans_out, band)
-    near, cross = lax.optimization_barrier((near, cross, done))[:2]
+    near = lax.optimization_barrier((near, done))[0]
     atom_main, next_out, shared, token_single, singles = atom_part(
-        place, cross, atom_act, tok_rows, near, atom_gain[None, :], w_attn, w_out, w_agg, w_single
+        place, atom_act, tok_rows, near, atom_gain[None, :], w_attn, w_out, w_agg, w_single
     )
     held = singles
     for k in range(3):

time: 85.5 us -> 87.9 us (1.028)
  the two profiles are of different devices: /device:TPU:1 before, /device:TPU:6 now
where the time goes in v4:
time: 87.9 us; the launch traced here: 87.1 us
  Pallas kernels  45.3 us (52%)
  starting transfers between devices  24.9 us (28%)
  waiting for transfers between devices  11.3 us (13%)
  local copies, waits for them, and re-layouts  4.19 us (5%)
    pallas_call x1, Pallas kernels, last_part(): pl.pallas_call(last_kernel, grid=(rows // ROWS,), in_specs=[pl.BlockSpec(...  25.1 us
    all_to_all x1, starting transfers between devices, on_device(): near = lax.all_to_all(band, 'col', 0, 0, tiled=True)  13 us
    pallas_call x1, Pallas kernels, early_part(): pl.pallas_call(early_kernel, grid=(rows // ROWS,), in_specs=[block, whole...  10.5 us
    ppermute x3, waiting for transfers between devices, on_device(): held = jnp.concatenate([held, lax.ppermute(held, 'col', pairs)])  7.92 us
    pallas_call x1, Pallas kernels, band_biases(): pl.pallas_call(band_kernel, in_specs=[pl.BlockSpec(memory_space=pltpu.SME...  5.86 us
    ppermute x1, starting transfers between devices, on_device(): col_all = lax.ppermute(held, both, turn)  4.87 us
    pallas_call x1, Pallas kernels, atom_part(): pl.pallas_call(atom_kernel, in_specs=[pl.BlockSpec(memory_space=pltpu.SME...  3.82 us
    ppermute x1, starting transfers between devices, on_device(): from_below = lax.ppermute(next_out, both, up)  3.07 us
  transfers between devices with their start and end apart: 9, of which 5 were waited for; matrix products, arithmetic and copies ran while one was open for 3% of the time, Pallas kernels for 41%

profile of v4, /device:TPU:6, one launch (start us, length us, event | category | flops | bytes accessed | tf_op | source)
XLA Modules:
  0.0 87.1 jit_solution(16056973312533251344)
XLA Ops:
  0.6 0.0 copy-start.2
  0.6 0.0 copy-start.1
  0.7 0.8 collective-permute-start
  1.5 0.7 collective-permute-start.1
  2.1 1.3 %dynamic_slice.3 = s32[1]{0:T(128)} dynamic-slice(s32[128]{0:T(128)} %constant.21.clone, s32[]{:T(128)S(6)} %select_n.7), dynamic_slice_sizes={1} | dynamic-slice | bytes 12 | tf_op jit(solution)/shard_map/dynamic_slice | solution.py:447
  3.4 1.2 %stack.15.place_ref = s32[5]{0:T(128)} concatenate(s32[1]{0:T(128)} %bitcast, s32[1]{0:T(128)} %bitcast.1, s32[1]{0:T(128)} %bitcast.2, s32[1]{0:T(128)} %constant.8.clone.1, s32[1]{0:T(128)} %dynamic_slice.3), dimensions={0} | concatenate | bytes 40 | tf_op jit(solution)/shard_map/stack | solution.py:446
  4.6 0.0 collective-permute-done.1
  4.6 0.0 copy-start.12
  4.6 0.0 collective-permute-done.far_atom_ref
  4.6 0.0 copy-start.11
  4.6 0.5 copy-done.12
  5.1 0.1 copy-done.11
  5.2 5.9 %band.1 = (bf16[16,128,128]{2,1,0:T(8,128)(2,1)}, bf16[16,128]{1,0:T(8,128)(2,1)}) custom-call(s32[5]{0:T(128)} %stack.15.place_ref, bf16[256,128,128]{2,1,0:T(8,128)(2,1)} %pair_ref.5, bf16[4,128]{1,0:T(4,128)(2,1)} %bitcast.8, bf16[128,128]{1,0:T(8,128)(2,1)} %own_ref.1, s32[1,128]{1,0:T(1,128)} %bitcast.9, bf16[128,128]{1,0:T(8,128)(2,1)} %copy-done.11, ...), custom_call_target="tpu_custom_call" | custom-call | flops 1000000000 | bytes 3000000 | tf_op jit(solution)/shard_map/band/pallas_call | solution.py:129
  11.1 13.0 %all-to-all-start = ((bf16[16,128,128]{2,1,0:T(8,128)(2,1)}), bf16[16,128,128]{2,1,0:T(8,128)(2,1)S(1)}, u32[]{:S(2)}, u32[]{:S(2)}) async-start(bf16[16,128,128]{2,1,0:T(8,128)(2,1)} %get-tuple-element.13.band_ref), calls=%async_computation | async-start | bytes 1048576 | tf_op jit(solution)/shard_map/all_to_all | solution.py:457
  24.1 0.0 copy-done.2
  24.1 0.0 copy-done.1
  24.1 0.0 copy-start
  24.1 1.0 %copy-done = bf16[16,128,128]{2,1,0:T(8,128)(2,1)S(1)} copy-done((bf16[16,128,128]{2,1,0:T(8,128)(2,1)S(1)}, bf16[16,128,128]{2,1,0:T(8,128)(2,1)}, u32[]{:S(2)}) %copy-start) | copy-done | bytes 524312
  25.2 0.0 copy-start.3
  25.2 0.0 copy-start.4
  25.2 0.0 copy-start.5
  25.2 0.0 copy-start.6
  25.2 0.0 copy-start.7
  25.2 0.0 copy-start.8
  25.2 0.0 copy-start.9
  25.2 0.0 copy-start.10
  25.2 10.5 %pair_early.1.done_ref = bf16[256,128,128]{2,1,0:T(8,128)(2,1)} custom-call(bf16[256,128,128]{2,1,0:T(8,128)(2,1)} %pair_ref.5, bf16[128,1024]{1,0:T(8,128)(2,1)S(1)} %copy-done.1, bf16[512,128]{1,0:T(8,128)(2,1)S(1)} %copy-done.2, bf16[16,128,128]{2,1,0:T(8,128)(2,1)S(1)} %copy-done), custom_call_target="tpu_custom_call" | custom-call | flops 3221225472 | bytes 4194304 | tf_op jit(solution)/shard_map/pair_early/pallas_call | solution.py:312
  35.8 0.0 all-to-all-done.near_ref
  35.8 0.0 copy-done.3
  35.8 0.0 copy-done.4
  35.8 0.0 copy-done.5
  35.8 0.0 copy-done.6
  35.8 0.0 copy-done.7
  35.8 0.0 copy-done.8
  35.8 0.0 copy-done.9
  35.8 0.0 copy-done.10
  35.8 3.8 %atoms.1 = (bf16[128,128]{1,0:T(8,128)(2,1)S(1)}, bf16[128,128]{1,0:T(8,128)(2,1)S(1)}, bf16[128,128]{1,0:T(8,128)(2,1)S(1)}, bf16[16,384]{1,0:T(8,128)(2,1)}, bf16[16,256]{1,0:T(8,128)(2,1)S(1)}) custom-call(s32[5]{0:T(128)S(1)} %copy-done.4, bf16[128,128]{1,0:T(8,128)(2,1)S(1)} %copy-done.3, bf16[16,128]{1,0:T(8,128)(2,1)S(1)} %copy-done.9, ...), custom_call_target="tpu_custom_call" | custom-call | flops 1000000000 | bytes 1000000 | tf_op jit(solution)/shard_map/atoms/pallas_call | solution.py:252
  39.6 0.1 collective-permute-start.3
  39.8 1.0 %collective-permute-done.3 = bf16[16,256]{1,0:T(8,128)(2,1)S(1)} collective-permute-done((bf16[16,256]{1,0:T(8,128)(2,1)S(1)}, bf16[16,256]{1,0:T(8,128)(2,1)S(1)}, u32[]{:S(2)}, u32[]{:S(2)}) %collective-permute-start.3) | collective-permute-done | bytes 8224 | tf_op jit(solution)/shard_map/ppermute | solution.py:466
  40.8 0.8 collective-permute-start.4
  41.6 4.5 %collective-permute-done.4 = bf16[32,256]{1,0:T(8,128)(2,1)S(1)} collective-permute-done((bf16[32,256]{1,0:T(8,128)(2,1)S(1)}, bf16[32,256]{1,0:T(8,128)(2,1)S(1)}, u32[]{:S(2)}, u32[]{:S(2)}) %collective-permute-start.4) | collective-permute-done | bytes 16416 | tf_op jit(solution)/shard_map/ppermute | solution.py:466
  46.1 1.5 %collective-permute-start.5 = (bf16[64,256]{1,0:T(8,128)(2,1)S(1)}, bf16[64,256]{1,0:T(8,128)(2,1)S(1)}, u32[]{:S(2)}, u32[]{:S(2)}) collective-permute-start(bf16[64,256]{1,0:T(8,128)(2,1)S(1)} %pad_maximum_fusion), channel_id=1, source_target_pairs={{0,4},{1,5},{2,6},{3,7},{4,0},{5,1},{6,2},{7,3},{8,12},{9,13},{10,... | collective-permute-start | bytes 98312 | tf_op jit(solution)/shard_map/ppermute | solution.py:466
  47.5 2.4 %collective-permute-done.5 = bf16[64,256]{1,0:T(8,128)(2,1)S(1)} collective-permute-done((bf16[64,256]{1,0:T(8,128)(2,1)S(1)}, bf16[64,256]{1,0:T(8,128)(2,1)S(1)}, u32[]{:S(2)}, u32[]{:S(2)}) %collective-permute-start.5) | collective-permute-done | bytes 32800 | tf_op jit(solution)/shard_map/ppermute | solution.py:466
  50.0 4.9 %collective-permute-start.7 = (bf16[128,256]{1,0:T(8,128)(2,1)S(1)}, bf16[128,256]{1,0:T(8,128)(2,1)S(1)}, u32[]{:S(2)}, u32[]{:S(2)}) collective-permute-start(bf16[128,256]{1,0:T(8,128)(2,1)S(1)} %constant_dynamic-update-slice_fusion.own_ref), channel_id=1, source_target_pairs={{0,16},{1,80},{2,112},{3,96},{4,32},{5,48},{6,0},{7,64},{8,17},{9,... | collective-permute-start | bytes 196616 | tf_op jit(solution)/shard_map/ppermute | solution.py:467
  54.9 0.1 collective-permute-start.6
  55.0 3.1 %collective-permute-start.2 = (bf16[128,128]{1,0:T(8,128)(2,1)S(1)}, bf16[128,128]{1,0:T(8,128)(2,1)S(1)}, u32[]{:S(2)}, u32[]{:S(2)}) collective-permute-start(bf16[128,128]{1,0:T(8,128)(2,1)S(1)} %get-tuple-element.16), channel_id=1, source_target_pairs={{0,1},{1,2},{2,3},{3,4},{4,5},{5,6},{6,7},{7,8},{8,9},{9,10},{10,1... | collective-permute-start | bytes 98312 | tf_op jit(solution)/shard_map/ppermute | solution.py:469
  58.0 1.7 %collective-permute-done.7.col_ref = bf16[128,256]{1,0:T(8,128)(2,1)S(1)} collective-permute-done((bf16[128,256]{1,0:T(8,128)(2,1)S(1)}, bf16[128,256]{1,0:T(8,128)(2,1)S(1)}, u32[]{:S(2)}, u32[]{:S(2)}) %collective-permute-start.7) | collective-permute-done | bytes 65568 | tf_op jit(solution)/shard_map/ppermute | solution.py:467
  59.7 1.7 %collective-permute-done.6.other_ref = bf16[128,256]{1,0:T(8,128)(2,1)S(1)} collective-permute-done((bf16[128,256]{1,0:T(8,128)(2,1)S(1)}, bf16[128,256]{1,0:T(8,128)(2,1)S(1)}, u32[]{:S(2)}, u32[]{:S(2)}) %collective-permute-start.6) | collective-permute-done | bytes 65568 | tf_op jit(solution)/shard_map/ppermute | solution.py:468
  61.4 25.1 %pair_last.1 = bf16[256,128,128]{2,1,0:T(8,128)(2,1)} custom-call(s32[5]{0:T(128)S(1)} %copy-done.4, bf16[256,128,128]{2,1,0:T(8,128)(2,1)} %pair_ref.5, bf16[256,128,128]{2,1,0:T(8,128)(2,1)} %pair_early.1.done_ref, bf16[128,1024]{1,0:T(8,128)(2,1)S(1)} %copy-done.1, bf16[512,128]{1,0:T(8,128)(2,1)S(1)} %copy-done.2, ...), custom_call_target="tpu_custom_call" | custom-call | flops 12884901888 | bytes 16777216 | tf_op jit(solution)/shard_map/pair_last/pallas_call | solution.py:366
  86.5 0.0 collective-permute-done.2
  86.5 0.6 compare_select_fusion
  (6 shorter events, 0.0 us)
Async XLA Ops:
  0.6 23.5 %copy-start.2 = (bf16[512,128]{1,0:T(8,128)(2,1)S(1)}, bf16[512,128]{1,0:T(8,128)(2,1)}, u32[]{:S(2)}) copy-start(bf16[512,128]{1,0:T(8,128)(2,1)} %w_out_ref.3) | copy-start | bytes 393220
  0.6 23.4 %copy-start.1 = (bf16[128,1024]{1,0:T(8,128)(2,1)S(1)}, bf16[128,1024]{1,0:T(8,128)(2,1)}, u32[]{:S(2)}) copy-start(bf16[128,1024]{1,0:T(8,128)(2,1)} %w_in_ref.3) | copy-start | bytes 786436
  0.7 4.0 %collective-permute-start = (bf16[128,128]{1,0:T(8,128)(2,1)}, bf16[128,128]{1,0:T(8,128)(2,1)S(1)}, u32[]{:S(2)}, u32[]{:S(2)}) collective-permute-start(bf16[128,128]{1,0:T(8,128)(2,1)} %own_ref.1), channel_id=1, source_target_pairs={{15,31},{31,47},{47,63},{63,79},{79,95},{95,111},{111,127},{16,0},... | collective-permute-start | bytes 98312 | tf_op jit(solution)/shard_map/ppermute | solution.py:452
  1.5 3.1 %collective-permute-start.1 = (s32[128]{0:T(128)}, s32[128]{0:T(128)S(1)}, u32[]{:S(2)}, u32[]{:S(2)}) collective-permute-start(s32[128]{0:T(128)} %param.14), channel_id=1, source_target_pairs={{15,31},{31,47},{47,63},{63,79},{79,95},{95,111},{111,127},{16,0},... | collective-permute-start | bytes 1544 | tf_op jit(solution)/shard_map/ppermute | solution.py:453
  4.6 0.5 copy-start.12
  4.6 0.6 copy-start.11
  11.1 24.7 %all-to-all-start = ((bf16[16,128,128]{2,1,0:T(8,128)(2,1)}), bf16[16,128,128]{2,1,0:T(8,128)(2,1)S(1)}, u32[]{:S(2)}, u32[]{:S(2)}) async-start(bf16[16,128,128]{2,1,0:T(8,128)(2,1)} %get-tuple-element.13.band_ref), calls=%async_computation | async-start | bytes 1048576 | tf_op jit(solution)/shard_map/all_to_all | solution.py:457
  24.1 1.1 %copy-start = (bf16[16,128,128]{2,1,0:T(8,128)(2,1)S(1)}, bf16[16,128,128]{2,1,0:T(8,128)(2,1)}, u32[]{:S(2)}) copy-start(bf16[16,128,128]{2,1,0:T(8,128)(2,1)} %get-tuple-element.13.band_ref) | copy-start | bytes 1572868
  25.2 10.6 %copy-start.3 = (bf16[128,128]{1,0:T(8,128)(2,1)S(1)}, bf16[128,128]{1,0:T(8,128)(2,1)}, u32[]{:S(2)}) copy-start(bf16[128,128]{1,0:T(8,128)(2,1)} %own_ref.1) | copy-start | bytes 98308
  25.2 10.6 %copy-start.4 = (s32[5]{0:T(128)S(1)}, s32[5]{0:T(128)}, u32[]{:S(2)}) copy-start(s32[5]{0:T(128)} %stack.15.place_ref) | copy-start | bytes 64
  25.2 10.6 %copy-start.5 = (bf16[384,256]{1,0:T(8,128)(2,1)S(1)}, bf16[384,256]{1,0:T(8,128)(2,1)}, u32[]{:S(2)}) copy-start(bf16[384,256]{1,0:T(8,128)(2,1)} %wsingle_ref.1) | copy-start | bytes 589828
  25.2 10.6 %copy-start.6 = (bf16[128,512]{1,0:T(8,128)(2,1)S(1)}, bf16[128,512]{1,0:T(8,128)(2,1)}, u32[]{:S(2)}) copy-start(bf16[128,512]{1,0:T(8,128)(2,1)} %wattn_ref.1) | copy-start | bytes 393220
  25.2 10.6 %copy-start.7 = (bf16[128,384]{1,0:T(8,128)(2,1)S(1)}, bf16[128,384]{1,0:T(8,128)(2,1)}, u32[]{:S(2)}) copy-start(bf16[128,384]{1,0:T(8,128)(2,1)} %wagg_ref.1) | copy-start | bytes 294916
  25.2 10.6 %copy-start.8 = (bf16[128,128]{1,0:T(8,128)(2,1)S(1)}, bf16[128,128]{1,0:T(8,128)(2,1)}, u32[]{:S(2)}) copy-start(bf16[128,128]{1,0:T(8,128)(2,1)} %wout_ref.1) | copy-start | bytes 98308
  25.2 10.6 %copy-start.9 = (bf16[16,128]{1,0:T(8,128)(2,1)S(1)}, bf16[16,128]{1,0:T(8,128)(2,1)}, u32[]{:S(2)}) copy-start(bf16[16,128]{1,0:T(8,128)(2,1)} %get-tuple-element.12.tok_ref) | copy-start | bytes 12292
  25.2 10.6 %copy-start.10 = (f32[128]{0:T(128)S(1)}, f32[128]{0:T(128)}, u32[]{:S(2)}) copy-start(f32[128]{0:T(128)} %param.15) | copy-start | bytes 1540
  39.6 1.2 %collective-permute-start.3 = (bf16[16,256]{1,0:T(8,128)(2,1)S(1)}, bf16[16,256]{1,0:T(8,128)(2,1)S(1)}, u32[]{:S(2)}, u32[]{:S(2)}) collective-permute-start(bf16[16,256]{1,0:T(8,128)(2,1)S(1)} %get-tuple-element.17), channel_id=1, source_target_pairs={{0,1},{1,0},{2,3},{3,2},{4,5},{5,4},{6,7},{7,6},{8,9},{9,8},{10,11... | collective-permute-start | bytes 24584 | tf_op jit(solution)/shard_map/ppermute | solution.py:466
  40.8 5.2 %collective-permute-start.4 = (bf16[32,256]{1,0:T(8,128)(2,1)S(1)}, bf16[32,256]{1,0:T(8,128)(2,1)S(1)}, u32[]{:S(2)}, u32[]{:S(2)}) collective-permute-start(bf16[32,256]{1,0:T(8,128)(2,1)S(1)} %pad_maximum_fusion.1), channel_id=1, source_target_pairs={{0,2},{1,3},{2,0},{3,1},{4,6},{5,7},{6,4},{7,5},{8,10},{9,11},{10,... | collective-permute-start | bytes 49160 | tf_op jit(solution)/shard_map/ppermute | solution.py:466
  46.1 3.9 %collective-permute-start.5 = (bf16[64,256]{1,0:T(8,128)(2,1)S(1)}, bf16[64,256]{1,0:T(8,128)(2,1)S(1)}, u32[]{:S(2)}, u32[]{:S(2)}) collective-permute-start(bf16[64,256]{1,0:T(8,128)(2,1)S(1)} %pad_maximum_fusion), channel_id=1, source_target_pairs={{0,4},{1,5},{2,6},{3,7},{4,0},{5,1},{6,2},{7,3},{8,12},{9,13},{10,... | collective-permute-start | bytes 98312 | tf_op jit(solution)/shard_map/ppermute | solution.py:466
  50.0 9.7 %collective-permute-start.7 = (bf16[128,256]{1,0:T(8,128)(2,1)S(1)}, bf16[128,256]{1,0:T(8,128)(2,1)S(1)}, u32[]{:S(2)}, u32[]{:S(2)}) collective-permute-start(bf16[128,256]{1,0:T(8,128)(2,1)S(1)} %constant_dynamic-update-slice_fusion.own_ref), channel_id=1, source_target_pairs={{0,16},{1,80},{2,112},{3,96},{4,32},{5,48},{6,0},{7,64},{8,17},{9,... | collective-permute-start | bytes 196616 | tf_op jit(solution)/shard_map/ppermute | solution.py:467
  54.9 6.5 %collective-permute-start.6 = (bf16[128,256]{1,0:T(8,128)(2,1)S(1)}, bf16[128,256]{1,0:T(8,128)(2,1)S(1)}, u32[]{:S(2)}, u32[]{:S(2)}) collective-permute-start(bf16[128,256]{1,0:T(8,128)(2,1)S(1)} %constant_dynamic-update-slice_fusion.own_ref), channel_id=1, source_target_pairs={{0,8},{1,9},{2,10},{3,11},{4,12},{5,13},{6,14},{7,15},{8,0},{9,1},... | collective-permute-start | bytes 196616 | tf_op jit(solution)/shard_map/ppermute | solution.py:468
  55.0 31.5 %collective-permute-start.2 = (bf16[128,128]{1,0:T(8,128)(2,1)S(1)}, bf16[128,128]{1,0:T(8,128)(2,1)S(1)}, u32[]{:S(2)}, u32[]{:S(2)}) collective-permute-start(bf16[128,128]{1,0:T(8,128)(2,1)S(1)} %get-tuple-element.16), channel_id=1, source_target_pairs={{0,1},{1,2},{2,3},{3,4},{4,5},{5,6},{6,7},{7,8},{8,9},{9,10},{10,1... | collective-permute-start | bytes 98312 | tf_op jit(solution)/shard_map/ppermute | solution.py:469

commit v5 on v4

--- a/solution.py
+++ b/solution.py
@@ -325,7 +325,7 @@
 
 
 def last_kernel(
-    place_ref, pair_ref, done_ref, w_in_ref, w_out_ref, own_ref, other_ref, col_ref,
+    place_ref, sender_ref, pair_ref, done_ref, w_in_ref, w_out_ref, own_ref, other_ref, col_ref,
     out_ref, w_in_scr, row_scr, col_scr,
 ):
     i = pl.program_id(0)
@@ -334,7 +334,7 @@
     @pl.when(i == 0)
     def _():
         halved_gate(w_in_ref, w_in_scr)
-        col, sender = place_ref[1], place_ref[4]
+        col, sender = place_ref[1], sender_ref[place_ref[2]]
         half = col // 8
         for block in range(8):
             at = slice(block * TOK_DEV, (block + 1) * TOK_DEV)
@@ -359,14 +359,15 @@
         out_ref[r] = (done_ref[r].astype(jnp.float32) + extra).astype(jnp.bfloat16)
 
 
-def last_part(place, pair_act, done, w_in, w_out, own, other, col):
+def last_part(place, senders, pair_act, done, w_in, w_out, own, other, col):
     rows, cols, width = pair_act.shape
     block = pl.BlockSpec((ROWS, cols, width), lambda i: (i, 0, 0))
     done_block = pl.BlockSpec((EARLY, cols, width), lambda i: (ROWS // EARLY * i, 0, 0))
     return pl.pallas_call(
         last_kernel,
         grid=(rows // ROWS,),
-        in_specs=[pl.BlockSpec(memory_space=pltpu.SMEM), block, done_block]
+        in_specs=[pl.BlockSpec(memory_space=pltpu.SMEM)] * 2
+        + [block, done_block]
         + [whole(x) for x in (w_in, w_out, own, other, col)],
         out_specs=block,
         out_shape=jax.ShapeDtypeStruct(pair_act.shape, jnp.bfloat16),
@@ -380,7 +381,7 @@
         ),
         compiler_params=pltpu.CompilerParams(vmem_limit_bytes=WIDE * MIB),
         name="pair_last",
-    )(place, pair_act, done, w_in, w_out, own, other, col)
+    )(place, senders, pair_act, done, w_in, w_out, own, other, col)
 
 
 def chip_of(row, col):
@@ -443,9 +444,7 @@
     senders = np.zeros(devices, np.int32)
     for source, target in turn:
         senders[target] = source % 8
-    place = jnp.stack(
-        [row_index, col_index, flat, jnp.int32(devices * atom_n), jnp.asarray(senders)[flat]]
-    ).astype(jnp.int32)
+    place = jnp.stack([row_index, col_index, flat, jnp.int32(devices * atom_n)]).astype(jnp.int32)
     ends = [(n_col * (i + 1) - 1, n_col * (i + 2) - 1) for i in range(n_row - 1)]
     ends += [(n_col * (i + 1), n_col * i) for i in range(n_row - 1)]
 
@@ -460,15 +459,16 @@
     atom_main, next_out, shared, token_single, singles = atom_part(
         place, atom_act, tok_rows, near, atom_gain[None, :], w_attn, w_out, w_agg, w_single
     )
-    held = singles
-    for k in range(3):
-        pairs = [(i, i ^ (1 << k)) for i in range(n_col)]
-        held = jnp.concatenate([held, lax.ppermute(held, "col", pairs)])
+    def swapped(value, bits):
+        return lax.ppermute(value, "col", [(i, i ^ bits) for i in range(n_col)])
+
+    held = jnp.concatenate([singles, swapped(singles, 1)])
+    held = jnp.concatenate([held] + [swapped(held, bits) for bits in (2, 4, 6)])
     col_all = lax.ppermute(held, both, turn)
     other = lax.ppermute(held, "col", [(i, i ^ 8) for i in range(n_col)])
     from_below = lax.ppermute(next_out, both, up)
     pair_out = last_part(
-        place, pair_act, done, w_trans_in, w_trans_out, held, other, col_all
+        place, jnp.asarray(senders), pair_act, done, w_trans_in, w_trans_out, held, other, col_all
     )
     from_below = lax.optimization_barrier((from_below, pair_out))[0]
     atom_out = jnp.where(shared < 0, from_below, atom_main)

time: 87.9 us -> 87.7 us (level)
  starting transfers between devices: 24.9 us -> 30.5 us
  waiting for transfers between devices: 11.3 us -> 7.6 us
  local copies, waits for them, and re-layouts: 4.19 us -> 1.73 us
    ppermute x3 -> x4, waiting for transfers between devices: 7.92 us -> 4.2 us  [swapped(): return lax.ppermute(value, 'col', [(i, i ^ bits) for i in range(n_col)])]
    ppermute x3 -> x4, starting transfers between devices: 2.4 us -> 5.14 us  [swapped(): return lax.ppermute(value, 'col', [(i, i ^ bits) for i in range(n_col)])]
    all_to_all x1, starting transfers between devices: 13 us -> 15.3 us  [on_device(): near = lax.all_to_all(band, 'col', 0, 0, tiled=True)]
    dynamic_slice x1 -> x0, local copies, waits for them, and re-layouts: 1.26 us -> none  [on_device(): jnp.asarray(senders)[flat]]
    another operation x1 -> x0, local copies, waits for them, and re-layouts: 1.21 us -> none  [on_device(): jnp.stack([row_index, col_index, flat, jnp.int32(devices * atom_n), jnp.a...]
    ppermute x1, starting transfers between devices: 4.87 us -> 5.8 us  [on_device(): col_all = lax.ppermute(held, both, turn)]
  transfers between devices with their start and end apart: 9 -> 10, of which waited for: 5 -> 5; matrix products, arithmetic and copies ran while one was open for 3% -> 1% of each run, Pallas kernels for 41% -> 41%
where the time goes in v5:
time: 87.7 us; the launch traced here: 87.3 us
  Pallas kernels  45.3 us (52%)
  starting transfers between devices  30.5 us (35%)
  waiting for transfers between devices  7.6 us (9%)
  local copies, waits for them, and re-layouts  1.73 us (2%)
  other arithmetic  1.24 us (1%)
    pallas_call x1, Pallas kernels, last_part(): pl.pallas_call(last_kernel, grid=(rows // ROWS,), in_specs=[pl.BlockSpec(...  25.1 us
    all_to_all x1, starting transfers between devices, on_device(): near = lax.all_to_all(band, 'col', 0, 0, tiled=True)  15.3 us
    pallas_call x1, Pallas kernels, early_part(): pl.pallas_call(early_kernel, grid=(rows // ROWS,), in_specs=[block, whole...  10.6 us
    pallas_call x1, Pallas kernels, band_biases(): pl.pallas_call(band_kernel, in_specs=[pl.BlockSpec(memory_space=pltpu.SME...  5.86 us
    ppermute x1, starting transfers between devices, on_device(): col_all = lax.ppermute(held, both, turn)  5.8 us
    ppermute x4, starting transfers between devices, swapped(): return lax.ppermute(value, 'col', [(i, i ^ bits) for i in range(n_col)])  5.14 us
    ppermute x4, waiting for transfers between devices, swapped(): return lax.ppermute(value, 'col', [(i, i ^ bits) for i in range(n_col)])  4.2 us
    pallas_call x1, Pallas kernels, atom_part(): pl.pallas_call(atom_kernel, in_specs=[pl.BlockSpec(memory_space=pltpu.SME...  3.82 us
  transfers between devices with their start and end apart: 10, of which 5 were waited for; matrix products, arithmetic and copies ran while one was open for 1% of the time, Pallas kernels for 41%

profile of v5, /device:TPU:6, one launch (start us, length us, event | category | flops | bytes accessed | tf_op | source)
XLA Modules:
  0.0 87.3 jit_solution(15257046627695455659)
XLA Ops:
  0.6 0.0 copy-start.2
  0.6 0.0 copy-start.1
  0.7 0.8 collective-permute-start.1
  1.5 0.7 collective-permute-start
  2.1 0.6 pad_add_fusion.place_ref
  2.7 0.0 collective-permute-done.1
  2.8 0.0 copy-start.13
  2.8 0.0 collective-permute-done.far_atom_ref
  2.8 0.0 copy-start.12
  2.8 0.6 copy-done.13
  3.3 0.0 copy-done.12
  3.4 5.9 %band.1 = (bf16[16,128,128]{2,1,0:T(8,128)(2,1)}, bf16[16,128]{1,0:T(8,128)(2,1)}) custom-call(s32[4]{0:T(128)} %pad_add_fusion.place_ref, bf16[256,128,128]{2,1,0:T(8,128)(2,1)} %pair_ref.5, bf16[4,128]{1,0:T(4,128)(2,1)} %bitcast.8, bf16[128,128]{1,0:T(8,128)(2,1)} %own_ref.1, s32[1,128]{1,0:T(1,128)} %bitcast.9, bf16[128,128]{1,0:T(8,128)(2,1)} %copy-done.12, ...), custom_call_target="tpu_custom_call" | custom-call | flops 1000000000 | bytes 3000000 | tf_op jit(solution)/shard_map/band/pallas_call | solution.py:129
  9.2 15.3 %all-to-all-start = ((bf16[16,128,128]{2,1,0:T(8,128)(2,1)}), bf16[16,128,128]{2,1,0:T(8,128)(2,1)S(1)}, u32[]{:S(2)}, u32[]{:S(2)}) async-start(bf16[16,128,128]{2,1,0:T(8,128)(2,1)} %get-tuple-element.13.band_ref), calls=%async_computation | async-start | bytes 1048576 | tf_op jit(solution)/shard_map/all_to_all | solution.py:456
  24.5 0.0 copy-done.2
  24.5 0.0 copy-done.1
  24.5 0.0 copy-start
  24.6 1.0 %copy-done = bf16[16,128,128]{2,1,0:T(8,128)(2,1)S(1)} copy-done((bf16[16,128,128]{2,1,0:T(8,128)(2,1)S(1)}, bf16[16,128,128]{2,1,0:T(8,128)(2,1)}, u32[]{:S(2)}) %copy-start) | copy-done | bytes 524312
  25.6 0.0 copy-start.3
  25.6 0.0 copy-start.4
  25.6 0.0 copy-start.5
  25.6 0.0 copy-start.6
  25.6 0.0 copy-start.7
  25.6 0.0 copy-start.8
  25.6 0.0 copy-start.9
  25.6 0.0 copy-start.10
  25.7 0.0 copy-start.11
  25.7 10.6 %pair_early.1.done_ref = bf16[256,128,128]{2,1,0:T(8,128)(2,1)} custom-call(bf16[256,128,128]{2,1,0:T(8,128)(2,1)} %pair_ref.5, bf16[128,1024]{1,0:T(8,128)(2,1)S(1)} %copy-done.1, bf16[512,128]{1,0:T(8,128)(2,1)S(1)} %copy-done.2, bf16[16,128,128]{2,1,0:T(8,128)(2,1)S(1)} %copy-done), custom_call_target="tpu_custom_call" | custom-call | flops 3221225472 | bytes 4194304 | tf_op jit(solution)/shard_map/pair_early/pallas_call | solution.py:312
  36.2 0.0 all-to-all-done.near_ref
  36.2 0.0 copy-done.3
  36.2 0.0 copy-done.4
  36.2 0.0 copy-done.5
  36.3 0.0 copy-done.6
  36.3 0.0 copy-done.7
  36.3 0.0 copy-done.8
  36.3 0.0 copy-done.9
  36.3 0.0 copy-done.10
  36.3 3.8 %atoms.1 = (bf16[128,128]{1,0:T(8,128)(2,1)S(1)}, bf16[128,128]{1,0:T(8,128)(2,1)S(1)}, bf16[128,128]{1,0:T(8,128)(2,1)S(1)}, bf16[16,384]{1,0:T(8,128)(2,1)}, bf16[16,256]{1,0:T(8,128)(2,1)S(1)}) custom-call(s32[4]{0:T(128)S(1)} %copy-done.4, bf16[128,128]{1,0:T(8,128)(2,1)S(1)} %copy-done.3, bf16[16,128]{1,0:T(8,128)(2,1)S(1)} %copy-done.9, ...), custom_call_target="tpu_custom_call" | custom-call | flops 1000000000 | bytes 1000000 | tf_op jit(solution)/shard_map/atoms/pallas_call | solution.py:252
  40.1 0.2 collective-permute-start.3
  40.3 1.0 %collective-permute-done.3 = bf16[16,256]{1,0:T(8,128)(2,1)S(1)} collective-permute-done((bf16[16,256]{1,0:T(8,128)(2,1)S(1)}, bf16[16,256]{1,0:T(8,128)(2,1)S(1)}, u32[]{:S(2)}, u32[]{:S(2)}) %collective-permute-start.3) | collective-permute-done | bytes 8224 | tf_op jit(solution)/shard_map/ppermute | solution.py:463
  41.3 0.7 collective-permute-start.4
  42.1 3.7 %collective-permute-start.6 = (bf16[32,256]{1,0:T(8,128)(2,1)S(1)}, bf16[32,256]{1,0:T(8,128)(2,1)S(1)}, u32[]{:S(2)}, u32[]{:S(2)}) collective-permute-start(bf16[32,256]{1,0:T(8,128)(2,1)S(1)} %get-tuple-element.21), channel_id=1, source_target_pairs={{0,6},{1,7},{2,4},{3,5},{4,2},{5,3},{6,0},{7,1},{8,14},{9,15},{10,... | collective-permute-start | bytes 49160 | tf_op jit(solution)/shard_map/ppermute | solution.py:463
  45.7 0.6 collective-permute-start.5
  46.3 0.2 collective-permute-done.4
  46.6 2.9 %collective-permute-done.5 = bf16[32,256]{1,0:T(8,128)(2,1)S(1)} collective-permute-done((bf16[32,256]{1,0:T(8,128)(2,1)S(1)}, bf16[32,256]{1,0:T(8,128)(2,1)S(1)}, u32[]{:S(2)}, u32[]{:S(2)}) %collective-permute-start.5) | collective-permute-done | bytes 16416 | tf_op jit(solution)/shard_map/ppermute | solution.py:463
  49.5 0.0 collective-permute-done.6
  49.5 5.8 %collective-permute-start.8 = (bf16[128,256]{1,0:T(8,128)(2,1)S(1)}, bf16[128,256]{1,0:T(8,128)(2,1)S(1)}, u32[]{:S(2)}, u32[]{:S(2)}) collective-permute-start(bf16[128,256]{1,0:T(8,128)(2,1)S(1)} %constant_dynamic-update-slice_fusion.2.own_ref), channel_id=1, source_target_pairs={{0,16},{1,80},{2,112},{3,96},{4,32},{5,48},{6,0},{7,64},{8,17},{9,... | collective-permute-start | bytes 196616 | tf_op jit(solution)/shard_map/ppermute | solution.py:467
  55.3 0.1 collective-permute-start.7
  55.4 2.8 %collective-permute-start.2 = (bf16[128,128]{1,0:T(8,128)(2,1)S(1)}, bf16[128,128]{1,0:T(8,128)(2,1)S(1)}, u32[]{:S(2)}, u32[]{:S(2)}) collective-permute-start(bf16[128,128]{1,0:T(8,128)(2,1)S(1)} %get-tuple-element.16), channel_id=1, source_target_pairs={{0,1},{1,2},{2,3},{3,4},{4,5},{5,6},{6,7},{7,8},{8,9},{9,10},{10,1... | collective-permute-start | bytes 98312 | tf_op jit(solution)/shard_map/ppermute | solution.py:469
  58.2 1.1 %collective-permute-done.8.col_ref = bf16[128,256]{1,0:T(8,128)(2,1)S(1)} collective-permute-done((bf16[128,256]{1,0:T(8,128)(2,1)S(1)}, bf16[128,256]{1,0:T(8,128)(2,1)S(1)}, u32[]{:S(2)}, u32[]{:S(2)}) %collective-permute-start.8) | collective-permute-done | bytes 65568 | tf_op jit(solution)/shard_map/ppermute | solution.py:467
  59.3 2.3 %collective-permute-done.7.other_ref = bf16[128,256]{1,0:T(8,128)(2,1)S(1)} collective-permute-done((bf16[128,256]{1,0:T(8,128)(2,1)S(1)}, bf16[128,256]{1,0:T(8,128)(2,1)S(1)}, u32[]{:S(2)}, u32[]{:S(2)}) %collective-permute-start.7) | collective-permute-done | bytes 65568 | tf_op jit(solution)/shard_map/ppermute | solution.py:468
  61.6 0.0 copy-done.11
  61.6 25.1 %pair_last.1 = bf16[256,128,128]{2,1,0:T(8,128)(2,1)} custom-call(s32[4]{0:T(128)S(1)} %copy-done.4, s32[128]{0:T(128)S(1)} %copy-done.11, bf16[256,128,128]{2,1,0:T(8,128)(2,1)} %pair_ref.5, bf16[256,128,128]{2,1,0:T(8,128)(2,1)} %pair_early.1.done_ref, bf16[128,1024]{1,0:T(8,128)(2,1)S(1)} %copy-done.1, bf16[512,128]{1,0:T(8,128)(2,1)S(1)} %copy-done.2, ...), custom_call_target="tpu_custom_call" | custom-call | flops 12884901888 | bytes 16777216 | tf_op jit(solution)/shard_map/pair_last/pallas_call | solution.py:366
  86.6 0.0 collective-permute-done.2
  86.6 0.6 compare_select_fusion
  (5 shorter events, 0.0 us)
Async XLA Ops:
  0.6 23.9 %copy-start.2 = (bf16[512,128]{1,0:T(8,128)(2,1)S(1)}, bf16[512,128]{1,0:T(8,128)(2,1)}, u32[]{:S(2)}) copy-start(bf16[512,128]{1,0:T(8,128)(2,1)} %w_out_ref.3) | copy-start | bytes 393220
  0.6 23.9 %copy-start.1 = (bf16[128,1024]{1,0:T(8,128)(2,1)S(1)}, bf16[128,1024]{1,0:T(8,128)(2,1)}, u32[]{:S(2)}) copy-start(bf16[128,1024]{1,0:T(8,128)(2,1)} %w_in_ref.3) | copy-start | bytes 786436
  0.7 2.1 %collective-permute-start.1 = (s32[128]{0:T(128)}, s32[128]{0:T(128)S(1)}, u32[]{:S(2)}, u32[]{:S(2)}) collective-permute-start(s32[128]{0:T(128)} %param.14), channel_id=1, source_target_pairs={{15,31},{31,47},{47,63},{63,79},{79,95},{95,111},{111,127},{16,0},... | collective-permute-start | bytes 1544 | tf_op jit(solution)/shard_map/ppermute | solution.py:452
  1.5 1.3 %collective-permute-start = (bf16[128,128]{1,0:T(8,128)(2,1)}, bf16[128,128]{1,0:T(8,128)(2,1)S(1)}, u32[]{:S(2)}, u32[]{:S(2)}) collective-permute-start(bf16[128,128]{1,0:T(8,128)(2,1)} %own_ref.1), channel_id=1, source_target_pairs={{15,31},{31,47},{47,63},{63,79},{79,95},{95,111},{111,127},{16,0},... | collective-permute-start | bytes 98312 | tf_op jit(solution)/shard_map/ppermute | solution.py:451
  2.8 0.6 copy-start.13
  2.8 0.6 copy-start.12
  9.2 27.0 %all-to-all-start = ((bf16[16,128,128]{2,1,0:T(8,128)(2,1)}), bf16[16,128,128]{2,1,0:T(8,128)(2,1)S(1)}, u32[]{:S(2)}, u32[]{:S(2)}) async-start(bf16[16,128,128]{2,1,0:T(8,128)(2,1)} %get-tuple-element.13.band_ref), calls=%async_computation | async-start | bytes 1048576 | tf_op jit(solution)/shard_map/all_to_all | solution.py:456
  24.5 1.1 %copy-start = (bf16[16,128,128]{2,1,0:T(8,128)(2,1)S(1)}, bf16[16,128,128]{2,1,0:T(8,128)(2,1)}, u32[]{:S(2)}) copy-start(bf16[16,128,128]{2,1,0:T(8,128)(2,1)} %get-tuple-element.13.band_ref) | copy-start | bytes 1572868
  25.6 10.6 %copy-start.3 = (bf16[128,128]{1,0:T(8,128)(2,1)S(1)}, bf16[128,128]{1,0:T(8,128)(2,1)}, u32[]{:S(2)}) copy-start(bf16[128,128]{1,0:T(8,128)(2,1)} %own_ref.1) | copy-start | bytes 98308
  25.6 10.6 %copy-start.4 = (s32[4]{0:T(128)S(1)}, s32[4]{0:T(128)}, u32[]{:S(2)}) copy-start(s32[4]{0:T(128)} %pad_add_fusion.place_ref) | copy-start | bytes 52
  25.6 10.6 %copy-start.5 = (bf16[384,256]{1,0:T(8,128)(2,1)S(1)}, bf16[384,256]{1,0:T(8,128)(2,1)}, u32[]{:S(2)}) copy-start(bf16[384,256]{1,0:T(8,128)(2,1)} %wsingle_ref.1) | copy-start | bytes 589828
  25.6 10.7 %copy-start.6 = (bf16[128,512]{1,0:T(8,128)(2,1)S(1)}, bf16[128,512]{1,0:T(8,128)(2,1)}, u32[]{:S(2)}) copy-start(bf16[128,512]{1,0:T(8,128)(2,1)} %wattn_ref.1) | copy-start | bytes 393220
  25.6 10.7 %copy-start.7 = (bf16[128,384]{1,0:T(8,128)(2,1)S(1)}, bf16[128,384]{1,0:T(8,128)(2,1)}, u32[]{:S(2)}) copy-start(bf16[128,384]{1,0:T(8,128)(2,1)} %wagg_ref.1) | copy-start | bytes 294916
  25.6 10.7 %copy-start.8 = (bf16[128,128]{1,0:T(8,128)(2,1)S(1)}, bf16[128,128]{1,0:T(8,128)(2,1)}, u32[]{:S(2)}) copy-start(bf16[128,128]{1,0:T(8,128)(2,1)} %wout_ref.1) | copy-start | bytes 98308
  25.6 10.7 %copy-start.9 = (bf16[16,128]{1,0:T(8,128)(2,1)S(1)}, bf16[16,128]{1,0:T(8,128)(2,1)}, u32[]{:S(2)}) copy-start(bf16[16,128]{1,0:T(8,128)(2,1)} %get-tuple-element.12.tok_ref) | copy-start | bytes 12292
  25.6 10.7 %copy-start.10 = (f32[128]{0:T(128)S(1)}, f32[128]{0:T(128)}, u32[]{:S(2)}) copy-start(f32[128]{0:T(128)} %param.15) | copy-start | bytes 1540
  25.7 35.9 %copy-start.11 = (s32[128]{0:T(128)S(1)}, s32[128]{0:T(128)}, u32[]{:S(2)}) copy-start(s32[128]{0:T(128)} %constant.17.clone.sender_ref) | copy-start | bytes 1540
  40.1 1.2 %collective-permute-start.3 = (bf16[16,256]{1,0:T(8,128)(2,1)S(1)}, bf16[16,256]{1,0:T(8,128)(2,1)S(1)}, u32[]{:S(2)}, u32[]{:S(2)}) collective-permute-start(bf16[16,256]{1,0:T(8,128)(2,1)S(1)} %get-tuple-element.17), channel_id=1, source_target_pairs={{0,1},{1,0},{2,3},{3,2},{4,5},{5,4},{6,7},{7,6},{8,9},{9,8},{10,11... | collective-permute-start | bytes 24584 | tf_op jit(solution)/shard_map/ppermute | solution.py:463
  41.3 5.2 %collective-permute-start.4 = (bf16[32,256]{1,0:T(8,128)(2,1)S(1)}, bf16[32,256]{1,0:T(8,128)(2,1)S(1)}, u32[]{:S(2)}, u32[]{:S(2)}) collective-permute-start(bf16[32,256]{1,0:T(8,128)(2,1)S(1)} %get-tuple-element.21), channel_id=1, source_target_pairs={{0,2},{1,3},{2,0},{3,1},{4,6},{5,7},{6,4},{7,5},{8,10},{9,11},{10,... | collective-permute-start | bytes 49160 | tf_op jit(solution)/shard_map/ppermute | solution.py:463
  42.1 7.4 %collective-permute-start.6 = (bf16[32,256]{1,0:T(8,128)(2,1)S(1)}, bf16[32,256]{1,0:T(8,128)(2,1)S(1)}, u32[]{:S(2)}, u32[]{:S(2)}) collective-permute-start(bf16[32,256]{1,0:T(8,128)(2,1)S(1)} %get-tuple-element.21), channel_id=1, source_target_pairs={{0,6},{1,7},{2,4},{3,5},{4,2},{5,3},{6,0},{7,1},{8,14},{9,15},{10,... | collective-permute-start | bytes 49160 | tf_op jit(solution)/shard_map/ppermute | solution.py:463
  45.7 3.7 %collective-permute-start.5 = (bf16[32,256]{1,0:T(8,128)(2,1)S(1)}, bf16[32,256]{1,0:T(8,128)(2,1)S(1)}, u32[]{:S(2)}, u32[]{:S(2)}) collective-permute-start(bf16[32,256]{1,0:T(8,128)(2,1)S(1)} %get-tuple-element.21), channel_id=1, source_target_pairs={{0,4},{1,5},{2,6},{3,7},{4,0},{5,1},{6,2},{7,3},{8,12},{9,13},{10,... | collective-permute-start | bytes 49160 | tf_op jit(solution)/shard_map/ppermute | solution.py:463
  49.5 9.8 %collective-permute-start.8 = (bf16[128,256]{1,0:T(8,128)(2,1)S(1)}, bf16[128,256]{1,0:T(8,128)(2,1)S(1)}, u32[]{:S(2)}, u32[]{:S(2)}) collective-permute-start(bf16[128,256]{1,0:T(8,128)(2,1)S(1)} %constant_dynamic-update-slice_fusion.2.own_ref), channel_id=1, source_target_pairs={{0,16},{1,80},{2,112},{3,96},{4,32},{5,48},{6,0},{7,64},{8,17},{9,... | collective-permute-start | bytes 196616 | tf_op jit(solution)/shard_map/ppermute | solution.py:467
  55.3 6.3 %collective-permute-start.7 = (bf16[128,256]{1,0:T(8,128)(2,1)S(1)}, bf16[128,256]{1,0:T(8,128)(2,1)S(1)}, u32[]{:S(2)}, u32[]{:S(2)}) collective-permute-start(bf16[128,256]{1,0:T(8,128)(2,1)S(1)} %constant_dynamic-update-slice_fusion.2.own_ref), channel_id=1, source_target_pairs={{0,8},{1,9},{2,10},{3,11},{4,12},{5,13},{6,14},{7,15},{8,0},{9,1},... | collective-permute-start | bytes 196616 | tf_op jit(solution)/shard_map/ppermute | solution.py:468
  55.4 31.3 %collective-permute-start.2 = (bf16[128,128]{1,0:T(8,128)(2,1)S(1)}, bf16[128,128]{1,0:T(8,128)(2,1)S(1)}, u32[]{:S(2)}, u32[]{:S(2)}) collective-permute-start(bf16[128,128]{1,0:T(8,128)(2,1)S(1)} %get-tuple-element.16), channel_id=1, source_target_pairs={{0,1},{1,2},{2,3},{3,4},{4,5},{5,6},{6,7},{7,8},{8,9},{9,10},{10,1... | collective-permute-start | bytes 98312 | tf_op jit(solution)/shard_map/ppermute | solution.py:469

commit v6 on v3

--- a/solution.py
+++ b/solution.py
@@ -3,6 +3,7 @@
 
 import jax
 import jax.numpy as jnp
+import numpy as np
 from jax import lax
 from jax.experimental import pallas as pl
 from jax.experimental.pallas import tpu as pltpu
@@ -42,11 +43,21 @@
 
 
 def band_kernel(
-    place_ref, pair_ref, weight_ref, atom_ref, token_ref, out_ref, cross_ref, tok_ref, cells, sems
+    pair_ref, weight_hbm, atom_hbm, token_hbm, out_ref, cross_ref, tok_ref, cells, weight_ref,
+    atom_ref, token_ref, sems, small_sems,
 ):
-    row, col = place_ref[0], place_ref[1]
+    row, col = lax.axis_index("row"), lax.axis_index("col")
+    flat_index = row * lax.axis_size("col") + col
     shift = col - 2 * row
     first = jnp.clip(8 * shift - 1, 0, 7)
+    small = [
+        pltpu.make_async_copy(source, target, small_sems.at[i])
+        for i, (source, target) in enumerate(
+            [(atom_hbm, atom_ref), (token_hbm, token_ref), (weight_hbm, weight_ref)]
+        )
+    ]
+    for copy in small:
+        copy.start()
     copies = []
     for j in range(GROUPS):
         group = first + j
@@ -65,8 +76,10 @@
         copy.start()
         copies.append(copy)
     out_ref[:, 0:BAND_ROWS, :] = jnp.zeros((out_ref.shape[0], BAND_ROWS, 128), jnp.bfloat16)
+    for copy in small:
+        copy.wait()
     atoms = atom_ref.shape[0]
-    token_rel = (token_ref[...] - place_ref[2] * TOK_DEV).astype(jnp.float32)
+    token_rel = (token_ref[...] - flat_index * TOK_DEV).astype(jnp.float32)
     tok_rows = jnp.broadcast_to(token_rel, (16, 128)).astype(jnp.bfloat16)
     tok_ref[...] = tok_rows
     low = BAND_ROWS
@@ -113,17 +126,11 @@
             out_ref[pl.ds(first + j, 1), 0:BAND_ROWS, :] = kept.astype(jnp.bfloat16)[None]
 
 
-def band_biases(place, pair_act, w_bias, atom_act, atom_token):
+def band_biases(pair_act, w_bias, atom_act, atom_token):
     vmem = pl.BlockSpec(memory_space=pltpu.VMEM)
     return pl.pallas_call(
         band_kernel,
-        in_specs=[
-            pl.BlockSpec(memory_space=pltpu.SMEM),
-            pl.BlockSpec(memory_space=pl.ANY),
-            vmem,
-            vmem,
-            vmem,
-        ],
+        in_specs=[pl.BlockSpec(memory_space=pltpu.HBM)] * 4,
         out_specs=[vmem] * 3,
         out_shape=[
             jax.ShapeDtypeStruct((16, BLOCK_ROWS, 128), jnp.bfloat16),
@@ -132,25 +139,30 @@
         ],
         scratch_shapes=[
             pltpu.VMEM((GROUPS, 16, WINDOW + 2 * EDGE, 128), jnp.bfloat16),
+            pltpu.VMEM((4, 128), jnp.bfloat16),
+            pltpu.VMEM(atom_act.shape, jnp.bfloat16),
+            pltpu.VMEM((1, atom_act.shape[0]), jnp.int32),
             pltpu.SemaphoreType.DMA((GROUPS,)),
+            pltpu.SemaphoreType.DMA((3,)),
         ],
         cost_estimate=pl.CostEstimate(flops=10**9, bytes_accessed=3 * 10**6, transcendentals=0),
-        compiler_params=pltpu.CompilerParams(vmem_limit_bytes=56 * MIB),
+        compiler_params=pltpu.CompilerParams(vmem_limit_bytes=WIDE * MIB),
         name="band",
-    )(place, pair_act, w_bias.T, atom_act, atom_token[None, :])
+    )(pair_act, w_bias.T, atom_act, atom_token[None, :])
 
 
 def atom_kernel(
-    place_ref, cross_ref, own_ref, tok_ref, near_ref, gain_ref, wattn_ref, wout_ref,
+    cross_ref, own_ref, tok_ref, near_ref, gain_ref, wattn_ref, wout_ref,
     wagg_ref, wsingle_ref, atom_out_ref, next_out_ref, shared_ref, token_ref, singles_ref,
     wide, q_scr, k_scr, v_scr, gate_scr,
 ):
-    flat = place_ref[2]
+    n_col = lax.axis_size("col")
+    col = lax.axis_index("col")
+    flat = lax.axis_index("row") * n_col + col
     atoms = own_ref.shape[0]
     heads = 4
     n_query = atoms + QB
-    total = place_ref[3]
-    col = place_ref[1]
+    total = lax.axis_size("row") * n_col * atoms
     last = near_ref.shape[0] - 1
     low = BAND_ROWS
     from_below = near_ref[jnp.maximum(col - 1, 0), low : low + 16 + BELOW, :].astype(jnp.float32)
@@ -237,12 +249,12 @@
     singles_ref[...] = singles
 
 
-def atom_part(place, cross, own, tok_rows, near, atom_gain, w_attn, w_out, w_agg, w_single):
+def atom_part(cross, own, tok_rows, near, atom_gain, w_attn, w_out, w_agg, w_single):
     atoms = own.shape[0]
     vmem = pl.BlockSpec(memory_space=pltpu.VMEM)
     return pl.pallas_call(
         atom_kernel,
-        in_specs=[pl.BlockSpec(memory_space=pltpu.SMEM)] + [vmem] * 9,
+        in_specs=[vmem] * 9,
         out_specs=[vmem] * 5,
         out_shape=[
             jax.ShapeDtypeStruct((atoms, 128), jnp.bfloat16),
@@ -261,7 +273,7 @@
         cost_estimate=pl.CostEstimate(flops=10**9, bytes_accessed=10**6, transcendentals=10**5),
         compiler_params=pltpu.CompilerParams(vmem_limit_bytes=16 * MIB),
         name="atoms",
-    )(place, cross, own, tok_rows, near, atom_gain, w_attn, w_out, w_agg, w_single)
+    )(cross, own, tok_rows, near, atom_gain, w_attn, w_out, w_agg, w_single)
 
 
 def whole(array):
@@ -316,7 +328,7 @@
 
 
 def last_kernel(
-    place_ref, pair_ref, done_ref, w_in_ref, w_out_ref, own_ref, other_ref, col_ref,
+    sender_ref, pair_ref, done_ref, w_in_ref, w_out_ref, own_ref, other_ref, col_ref,
     out_ref, w_in_scr, row_scr, col_scr,
 ):
     i = pl.program_id(0)
@@ -325,12 +337,13 @@
     @pl.when(i == 0)
     def _():
         halved_gate(w_in_ref, w_in_scr)
-        row, col = place_ref[0], place_ref[1]
+        col = lax.axis_index("col")
+        sender = sender_ref[lax.axis_index("row") * lax.axis_size("col") + col]
         half = col // 8
         for block in range(8):
             at = slice(block * TOK_DEV, (block + 1) * TOK_DEV)
             row_at = pl.ds(pl.multiple_of((block ^ (col % 8)) * 16, 16), 16)
-            col_at = pl.ds(pl.multiple_of((block ^ row) * 16, 16), 16)
+            col_at = pl.ds(pl.multiple_of((block ^ sender) * 16, 16), 16)
             own_to = pl.ds(pl.multiple_of(half * 128 + block * 16, 16), 16)
             other_to = pl.ds(pl.multiple_of((1 - half) * 128 + block * 16, 16), 16)
             row_scr[own_to, :] = own_ref[row_at, 0:128].astype(jnp.float32)
@@ -350,7 +363,7 @@
         out_ref[r] = (done_ref[r].astype(jnp.float32) + extra).astype(jnp.bfloat16)
 
 
-def last_part(place, pair_act, done, w_in, w_out, own, other, col):
+def last_part(senders, pair_act, done, w_in, w_out, own, other, col):
     rows, cols, width = pair_act.shape
     block = pl.BlockSpec((ROWS, cols, width), lambda i: (i, 0, 0))
     done_block = pl.BlockSpec((EARLY, cols, width), lambda i: (ROWS // EARLY * i, 0, 0))
@@ -371,7 +384,52 @@
         ),
         compiler_params=pltpu.CompilerParams(vmem_limit_bytes=WIDE * MIB),
         name="pair_last",
-    )(place, pair_act, done, w_in, w_out, own, other, col)
+    )(senders, pair_act, done, w_in, w_out, own, other, col)
+
+
+def chip_of(row, col):
+    x_lo, z = divmod(row, 4)
+    y, rest = divmod(col, 4)
+    return (2 * (rest // 2) + x_lo, y, z)
+
+
+def hops(one, other):
+    return sum(min((a - b) % 4, (b - a) % 4) for a, b in zip(one, other))
+
+
+def assigned(costs, most):
+    owner = {}
+
+    def place(source, seen):
+        for target in sorted(range(len(costs)), key=lambda t: costs[source][t]):
+            if costs[source][target] <= most and target not in seen:
+                seen.add(target)
+                if target not in owner or place(owner[target], seen):
+                    owner[target] = source
+                    return True
+        return False
+
+    for source in range(len(costs)):
+        if not place(source, set()):
+            return None
+    return {source: target for target, source in owner.items()}
+
+
+def column_turn():
+    pairs = []
+    for row in range(8):
+        for half in range(2):
+            column = 2 * row + half
+            costs = [
+                [hops(chip_of(row, 8 * half + k), chip_of(target, column)) for target in range(8)]
+                for k in range(8)
+            ]
+            most = 0
+            while assigned(costs, most) is None:
+                most += 1
+            found = assigned(costs, most)
+            pairs += [(16 * row + 8 * half + k, 16 * found[k] + column) for k in range(8)]
+    return pairs
 
 
 def on_device(
@@ -381,37 +439,33 @@
     atom_n = atom_act.shape[0]
     n_row, n_col = lax.axis_size("row"), lax.axis_size("col")
     devices = n_row * n_col
-    row_index, col_index = lax.axis_index("row"), lax.axis_index("col")
-    flat = row_index * n_col + col_index
-    place = jnp.stack([row_index, col_index, flat, jnp.int32(devices * atom_n)]).astype(jnp.int32)
     both = ("row", "col")
     up = [(i, i + 1) for i in range(devices - 1)]
     firsts = [n_col * i for i in range(1, n_row)]
     ends = [(i - 1, i) for i in firsts] + [(i, i - 1) for i in firsts]
-    turn = [
-        (16 * a + 8 * h + k, 16 * k + 2 * a + h)
-        for a in range(n_row)
-        for h in range(2)
-        for k in range(8)
-    ]
-
-    band, cross, tok_rows = band_biases(place, pair_act, w_bias, atom_act, atom_token)
+    turn = column_turn()
+    senders = np.zeros(devices, np.int32)
+    for source, target in turn:
+        senders[target] = source % 8
+
+    band, cross, tok_rows = band_biases(pair_act, w_bias, atom_act, atom_token)
     cross = lax.ppermute(cross, both, ends)
     near = lax.all_to_all(band, "col", 0, 0, tiled=True)
     done = early_part(pair_act, w_trans_in, w_trans_out, band)
     near, cross = lax.optimization_barrier((near, cross, done))[:2]
     atom_main, next_out, shared, token_single, singles = atom_part(
-        place, cross, atom_act, tok_rows, near, atom_gain[None, :], w_attn, w_out, w_agg, w_single
-    )
-    held = singles
-    for k in range(3):
-        pairs = [(i, i ^ (1 << k)) for i in range(n_col)]
-        held = jnp.concatenate([held, lax.ppermute(held, "col", pairs)])
+        cross, atom_act, tok_rows, near, atom_gain[None, :], w_attn, w_out, w_agg, w_single
+    )
+    def swapped(value, bits):
+        return lax.ppermute(value, "col", [(i, i ^ bits) for i in range(n_col)])
+
+    held = jnp.concatenate([singles, swapped(singles, 1)])
+    held = jnp.concatenate([held] + [swapped(held, bits) for bits in (2, 4, 6)])
     col_all = lax.ppermute(held, both, turn)
     other = lax.ppermute(held, "col", [(i, i ^ 8) for i in range(n_col)])
     from_below = lax.ppermute(next_out, both, up)
     pair_out = last_part(
-        place, pair_act, done, w_trans_in, w_trans_out, held, other, col_all
+        jnp.asarray(senders), pair_act, done, w_trans_in, w_trans_out, held, other, col_all
     )
     from_below = lax.optimization_barrier((from_below, pair_out))[0]
     atom_out = jnp.where(shared < 0, from_below, atom_main)

time: 85.5 us -> 82.9 us (0.970)
  the two profiles are of different devices: /device:TPU:1 before, /device:TPU:6 now
where the time goes in v6:
time: 82.9 us; the launch traced here: 82.5 us
  Pallas kernels  43.9 us (53%)
  starting transfers between devices  23.5 us (28%)
  waiting for transfers between devices  11.6 us (14%)
  local copies, waits for them, and re-layouts  2.2 us (3%)
    pallas_call x1, Pallas kernels, last_part(): pl.pallas_call(last_kernel, grid=(rows // ROWS,), in_specs=[pl.BlockSpec(...  25.1 us
    ppermute x4, starting transfers between devices, swapped(): return lax.ppermute(value, 'col', [(i, i ^ bits) for i in range(n_col)])  11.1 us
    pallas_call x1, Pallas kernels, early_part(): pl.pallas_call(early_kernel, grid=(rows // ROWS,), in_specs=[block, whole...  10.4 us
    all_to_all x1, starting transfers between devices, on_device(): near = lax.all_to_all(band, 'col', 0, 0, tiled=True)  7.46 us
    ppermute x1, waiting for transfers between devices, on_device(): col_all = lax.ppermute(held, both, turn)  5.87 us
    ppermute x4, waiting for transfers between devices, swapped(): return lax.ppermute(value, 'col', [(i, i ^ bits) for i in range(n_col)])  5.69 us
    pallas_call x1, Pallas kernels, band_biases(): pl.pallas_call(band_kernel, in_specs=[pl.BlockSpec(memory_space=pltpu.HBM...  5.09 us
    pallas_call x1, Pallas kernels, atom_part(): pl.pallas_call(atom_kernel, in_specs=[vmem] * 9, out_specs=[vmem] * 5, ou...  3.28 us
  transfers between devices with their start and end apart: 9, of which 5 were waited for; matrix products, arithmetic and copies ran while one was open for 0% of the time, Pallas kernels for 43%

profile of v6, /device:TPU:6, one launch (start us, length us, event | category | flops | bytes accessed | tf_op | source)
XLA Modules:
  0.0 82.5 jit_solution(16249604586293200248)
XLA Ops:
  0.6 0.0 copy-start.1
  0.6 0.0 copy-start
  0.7 0.0 copy-start.2
  0.7 0.8 copy-done.2
  1.5 0.0 copy-start.4
  1.5 0.7 copy-done.4
  2.1 0.0 copy-start.5
  2.1 0.7 copy-done.5
  2.8 5.1 %band.1 = (bf16[16,128,128]{2,1,0:T(8,128)(2,1)}, bf16[96,128]{1,0:T(8,128)(2,1)S(1)}, bf16[16,128]{1,0:T(8,128)(2,1)S(1)}) custom-call(bf16[256,128,128]{2,1,0:T(8,128)(2,1)} %pair_ref.5, bf16[4,128]{1,0:T(4,128)(2,1)S(1)} %bitcast.3, bf16[128,128]{1,0:T(8,128)(2,1)S(1)} %copy-done.2, s32[1,128]{1,0:T(1,128)S(1)} %bitcast.4), custom_call_target="tpu_custom_call" | custom-call | flops 1000000000 | bytes 3000000 | tf_op jit(solution)/shard_map/band/pallas_call | solution.py:131
  7.9 7.5 %all-to-all-start = ((bf16[16,128,128]{2,1,0:T(8,128)(2,1)}), bf16[16,128,128]{2,1,0:T(8,128)(2,1)S(1)}, u32[]{:S(2)}, u32[]{:S(2)}) async-start(bf16[16,128,128]{2,1,0:T(8,128)(2,1)} %get-tuple-element.14.band_ref), calls=%async_computation | async-start | bytes 1048576 | tf_op jit(solution)/shard_map/all_to_all | solution.py:453
  15.4 0.0 copy-start.3
  15.4 0.0 copy-start.6
  15.4 0.0 copy-start.7
  15.4 0.0 copy-start.8
  15.4 0.0 copy-start.9
  15.4 0.0 copy-start.10
  15.4 0.0 copy-start.11
  15.4 0.8 collective-permute-start
  16.2 0.0 copy-done.1
  16.2 0.0 copy-done
  16.3 10.4 %pair_early.1.done_ref = bf16[256,128,128]{2,1,0:T(8,128)(2,1)} custom-call(bf16[256,128,128]{2,1,0:T(8,128)(2,1)} %pair_ref.5, bf16[128,1024]{1,0:T(8,128)(2,1)S(1)} %copy-done, bf16[512,128]{1,0:T(8,128)(2,1)S(1)} %copy-done.1, bf16[16,128,128]{2,1,0:T(8,128)(2,1)} %get-tuple-element.14.band_ref), custom_call_target="tpu_custom_call" | custom-call | flops 3221225472 | bytes 4194304 | tf_op jit(solution)/shard_map/pair_early/pallas_call | solution.py:315
  26.7 0.0 collective-permute-done.cross_ref
  26.7 0.0 all-to-all-done.near_ref
  26.7 0.0 copy-done.3
  26.7 0.0 copy-done.6
  26.7 0.0 copy-done.7
  26.7 0.0 copy-done.8
  26.7 0.0 copy-done.9
  26.7 0.0 copy-done.10
  26.8 3.3 %atoms.1 = (bf16[128,128]{1,0:T(8,128)(2,1)S(1)}, bf16[128,128]{1,0:T(8,128)(2,1)S(1)}, bf16[128,128]{1,0:T(8,128)(2,1)S(1)}, bf16[16,384]{1,0:T(8,128)(2,1)}, bf16[16,256]{1,0:T(8,128)(2,1)S(1)}) custom-call(bf16[96,128]{1,0:T(8,128)(2,1)S(1)} %collective-permute-done.cross_ref, bf16[128,128]{1,0:T(8,128)(2,1)S(1)} %copy-done.3, ...), custom_call_target="tpu_custom_call" | custom-call | flops 1000000000 | bytes 1000000 | tf_op jit(solution)/shard_map/atoms/pallas_call | solution.py:255
  30.0 0.1 collective-permute-start.2
  30.2 1.0 %collective-permute-done.2 = bf16[16,256]{1,0:T(8,128)(2,1)S(1)} collective-permute-done((bf16[16,256]{1,0:T(8,128)(2,1)S(1)}, bf16[16,256]{1,0:T(8,128)(2,1)S(1)}, u32[]{:S(2)}, u32[]{:S(2)}) %collective-permute-start.2) | collective-permute-done | bytes 8224 | tf_op jit(solution)/shard_map/ppermute | solution.py:460
  31.2 9.5 %collective-permute-start.3 = (bf16[32,256]{1,0:T(8,128)(2,1)S(1)}, bf16[32,256]{1,0:T(8,128)(2,1)S(1)}, u32[]{:S(2)}, u32[]{:S(2)}) collective-permute-start(bf16[32,256]{1,0:T(8,128)(2,1)S(1)} %get-tuple-element.25), channel_id=1, source_target_pairs={{0,2},{1,3},{2,0},{3,1},{4,6},{5,7},{6,4},{7,5},{8,10},{9,11},{10,... | collective-permute-start | bytes 49160 | tf_op jit(solution)/shard_map/ppermute | solution.py:460
  40.7 0.0 collective-permute-start.5
  40.7 1.5 %collective-permute-start.4 = (bf16[32,256]{1,0:T(8,128)(2,1)S(1)}, bf16[32,256]{1,0:T(8,128)(2,1)S(1)}, u32[]{:S(2)}, u32[]{:S(2)}) collective-permute-start(bf16[32,256]{1,0:T(8,128)(2,1)S(1)} %get-tuple-element.25), channel_id=1, source_target_pairs={{0,4},{1,5},{2,6},{3,7},{4,0},{5,1},{6,2},{7,3},{8,12},{9,13},{10,... | collective-permute-start | bytes 49160 | tf_op jit(solution)/shard_map/ppermute | solution.py:460
  42.2 0.2 collective-permute-done.3
  42.4 2.0 %collective-permute-done.4 = bf16[32,256]{1,0:T(8,128)(2,1)S(1)} collective-permute-done((bf16[32,256]{1,0:T(8,128)(2,1)S(1)}, bf16[32,256]{1,0:T(8,128)(2,1)S(1)}, u32[]{:S(2)}, u32[]{:S(2)}) %collective-permute-start.4) | collective-permute-done | bytes 16416 | tf_op jit(solution)/shard_map/ppermute | solution.py:460
  44.4 2.4 %collective-permute-done.5 = bf16[32,256]{1,0:T(8,128)(2,1)S(1)} collective-permute-done((bf16[32,256]{1,0:T(8,128)(2,1)S(1)}, bf16[32,256]{1,0:T(8,128)(2,1)S(1)}, u32[]{:S(2)}, u32[]{:S(2)}) %collective-permute-start.5) | collective-permute-done | bytes 16416 | tf_op jit(solution)/shard_map/ppermute | solution.py:460
  46.8 1.9 %collective-permute-start.7 = (bf16[128,256]{1,0:T(8,128)(2,1)S(1)}, bf16[128,256]{1,0:T(8,128)(2,1)S(1)}, u32[]{:S(2)}, u32[]{:S(2)}) collective-permute-start(bf16[128,256]{1,0:T(8,128)(2,1)S(1)} %constant_dynamic-update-slice_fusion.2.own_ref), channel_id=1, source_target_pairs={{0,16},{1,80},{2,112},{3,96},{4,32},{5,48},{6,0},{7,64},{8,17},{9,... | collective-permute-start | bytes 196616 | tf_op jit(solution)/shard_map/ppermute | solution.py:464
  48.8 0.1 collective-permute-start.6
  48.9 2.1 %collective-permute-start.1 = (bf16[128,128]{1,0:T(8,128)(2,1)S(1)}, bf16[128,128]{1,0:T(8,128)(2,1)S(1)}, u32[]{:S(2)}, u32[]{:S(2)}) collective-permute-start(bf16[128,128]{1,0:T(8,128)(2,1)S(1)} %get-tuple-element.20), channel_id=1, source_target_pairs={{0,1},{1,2},{2,3},{3,4},{4,5},{5,6},{6,7},{7,8},{8,9},{9,10},{10,1... | collective-permute-start | bytes 98312 | tf_op jit(solution)/shard_map/ppermute | solution.py:466
  51.0 5.9 %collective-permute-done.7.col_ref = bf16[128,256]{1,0:T(8,128)(2,1)S(1)} collective-permute-done((bf16[128,256]{1,0:T(8,128)(2,1)S(1)}, bf16[128,256]{1,0:T(8,128)(2,1)S(1)}, u32[]{:S(2)}, u32[]{:S(2)}) %collective-permute-start.7) | collective-permute-done | bytes 65568 | tf_op jit(solution)/shard_map/ppermute | solution.py:464
  56.8 0.0 collective-permute-done.6.other_ref
  56.8 0.0 copy-done.11
  56.8 25.1 %pair_last.1 = bf16[256,128,128]{2,1,0:T(8,128)(2,1)} custom-call(s32[128]{0:T(128)S(1)} %copy-done.11, bf16[256,128,128]{2,1,0:T(8,128)(2,1)} %pair_ref.5, bf16[256,128,128]{2,1,0:T(8,128)(2,1)} %pair_early.1.done_ref, bf16[128,1024]{1,0:T(8,128)(2,1)S(1)} %copy-done, bf16[512,128]{1,0:T(8,128)(2,1)S(1)} %copy-done.1, ...), custom_call_target="tpu_custom_call" | custom-call | flops 12884901888 | bytes 16777216 | tf_op jit(solution)/shard_map/pair_last/pallas_call | solution.py:370
  81.9 0.0 collective-permute-done.1
  81.9 0.6 compare_select_fusion
  (5 shorter events, 0.0 us)
Async XLA Ops:
  0.6 15.6 %copy-start.1 = (bf16[512,128]{1,0:T(8,128)(2,1)S(1)}, bf16[512,128]{1,0:T(8,128)(2,1)}, u32[]{:S(2)}) copy-start(bf16[512,128]{1,0:T(8,128)(2,1)} %w_out_ref.3) | copy-start | bytes 393220
  0.6 15.6 %copy-start = (bf16[128,1024]{1,0:T(8,128)(2,1)S(1)}, bf16[128,1024]{1,0:T(8,128)(2,1)}, u32[]{:S(2)}) copy-start(bf16[128,1024]{1,0:T(8,128)(2,1)} %w_in_ref.3) | copy-start | bytes 786436
  0.7 0.8 copy-start.2
  1.5 0.7 copy-start.4
  2.1 0.7 copy-start.5
  7.9 18.8 %all-to-all-start = ((bf16[16,128,128]{2,1,0:T(8,128)(2,1)}), bf16[16,128,128]{2,1,0:T(8,128)(2,1)S(1)}, u32[]{:S(2)}, u32[]{:S(2)}) async-start(bf16[16,128,128]{2,1,0:T(8,128)(2,1)} %get-tuple-element.14.band_ref), calls=%async_computation | async-start | bytes 1048576 | tf_op jit(solution)/shard_map/all_to_all | solution.py:453
  15.4 11.3 %copy-start.3 = (bf16[128,128]{1,0:T(8,128)(2,1)S(1)}, bf16[128,128]{1,0:T(8,128)(2,1)}, u32[]{:S(2)}) copy-start(bf16[128,128]{1,0:T(8,128)(2,1)} %own_ref.1) | copy-start | bytes 98308
  15.4 11.3 %copy-start.6 = (bf16[384,256]{1,0:T(8,128)(2,1)S(1)}, bf16[384,256]{1,0:T(8,128)(2,1)}, u32[]{:S(2)}) copy-start(bf16[384,256]{1,0:T(8,128)(2,1)} %wsingle_ref.1) | copy-start | bytes 589828
  15.4 11.3 %copy-start.7 = (bf16[128,512]{1,0:T(8,128)(2,1)S(1)}, bf16[128,512]{1,0:T(8,128)(2,1)}, u32[]{:S(2)}) copy-start(bf16[128,512]{1,0:T(8,128)(2,1)} %wattn_ref.1) | copy-start | bytes 393220
  15.4 11.3 %copy-start.8 = (bf16[128,384]{1,0:T(8,128)(2,1)S(1)}, bf16[128,384]{1,0:T(8,128)(2,1)}, u32[]{:S(2)}) copy-start(bf16[128,384]{1,0:T(8,128)(2,1)} %wagg_ref.1) | copy-start | bytes 294916
  15.4 11.3 %copy-start.9 = (bf16[128,128]{1,0:T(8,128)(2,1)S(1)}, bf16[128,128]{1,0:T(8,128)(2,1)}, u32[]{:S(2)}) copy-start(bf16[128,128]{1,0:T(8,128)(2,1)} %wout_ref.1) | copy-start | bytes 98308
  15.4 11.3 %copy-start.10 = (f32[128]{0:T(128)S(1)}, f32[128]{0:T(128)}, u32[]{:S(2)}) copy-start(f32[128]{0:T(128)} %param.15) | copy-start | bytes 1540
  15.4 41.4 %copy-start.11 = (s32[128]{0:T(128)S(1)}, s32[128]{0:T(128)}, u32[]{:S(2)}) copy-start(s32[128]{0:T(128)} %constant.4.clone.sender_ref) | copy-start | bytes 1540
  15.4 11.3 %collective-permute-start = (bf16[96,128]{1,0:T(8,128)(2,1)S(1)}, bf16[96,128]{1,0:T(8,128)(2,1)S(1)}, u32[]{:S(2)}, u32[]{:S(2)}) collective-permute-start(bf16[96,128]{1,0:T(8,128)(2,1)S(1)} %get-tuple-element.15), channel_id=1, source_target_pairs={{15,16},{31,32},{47,48},{63,64},{79,80},{95,96},{111,112},{16,15},... | collective-permute-start | bytes 73736 | tf_op jit(solution)/shard_map/ppermute | solution.py:452
  30.0 1.2 %collective-permute-start.2 = (bf16[16,256]{1,0:T(8,128)(2,1)S(1)}, bf16[16,256]{1,0:T(8,128)(2,1)S(1)}, u32[]{:S(2)}, u32[]{:S(2)}) collective-permute-start(bf16[16,256]{1,0:T(8,128)(2,1)S(1)} %get-tuple-element.21), channel_id=1, source_target_pairs={{0,1},{1,0},{2,3},{3,2},{4,5},{5,4},{6,7},{7,6},{8,9},{9,8},{10,11... | collective-permute-start | bytes 24584 | tf_op jit(solution)/shard_map/ppermute | solution.py:460
  31.2 11.2 %collective-permute-start.3 = (bf16[32,256]{1,0:T(8,128)(2,1)S(1)}, bf16[32,256]{1,0:T(8,128)(2,1)S(1)}, u32[]{:S(2)}, u32[]{:S(2)}) collective-permute-start(bf16[32,256]{1,0:T(8,128)(2,1)S(1)} %get-tuple-element.25), channel_id=1, source_target_pairs={{0,2},{1,3},{2,0},{3,1},{4,6},{5,7},{6,4},{7,5},{8,10},{9,11},{10,... | collective-permute-start | bytes 49160 | tf_op jit(solution)/shard_map/ppermute | solution.py:460
  40.7 6.1 %collective-permute-start.5 = (bf16[32,256]{1,0:T(8,128)(2,1)S(1)}, bf16[32,256]{1,0:T(8,128)(2,1)S(1)}, u32[]{:S(2)}, u32[]{:S(2)}) collective-permute-start(bf16[32,256]{1,0:T(8,128)(2,1)S(1)} %get-tuple-element.25), channel_id=1, source_target_pairs={{0,6},{1,7},{2,4},{3,5},{4,2},{5,3},{6,0},{7,1},{8,14},{9,15},{10,... | collective-permute-start | bytes 49160 | tf_op jit(solution)/shard_map/ppermute | solution.py:460
  40.7 3.7 %collective-permute-start.4 = (bf16[32,256]{1,0:T(8,128)(2,1)S(1)}, bf16[32,256]{1,0:T(8,128)(2,1)S(1)}, u32[]{:S(2)}, u32[]{:S(2)}) collective-permute-start(bf16[32,256]{1,0:T(8,128)(2,1)S(1)} %get-tuple-element.25), channel_id=1, source_target_pairs={{0,4},{1,5},{2,6},{3,7},{4,0},{5,1},{6,2},{7,3},{8,12},{9,13},{10,... | collective-permute-start | bytes 49160 | tf_op jit(solution)/shard_map/ppermute | solution.py:460
  46.8 10.0 %collective-permute-start.7 = (bf16[128,256]{1,0:T(8,128)(2,1)S(1)}, bf16[128,256]{1,0:T(8,128)(2,1)S(1)}, u32[]{:S(2)}, u32[]{:S(2)}) collective-permute-start(bf16[128,256]{1,0:T(8,128)(2,1)S(1)} %constant_dynamic-update-slice_fusion.2.own_ref), channel_id=1, source_target_pairs={{0,16},{1,80},{2,112},{3,96},{4,32},{5,48},{6,0},{7,64},{8,17},{9,... | collective-permute-start | bytes 196616 | tf_op jit(solution)/shard_map/ppermute | solution.py:464
  48.8 8.1 %collective-permute-start.6 = (bf16[128,256]{1,0:T(8,128)(2,1)S(1)}, bf16[128,256]{1,0:T(8,128)(2,1)S(1)}, u32[]{:S(2)}, u32[]{:S(2)}) collective-permute-start(bf16[128,256]{1,0:T(8,128)(2,1)S(1)} %constant_dynamic-update-slice_fusion.2.own_ref), channel_id=1, source_target_pairs={{0,8},{1,9},{2,10},{3,11},{4,12},{5,13},{6,14},{7,15},{8,0},{9,1},... | collective-permute-start | bytes 196616 | tf_op jit(solution)/shard_map/ppermute | solution.py:465
  48.9 33.1 %collective-permute-start.1 = (bf16[128,128]{1,0:T(8,128)(2,1)S(1)}, bf16[128,128]{1,0:T(8,128)(2,1)S(1)}, u32[]{:S(2)}, u32[]{:S(2)}) collective-permute-start(bf16[128,128]{1,0:T(8,128)(2,1)S(1)} %get-tuple-element.20), channel_id=1, source_target_pairs={{0,1},{1,2},{2,3},{3,4},{4,5},{5,6},{6,7},{7,8},{8,9},{9,10},{10,1... | collective-permute-start | bytes 98312 | tf_op jit(solution)/shard_map/ppermute | solution.py:466

commit v7 on v6

--- a/solution.py
+++ b/solution.py
@@ -24,7 +24,7 @@
 MIB = 1024 * 1024
 WIDE = 50
 ROWS = 64
-EARLY = 16
+EARLY = 32
 SUB = 512
 
 
@@ -146,7 +146,7 @@
             pltpu.SemaphoreType.DMA((3,)),
         ],
         cost_estimate=pl.CostEstimate(flops=10**9, bytes_accessed=3 * 10**6, transcendentals=0),
-        compiler_params=pltpu.CompilerParams(vmem_limit_bytes=WIDE * MIB),
+        compiler_params=pltpu.CompilerParams(vmem_limit_bytes=56 * MIB),
         name="band",
     )(pair_act, w_bias.T, atom_act, atom_token[None, :])
 
@@ -310,11 +310,11 @@
 
 def early_part(pair_act, w_in, w_out, band):
     rows, cols, width = pair_act.shape
-    block = pl.BlockSpec((EARLY, cols, width), lambda i: (ROWS // EARLY * i, 0, 0))
-    cells = rows // ROWS * EARLY * cols
+    block = pl.BlockSpec((EARLY, cols, width), lambda i: (i, 0, 0))
+    cells = ROWS * cols
     return pl.pallas_call(
         early_kernel,
-        grid=(rows // ROWS,),
+        grid=(ROWS // EARLY,),
         in_specs=[block, whole(w_in), whole(w_out), pl.BlockSpec(memory_space=pl.ANY)],
         out_specs=block,
         out_shape=jax.ShapeDtypeStruct(pair_act.shape, jnp.bfloat16),
@@ -353,24 +353,31 @@
     base = pl.multiple_of(i * rows, rows)
     col_add = col_scr[...]
     step = SUB // cols
-    for k in range(EARLY, rows, step):
-        moved = transition(pair_ref[k : k + step], w_in_scr, w_out_ref)
-        for s in range(step):
-            extra = row_scr[pl.ds(base + k + s, 1), :] + col_add
-            out_ref[k + s] = (moved[s * cols : (s + 1) * cols] + extra).astype(jnp.bfloat16)
-    for r in range(EARLY):
-        extra = row_scr[pl.ds(base + r, 1), :] + col_add
-        out_ref[r] = (done_ref[r].astype(jnp.float32) + extra).astype(jnp.bfloat16)
+
+    @pl.when(i == 0)
+    def _():
+        for r in range(rows):
+            extra = row_scr[r : r + 1, :] + col_add
+            out_ref[r] = (done_ref[r].astype(jnp.float32) + extra).astype(jnp.bfloat16)
+
+    @pl.when(i > 0)
+    def _():
+        for k in range(0, rows, step):
+            moved = transition(pair_ref[k : k + step], w_in_scr, w_out_ref)
+            for s in range(step):
+                extra = row_scr[pl.ds(base + k + s, 1), :] + col_add
+                out_ref[k + s] = (moved[s * cols : (s + 1) * cols] + extra).astype(jnp.bfloat16)
 
 
 def last_part(senders, pair_act, done, w_in, w_out, own, other, col):
     rows, cols, width = pair_act.shape
     block = pl.BlockSpec((ROWS, cols, width), lambda i: (i, 0, 0))
-    done_block = pl.BlockSpec((EARLY, cols, width), lambda i: (ROWS // EARLY * i, 0, 0))
+    done_block = pl.BlockSpec((ROWS, cols, width), lambda i: (0, 0, 0))
+    pair_block = pl.BlockSpec((ROWS, cols, width), lambda i: (jnp.maximum(i, 1), 0, 0))
     return pl.pallas_call(
         last_kernel,
         grid=(rows // ROWS,),
-        in_specs=[pl.BlockSpec(memory_space=pltpu.SMEM), block, done_block]
+        in_specs=[pl.BlockSpec(memory_space=pltpu.SMEM), pair_block, done_block]
         + [whole(x) for x in (w_in, w_out, own, other, col)],
         out_specs=block,
         out_shape=jax.ShapeDtypeStruct(pair_act.shape, jnp.bfloat16),

time: 82.9 us -> 81.6 us (0.984)
  local copies, waits for them, and re-layouts: 2.2 us -> 1.1 us
    unnamed x27 -> x25, local copies, waits for them, and re-layouts: 2.19 us -> 1.09 us
where the time goes in v7:
time: 81.6 us; the launch traced here: 81.3 us
  Pallas kernels  43.9 us (54%)
  starting transfers between devices  23.3 us (29%)
  waiting for transfers between devices  11.6 us (14%)
  local copies, waits for them, and re-layouts  1.1 us (1%)
    pallas_call x1, Pallas kernels, last_part(): pl.pallas_call(last_kernel, grid=(rows // ROWS,), in_specs=[pl.BlockSpec(...  25.4 us
    ppermute x4, starting transfers between devices, swapped(): return lax.ppermute(value, 'col', [(i, i ^ bits) for i in range(n_col)])  11.1 us
    pallas_call x1, Pallas kernels, early_part(): pl.pallas_call(early_kernel, grid=(ROWS // EARLY,), in_specs=[block, whol...  9.88 us
    all_to_all x1, starting transfers between devices, on_device(): near = lax.all_to_all(band, 'col', 0, 0, tiled=True)  7.46 us
    ppermute x1, waiting for transfers between devices, on_device(): col_all = lax.ppermute(held, both, turn)  5.87 us
    ppermute x4, waiting for transfers between devices, swapped(): return lax.ppermute(value, 'col', [(i, i ^ bits) for i in range(n_col)])  5.69 us
    pallas_call x1, Pallas kernels, band_biases(): pl.pallas_call(band_kernel, in_specs=[pl.BlockSpec(memory_space=pltpu.HBM...  5.33 us
    pallas_call x1, Pallas kernels, atom_part(): pl.pallas_call(atom_kernel, in_specs=[vmem] * 9, out_specs=[vmem] * 5, ou...  3.28 us
  transfers between devices with their start and end apart: 9, of which 5 were waited for; matrix products, arithmetic and copies ran while one was open for 0% of the time, Pallas kernels for 43%

profile of v7, /device:TPU:6, one launch (start us, length us, event | category | flops | bytes accessed | tf_op | source)
XLA Modules:
  0.0 81.3 jit_solution(15826962462806963808)
XLA Ops:
  0.6 0.0 copy-start.2
  0.6 0.0 copy-start.1
  0.7 5.3 %band.1 = (bf16[16,128,128]{2,1,0:T(8,128)(2,1)}, bf16[96,128]{1,0:T(8,128)(2,1)}, bf16[16,128]{1,0:T(8,128)(2,1)}) custom-call(bf16[256,128,128]{2,1,0:T(8,128)(2,1)} %pair_ref.5, bf16[4,128]{1,0:T(4,128)(2,1)} %bitcast.4, bf16[128,128]{1,0:T(8,128)(2,1)} %own_ref.1, s32[1,128]{1,0:T(1,128)} %bitcast.5), custom_call_target="tpu_custom_call" | custom-call | flops 1000000000 | bytes 3000000 | tf_op jit(solution)/shard_map/band/pallas_call | solution.py:131
  6.0 7.5 %all-to-all-start = ((bf16[16,128,128]{2,1,0:T(8,128)(2,1)}), bf16[16,128,128]{2,1,0:T(8,128)(2,1)S(1)}, u32[]{:S(2)}, u32[]{:S(2)}) async-start(bf16[16,128,128]{2,1,0:T(8,128)(2,1)} %get-tuple-element.14.band_ref), calls=%async_computation | async-start | bytes 1048576 | tf_op jit(solution)/shard_map/all_to_all | solution.py:460
  13.4 0.7 collective-permute-start
  14.1 0.0 copy-done.2
  14.1 0.0 copy-done.1
  14.1 0.0 copy-start
  14.1 1.0 %copy-done = bf16[16,128,128]{2,1,0:T(8,128)(2,1)S(1)} copy-done((bf16[16,128,128]{2,1,0:T(8,128)(2,1)S(1)}, bf16[16,128,128]{2,1,0:T(8,128)(2,1)}, u32[]{:S(2)}) %copy-start) | copy-done | bytes 524312
  15.2 0.0 copy-start.3
  15.2 0.0 copy-start.4
  15.2 0.0 copy-start.5
  15.2 0.0 copy-start.6
  15.2 0.0 copy-start.7
  15.2 0.0 copy-start.8
  15.2 0.0 copy-start.9
  15.2 0.0 copy-start.10
  15.2 9.9 %pair_early.1.done_ref = bf16[256,128,128]{2,1,0:T(8,128)(2,1)} custom-call(bf16[256,128,128]{2,1,0:T(8,128)(2,1)} %pair_ref.5, bf16[128,1024]{1,0:T(8,128)(2,1)S(1)} %copy-done.1, bf16[512,128]{1,0:T(8,128)(2,1)S(1)} %copy-done.2, bf16[16,128,128]{2,1,0:T(8,128)(2,1)S(1)} %copy-done), custom_call_target="tpu_custom_call" | custom-call | flops 3221225472 | bytes 4194304 | tf_op jit(solution)/shard_map/pair_early/pallas_call | solution.py:315
  25.1 0.0 collective-permute-done.cross_ref
  25.1 0.0 all-to-all-done.near_ref
  25.1 0.0 copy-done.3
  25.1 0.0 copy-done.4
  25.1 0.0 copy-done.5
  25.1 0.0 copy-done.6
  25.1 0.0 copy-done.7
  25.2 0.0 copy-done.8
  25.2 0.0 copy-done.9
  25.2 3.3 %atoms.1 = (bf16[128,128]{1,0:T(8,128)(2,1)S(1)}, bf16[128,128]{1,0:T(8,128)(2,1)S(1)}, bf16[128,128]{1,0:T(8,128)(2,1)S(1)}, bf16[16,384]{1,0:T(8,128)(2,1)}, bf16[16,256]{1,0:T(8,128)(2,1)S(1)}) custom-call(bf16[96,128]{1,0:T(8,128)(2,1)S(1)} %collective-permute-done.cross_ref, bf16[128,128]{1,0:T(8,128)(2,1)S(1)} %copy-done.3, ...), custom_call_target="tpu_custom_call" | custom-call | flops 1000000000 | bytes 1000000 | tf_op jit(solution)/shard_map/atoms/pallas_call | solution.py:255
  28.5 0.1 collective-permute-start.2
  28.6 1.0 %collective-permute-done.2 = bf16[16,256]{1,0:T(8,128)(2,1)S(1)} collective-permute-done((bf16[16,256]{1,0:T(8,128)(2,1)S(1)}, bf16[16,256]{1,0:T(8,128)(2,1)S(1)}, u32[]{:S(2)}, u32[]{:S(2)}) %collective-permute-start.2) | collective-permute-done | bytes 8224 | tf_op jit(solution)/shard_map/ppermute | solution.py:467
  29.6 9.5 %collective-permute-start.3 = (bf16[32,256]{1,0:T(8,128)(2,1)S(1)}, bf16[32,256]{1,0:T(8,128)(2,1)S(1)}, u32[]{:S(2)}, u32[]{:S(2)}) collective-permute-start(bf16[32,256]{1,0:T(8,128)(2,1)S(1)} %get-tuple-element.25), channel_id=1, source_target_pairs={{0,2},{1,3},{2,0},{3,1},{4,6},{5,7},{6,4},{7,5},{8,10},{9,11},{10,... | collective-permute-start | bytes 49160 | tf_op jit(solution)/shard_map/ppermute | solution.py:467
  39.1 0.0 collective-permute-start.5
  39.1 1.5 %collective-permute-start.4 = (bf16[32,256]{1,0:T(8,128)(2,1)S(1)}, bf16[32,256]{1,0:T(8,128)(2,1)S(1)}, u32[]{:S(2)}, u32[]{:S(2)}) collective-permute-start(bf16[32,256]{1,0:T(8,128)(2,1)S(1)} %get-tuple-element.25), channel_id=1, source_target_pairs={{0,4},{1,5},{2,6},{3,7},{4,0},{5,1},{6,2},{7,3},{8,12},{9,13},{10,... | collective-permute-start | bytes 49160 | tf_op jit(solution)/shard_map/ppermute | solution.py:467
  40.6 0.2 collective-permute-done.3
  40.8 2.0 %collective-permute-done.4 = bf16[32,256]{1,0:T(8,128)(2,1)S(1)} collective-permute-done((bf16[32,256]{1,0:T(8,128)(2,1)S(1)}, bf16[32,256]{1,0:T(8,128)(2,1)S(1)}, u32[]{:S(2)}, u32[]{:S(2)}) %collective-permute-start.4) | collective-permute-done | bytes 16416 | tf_op jit(solution)/shard_map/ppermute | solution.py:467
  42.9 2.4 %collective-permute-done.5 = bf16[32,256]{1,0:T(8,128)(2,1)S(1)} collective-permute-done((bf16[32,256]{1,0:T(8,128)(2,1)S(1)}, bf16[32,256]{1,0:T(8,128)(2,1)S(1)}, u32[]{:S(2)}, u32[]{:S(2)}) %collective-permute-start.5) | collective-permute-done | bytes 16416 | tf_op jit(solution)/shard_map/ppermute | solution.py:467
  45.3 1.9 %collective-permute-start.7 = (bf16[128,256]{1,0:T(8,128)(2,1)S(1)}, bf16[128,256]{1,0:T(8,128)(2,1)S(1)}, u32[]{:S(2)}, u32[]{:S(2)}) collective-permute-start(bf16[128,256]{1,0:T(8,128)(2,1)S(1)} %constant_dynamic-update-slice_fusion.2.own_ref), channel_id=1, source_target_pairs={{0,16},{1,80},{2,112},{3,96},{4,32},{5,48},{6,0},{7,64},{8,17},{9,... | collective-permute-start | bytes 196616 | tf_op jit(solution)/shard_map/ppermute | solution.py:471
  47.2 0.1 collective-permute-start.6
  47.3 2.1 %collective-permute-start.1 = (bf16[128,128]{1,0:T(8,128)(2,1)S(1)}, bf16[128,128]{1,0:T(8,128)(2,1)S(1)}, u32[]{:S(2)}, u32[]{:S(2)}) collective-permute-start(bf16[128,128]{1,0:T(8,128)(2,1)S(1)} %get-tuple-element.20), channel_id=1, source_target_pairs={{0,1},{1,2},{2,3},{3,4},{4,5},{5,6},{6,7},{7,8},{8,9},{9,10},{10,1... | collective-permute-start | bytes 98312 | tf_op jit(solution)/shard_map/ppermute | solution.py:473
  49.4 5.9 %collective-permute-done.7.col_ref = bf16[128,256]{1,0:T(8,128)(2,1)S(1)} collective-permute-done((bf16[128,256]{1,0:T(8,128)(2,1)S(1)}, bf16[128,256]{1,0:T(8,128)(2,1)S(1)}, u32[]{:S(2)}, u32[]{:S(2)}) %collective-permute-start.7) | collective-permute-done | bytes 65568 | tf_op jit(solution)/shard_map/ppermute | solution.py:471
  55.3 0.0 collective-permute-done.6.other_ref
  55.3 0.0 copy-done.10
  55.3 25.4 %pair_last.1 = bf16[256,128,128]{2,1,0:T(8,128)(2,1)} custom-call(s32[128]{0:T(128)S(1)} %copy-done.10, bf16[256,128,128]{2,1,0:T(8,128)(2,1)} %pair_ref.5, bf16[256,128,128]{2,1,0:T(8,128)(2,1)} %pair_early.1.done_ref, bf16[128,1024]{1,0:T(8,128)(2,1)S(1)} %copy-done.1, bf16[512,128]{1,0:T(8,128)(2,1)S(1)} %copy-done.2, ...), custom_call_target="tpu_custom_call" | custom-call | flops 12884901888 | bytes 16777216 | tf_op jit(solution)/shard_map/pair_last/pallas_call | solution.py:377
  80.6 0.0 collective-permute-done.1
  80.7 0.6 compare_select_fusion
  (5 shorter events, 0.0 us)
Async XLA Ops:
  0.6 13.5 %copy-start.2 = (bf16[512,128]{1,0:T(8,128)(2,1)S(1)}, bf16[512,128]{1,0:T(8,128)(2,1)}, u32[]{:S(2)}) copy-start(bf16[512,128]{1,0:T(8,128)(2,1)} %w_out_ref.3) | copy-start | bytes 393220
  0.6 13.5 %copy-start.1 = (bf16[128,1024]{1,0:T(8,128)(2,1)S(1)}, bf16[128,1024]{1,0:T(8,128)(2,1)}, u32[]{:S(2)}) copy-start(bf16[128,1024]{1,0:T(8,128)(2,1)} %w_in_ref.3) | copy-start | bytes 786436
  6.0 19.1 %all-to-all-start = ((bf16[16,128,128]{2,1,0:T(8,128)(2,1)}), bf16[16,128,128]{2,1,0:T(8,128)(2,1)S(1)}, u32[]{:S(2)}, u32[]{:S(2)}) async-start(bf16[16,128,128]{2,1,0:T(8,128)(2,1)} %get-tuple-element.14.band_ref), calls=%async_computation | async-start | bytes 1048576 | tf_op jit(solution)/shard_map/all_to_all | solution.py:460
  13.4 11.7 %collective-permute-start = (bf16[96,128]{1,0:T(8,128)(2,1)}, bf16[96,128]{1,0:T(8,128)(2,1)S(1)}, u32[]{:S(2)}, u32[]{:S(2)}) collective-permute-start(bf16[96,128]{1,0:T(8,128)(2,1)} %get-tuple-element.15), channel_id=1, source_target_pairs={{15,16},{31,32},{47,48},{63,64},{79,80},{95,96},{111,112},{16,15},... | collective-permute-start | bytes 73736 | tf_op jit(solution)/shard_map/ppermute | solution.py:459
  14.1 1.0 %copy-start = (bf16[16,128,128]{2,1,0:T(8,128)(2,1)S(1)}, bf16[16,128,128]{2,1,0:T(8,128)(2,1)}, u32[]{:S(2)}) copy-start(bf16[16,128,128]{2,1,0:T(8,128)(2,1)} %get-tuple-element.14.band_ref) | copy-start | bytes 1572868
  15.2 9.9 %copy-start.3 = (bf16[128,128]{1,0:T(8,128)(2,1)S(1)}, bf16[128,128]{1,0:T(8,128)(2,1)}, u32[]{:S(2)}) copy-start(bf16[128,128]{1,0:T(8,128)(2,1)} %own_ref.1) | copy-start | bytes 98308
  15.2 9.9 %copy-start.4 = (bf16[384,256]{1,0:T(8,128)(2,1)S(1)}, bf16[384,256]{1,0:T(8,128)(2,1)}, u32[]{:S(2)}) copy-start(bf16[384,256]{1,0:T(8,128)(2,1)} %wsingle_ref.1) | copy-start | bytes 589828
  15.2 10.0 %copy-start.5 = (bf16[128,512]{1,0:T(8,128)(2,1)S(1)}, bf16[128,512]{1,0:T(8,128)(2,1)}, u32[]{:S(2)}) copy-start(bf16[128,512]{1,0:T(8,128)(2,1)} %wattn_ref.1) | copy-start | bytes 393220
  15.2 10.0 %copy-start.6 = (bf16[128,384]{1,0:T(8,128)(2,1)S(1)}, bf16[128,384]{1,0:T(8,128)(2,1)}, u32[]{:S(2)}) copy-start(bf16[128,384]{1,0:T(8,128)(2,1)} %wagg_ref.1) | copy-start | bytes 294916
  15.2 10.0 %copy-start.7 = (bf16[128,128]{1,0:T(8,128)(2,1)S(1)}, bf16[128,128]{1,0:T(8,128)(2,1)}, u32[]{:S(2)}) copy-start(bf16[128,128]{1,0:T(8,128)(2,1)} %wout_ref.1) | copy-start | bytes 98308
  15.2 10.0 %copy-start.8 = (bf16[16,128]{1,0:T(8,128)(2,1)S(1)}, bf16[16,128]{1,0:T(8,128)(2,1)}, u32[]{:S(2)}) copy-start(bf16[16,128]{1,0:T(8,128)(2,1)} %get-tuple-element.17.tok_ref) | copy-start | bytes 12292
  15.2 10.0 %copy-start.9 = (f32[128]{0:T(128)S(1)}, f32[128]{0:T(128)}, u32[]{:S(2)}) copy-start(f32[128]{0:T(128)} %param.15) | copy-start | bytes 1540
  15.2 40.0 %copy-start.10 = (s32[128]{0:T(128)S(1)}, s32[128]{0:T(128)}, u32[]{:S(2)}) copy-start(s32[128]{0:T(128)} %constant.4.clone.sender_ref) | copy-start | bytes 1540
  28.5 1.2 %collective-permute-start.2 = (bf16[16,256]{1,0:T(8,128)(2,1)S(1)}, bf16[16,256]{1,0:T(8,128)(2,1)S(1)}, u32[]{:S(2)}, u32[]{:S(2)}) collective-permute-start(bf16[16,256]{1,0:T(8,128)(2,1)S(1)} %get-tuple-element.21), channel_id=1, source_target_pairs={{0,1},{1,0},{2,3},{3,2},{4,5},{5,4},{6,7},{7,6},{8,9},{9,8},{10,11... | collective-permute-start | bytes 24584 | tf_op jit(solution)/shard_map/ppermute | solution.py:467
  29.6 11.2 %collective-permute-start.3 = (bf16[32,256]{1,0:T(8,128)(2,1)S(1)}, bf16[32,256]{1,0:T(8,128)(2,1)S(1)}, u32[]{:S(2)}, u32[]{:S(2)}) collective-permute-start(bf16[32,256]{1,0:T(8,128)(2,1)S(1)} %get-tuple-element.25), channel_id=1, source_target_pairs={{0,2},{1,3},{2,0},{3,1},{4,6},{5,7},{6,4},{7,5},{8,10},{9,11},{10,... | collective-permute-start | bytes 49160 | tf_op jit(solution)/shard_map/ppermute | solution.py:467
  39.1 6.1 %collective-permute-start.5 = (bf16[32,256]{1,0:T(8,128)(2,1)S(1)}, bf16[32,256]{1,0:T(8,128)(2,1)S(1)}, u32[]{:S(2)}, u32[]{:S(2)}) collective-permute-start(bf16[32,256]{1,0:T(8,128)(2,1)S(1)} %get-tuple-element.25), channel_id=1, source_target_pairs={{0,6},{1,7},{2,4},{3,5},{4,2},{5,3},{6,0},{7,1},{8,14},{9,15},{10,... | collective-permute-start | bytes 49160 | tf_op jit(solution)/shard_map/ppermute | solution.py:467
  39.1 3.7 %collective-permute-start.4 = (bf16[32,256]{1,0:T(8,128)(2,1)S(1)}, bf16[32,256]{1,0:T(8,128)(2,1)S(1)}, u32[]{:S(2)}, u32[]{:S(2)}) collective-permute-start(bf16[32,256]{1,0:T(8,128)(2,1)S(1)} %get-tuple-element.25), channel_id=1, source_target_pairs={{0,4},{1,5},{2,6},{3,7},{4,0},{5,1},{6,2},{7,3},{8,12},{9,13},{10,... | collective-permute-start | bytes 49160 | tf_op jit(solution)/shard_map/ppermute | solution.py:467
  45.3 10.0 %collective-permute-start.7 = (bf16[128,256]{1,0:T(8,128)(2,1)S(1)}, bf16[128,256]{1,0:T(8,128)(2,1)S(1)}, u32[]{:S(2)}, u32[]{:S(2)}) collective-permute-start(bf16[128,256]{1,0:T(8,128)(2,1)S(1)} %constant_dynamic-update-slice_fusion.2.own_ref), channel_id=1, source_target_pairs={{0,16},{1,80},{2,112},{3,96},{4,32},{5,48},{6,0},{7,64},{8,17},{9,... | collective-permute-start | bytes 196616 | tf_op jit(solution)/shard_map/ppermute | solution.py:471
  47.2 8.1 %collective-permute-start.6 = (bf16[128,256]{1,0:T(8,128)(2,1)S(1)}, bf16[128,256]{1,0:T(8,128)(2,1)S(1)}, u32[]{:S(2)}, u32[]{:S(2)}) collective-permute-start(bf16[128,256]{1,0:T(8,128)(2,1)S(1)} %constant_dynamic-update-slice_fusion.2.own_ref), channel_id=1, source_target_pairs={{0,8},{1,9},{2,10},{3,11},{4,12},{5,13},{6,14},{7,15},{8,0},{9,1},... | collective-permute-start | bytes 196616 | tf_op jit(solution)/shard_map/ppermute | solution.py:472
  47.3 33.4 %collective-permute-start.1 = (bf16[128,128]{1,0:T(8,128)(2,1)S(1)}, bf16[128,128]{1,0:T(8,128)(2,1)S(1)}, u32[]{:S(2)}, u32[]{:S(2)}) collective-permute-start(bf16[128,128]{1,0:T(8,128)(2,1)S(1)} %get-tuple-element.20), channel_id=1, source_target_pairs={{0,1},{1,2},{2,3},{3,4},{4,5},{5,6},{6,7},{7,8},{8,9},{9,10},{10,1... | collective-permute-start | bytes 98312 | tf_op jit(solution)/shard_map/ppermute | solution.py:473

commit v8 on v7

--- a/solution.py
+++ b/solution.py
@@ -322,7 +322,7 @@
         cost_estimate=pl.CostEstimate(
             flops=cells * 196608 * 2, bytes_accessed=cells * 512, transcendentals=0
         ),
-        compiler_params=pltpu.CompilerParams(vmem_limit_bytes=WIDE * MIB),
+        compiler_params=pltpu.CompilerParams(vmem_limit_bytes=56 * MIB),
         name="pair_early",
     )(pair_act, w_in, w_out, band)
 

time: 81.6 us -> 80.7 us (0.989)
  local copies, waits for them, and re-layouts: 1.1 us -> 0.07 us
    unnamed x25 -> x23, local copies, waits for them, and re-layouts: 1.09 us -> 0.07 us
  transfers between devices with their start and end apart: 9 -> 9, of which waited for: 5 -> 5; matrix products, arithmetic and copies ran while one was open for 0% -> 0% of each run, Pallas kernels for 43% -> 44%
where the time goes in v8:
time: 80.7 us; the launch traced here: 80.3 us
  Pallas kernels  44 us (55%)
  starting transfers between devices  23.4 us (29%)
  waiting for transfers between devices  11.3 us (14%)
  between operations  0.83 us (1%)
    pallas_call x1, Pallas kernels, last_part(): pl.pallas_call(last_kernel, grid=(rows // ROWS,), in_specs=[pl.BlockSpec(...  25.4 us
    ppermute x4, starting transfers between devices, swapped(): return lax.ppermute(value, 'col', [(i, i ^ bits) for i in range(n_col)])  10.9 us
    pallas_call x1, Pallas kernels, early_part(): pl.pallas_call(early_kernel, grid=(ROWS // EARLY,), in_specs=[block, whol...  10.1 us
    all_to_all x1, starting transfers between devices, on_device(): near = lax.all_to_all(band, 'col', 0, 0, tiled=True)  7.46 us
    ppermute x4, waiting for transfers between devices, swapped(): return lax.ppermute(value, 'col', [(i, i ^ bits) for i in range(n_col)])  5.68 us
    ppermute x1, waiting for transfers between devices, on_device(): col_all = lax.ppermute(held, both, turn)  5.63 us
    pallas_call x1, Pallas kernels, band_biases(): pl.pallas_call(band_kernel, in_specs=[pl.BlockSpec(memory_space=pltpu.HBM...  5.25 us
    pallas_call x1, Pallas kernels, atom_part(): pl.pallas_call(atom_kernel, in_specs=[vmem] * 9, out_specs=[vmem] * 5, ou...  3.28 us
  transfers between devices with their start and end apart: 9, of which 5 were waited for; matrix products, arithmetic and copies ran while one was open for 0% of the time, Pallas kernels for 44%

profile of v8, /device:TPU:6, one launch (start us, length us, event | category | flops | bytes accessed | tf_op | source)
XLA Modules:
  0.0 80.3 jit_solution(12989009086799402438)
XLA Ops:
  0.6 5.2 %band.1 = (bf16[16,128,128]{2,1,0:T(8,128)(2,1)}, bf16[96,128]{1,0:T(8,128)(2,1)}, bf16[16,128]{1,0:T(8,128)(2,1)}) custom-call(bf16[256,128,128]{2,1,0:T(8,128)(2,1)} %pair_ref.5, bf16[4,128]{1,0:T(4,128)(2,1)} %bitcast.4, bf16[128,128]{1,0:T(8,128)(2,1)} %own_ref.1, s32[1,128]{1,0:T(1,128)} %bitcast.5), custom_call_target="tpu_custom_call" | custom-call | flops 1000000000 | bytes 3000000 | tf_op jit(solution)/shard_map/band/pallas_call | solution.py:131
  5.9 7.5 %all-to-all-start = ((bf16[16,128,128]{2,1,0:T(8,128)(2,1)}), bf16[16,128,128]{2,1,0:T(8,128)(2,1)S(1)}, u32[]{:S(2)}, u32[]{:S(2)}) async-start(bf16[16,128,128]{2,1,0:T(8,128)(2,1)} %get-tuple-element.14.band_ref), calls=%async_computation | async-start | bytes 1048576 | tf_op jit(solution)/shard_map/all_to_all | solution.py:460
  13.3 0.0 copy-start.2
  13.4 0.0 copy-start.3
  13.4 0.0 copy-start.4
  13.4 0.0 copy-start.5
  13.4 0.0 copy-start.6
  13.4 0.0 copy-start.7
  13.4 0.0 copy-start.8
  13.4 0.0 copy-start
  13.4 0.0 copy-start.1
  13.4 0.0 copy-start.9
  13.5 0.8 collective-permute-start
  14.3 10.1 %pair_early.1.done_ref = bf16[256,128,128]{2,1,0:T(8,128)(2,1)} custom-call(bf16[256,128,128]{2,1,0:T(8,128)(2,1)} %pair_ref.5, bf16[128,1024]{1,0:T(8,128)(2,1)} %w_in_ref.3, bf16[512,128]{1,0:T(8,128)(2,1)} %w_out_ref.3, bf16[16,128,128]{2,1,0:T(8,128)(2,1)} %get-tuple-element.14.band_ref), custom_call_target="tpu_custom_call" | custom-call | flops 3221225472 | bytes 4194304 | tf_op jit(solution)/shard_map/pair_early/pallas_call | solution.py:315
  24.4 0.0 collective-permute-done.cross_ref
  24.4 0.0 all-to-all-done.near_ref
  24.4 0.0 copy-done.2
  24.4 0.0 copy-done.3
  24.4 0.0 copy-done.4
  24.4 0.0 copy-done.5
  24.4 0.0 copy-done.6
  24.4 0.0 copy-done.7
  24.4 0.0 copy-done.8
  24.4 3.3 %atoms.1 = (bf16[128,128]{1,0:T(8,128)(2,1)S(1)}, bf16[128,128]{1,0:T(8,128)(2,1)S(1)}, bf16[128,128]{1,0:T(8,128)(2,1)S(1)}, bf16[16,384]{1,0:T(8,128)(2,1)}, bf16[16,256]{1,0:T(8,128)(2,1)S(1)}) custom-call(bf16[96,128]{1,0:T(8,128)(2,1)S(1)} %collective-permute-done.cross_ref, bf16[128,128]{1,0:T(8,128)(2,1)S(1)} %copy-done.2, ...), custom_call_target="tpu_custom_call" | custom-call | flops 1000000000 | bytes 1000000 | tf_op jit(solution)/shard_map/atoms/pallas_call | solution.py:255
  27.7 0.2 collective-permute-start.2
  27.9 1.0 %collective-permute-done.2 = bf16[16,256]{1,0:T(8,128)(2,1)S(1)} collective-permute-done((bf16[16,256]{1,0:T(8,128)(2,1)S(1)}, bf16[16,256]{1,0:T(8,128)(2,1)S(1)}, u32[]{:S(2)}, u32[]{:S(2)}) %collective-permute-start.2) | collective-permute-done | bytes 8224 | tf_op jit(solution)/shard_map/ppermute | solution.py:467
  28.9 9.2 %collective-permute-start.3 = (bf16[32,256]{1,0:T(8,128)(2,1)S(1)}, bf16[32,256]{1,0:T(8,128)(2,1)S(1)}, u32[]{:S(2)}, u32[]{:S(2)}) collective-permute-start(bf16[32,256]{1,0:T(8,128)(2,1)S(1)} %get-tuple-element.25), channel_id=1, source_target_pairs={{0,2},{1,3},{2,0},{3,1},{4,6},{5,7},{6,4},{7,5},{8,10},{9,11},{10,... | collective-permute-start | bytes 49160 | tf_op jit(solution)/shard_map/ppermute | solution.py:467
  38.1 0.0 collective-permute-start.5
  38.2 1.5 %collective-permute-start.4 = (bf16[32,256]{1,0:T(8,128)(2,1)S(1)}, bf16[32,256]{1,0:T(8,128)(2,1)S(1)}, u32[]{:S(2)}, u32[]{:S(2)}) collective-permute-start(bf16[32,256]{1,0:T(8,128)(2,1)S(1)} %get-tuple-element.25), channel_id=1, source_target_pairs={{0,4},{1,5},{2,6},{3,7},{4,0},{5,1},{6,2},{7,3},{8,12},{9,13},{10,... | collective-permute-start | bytes 49160 | tf_op jit(solution)/shard_map/ppermute | solution.py:467
  39.6 0.2 collective-permute-done.3
  39.9 2.0 %collective-permute-done.4 = bf16[32,256]{1,0:T(8,128)(2,1)S(1)} collective-permute-done((bf16[32,256]{1,0:T(8,128)(2,1)S(1)}, bf16[32,256]{1,0:T(8,128)(2,1)S(1)}, u32[]{:S(2)}, u32[]{:S(2)}) %collective-permute-start.4) | collective-permute-done | bytes 16416 | tf_op jit(solution)/shard_map/ppermute | solution.py:467
  41.9 2.4 %collective-permute-done.5 = bf16[32,256]{1,0:T(8,128)(2,1)S(1)} collective-permute-done((bf16[32,256]{1,0:T(8,128)(2,1)S(1)}, bf16[32,256]{1,0:T(8,128)(2,1)S(1)}, u32[]{:S(2)}, u32[]{:S(2)}) %collective-permute-start.5) | collective-permute-done | bytes 16416 | tf_op jit(solution)/shard_map/ppermute | solution.py:467
  44.3 1.9 %collective-permute-start.7 = (bf16[128,256]{1,0:T(8,128)(2,1)S(1)}, bf16[128,256]{1,0:T(8,128)(2,1)S(1)}, u32[]{:S(2)}, u32[]{:S(2)}) collective-permute-start(bf16[128,256]{1,0:T(8,128)(2,1)S(1)} %constant_dynamic-update-slice_fusion.2.own_ref), channel_id=1, source_target_pairs={{0,16},{1,80},{2,112},{3,96},{4,32},{5,48},{6,0},{7,64},{8,17},{9,... | collective-permute-start | bytes 196616 | tf_op jit(solution)/shard_map/ppermute | solution.py:471
  46.2 0.1 collective-permute-start.6
  46.3 2.3 %collective-permute-start.1 = (bf16[128,128]{1,0:T(8,128)(2,1)S(1)}, bf16[128,128]{1,0:T(8,128)(2,1)S(1)}, u32[]{:S(2)}, u32[]{:S(2)}) collective-permute-start(bf16[128,128]{1,0:T(8,128)(2,1)S(1)} %get-tuple-element.20), channel_id=1, source_target_pairs={{0,1},{1,2},{2,3},{3,4},{4,5},{5,6},{6,7},{7,8},{8,9},{9,10},{10,1... | collective-permute-start | bytes 98312 | tf_op jit(solution)/shard_map/ppermute | solution.py:473
  48.6 5.6 %collective-permute-done.7.col_ref = bf16[128,256]{1,0:T(8,128)(2,1)S(1)} collective-permute-done((bf16[128,256]{1,0:T(8,128)(2,1)S(1)}, bf16[128,256]{1,0:T(8,128)(2,1)S(1)}, u32[]{:S(2)}, u32[]{:S(2)}) %collective-permute-start.7) | collective-permute-done | bytes 65568 | tf_op jit(solution)/shard_map/ppermute | solution.py:471
  54.3 0.0 collective-permute-done.6.other_ref
  54.3 0.0 copy-done
  54.3 0.0 copy-done.1
  54.3 0.0 copy-done.9
  54.3 25.4 %pair_last.1 = bf16[256,128,128]{2,1,0:T(8,128)(2,1)} custom-call(s32[128]{0:T(128)S(1)} %copy-done.9, bf16[256,128,128]{2,1,0:T(8,128)(2,1)} %pair_ref.5, bf16[256,128,128]{2,1,0:T(8,128)(2,1)} %pair_early.1.done_ref, bf16[128,1024]{1,0:T(8,128)(2,1)S(1)} %copy-done, bf16[512,128]{1,0:T(8,128)(2,1)S(1)} %copy-done.1, ...), custom_call_target="tpu_custom_call" | custom-call | flops 12884901888 | bytes 16777216 | tf_op jit(solution)/shard_map/pair_last/pallas_call | solution.py:377
  79.7 0.0 collective-permute-done.1
  79.7 0.6 compare_select_fusion
  (5 shorter events, 0.0 us)
Async XLA Ops:
  5.9 18.5 %all-to-all-start = ((bf16[16,128,128]{2,1,0:T(8,128)(2,1)}), bf16[16,128,128]{2,1,0:T(8,128)(2,1)S(1)}, u32[]{:S(2)}, u32[]{:S(2)}) async-start(bf16[16,128,128]{2,1,0:T(8,128)(2,1)} %get-tuple-element.14.band_ref), calls=%async_computation | async-start | bytes 1048576 | tf_op jit(solution)/shard_map/all_to_all | solution.py:460
  13.3 11.0 %copy-start.2 = (bf16[128,128]{1,0:T(8,128)(2,1)S(1)}, bf16[128,128]{1,0:T(8,128)(2,1)}, u32[]{:S(2)}) copy-start(bf16[128,128]{1,0:T(8,128)(2,1)} %own_ref.1) | copy-start | bytes 98308
  13.4 11.0 %copy-start.3 = (bf16[384,256]{1,0:T(8,128)(2,1)S(1)}, bf16[384,256]{1,0:T(8,128)(2,1)}, u32[]{:S(2)}) copy-start(bf16[384,256]{1,0:T(8,128)(2,1)} %wsingle_ref.1) | copy-start | bytes 589828
  13.4 11.0 %copy-start.4 = (bf16[128,512]{1,0:T(8,128)(2,1)S(1)}, bf16[128,512]{1,0:T(8,128)(2,1)}, u32[]{:S(2)}) copy-start(bf16[128,512]{1,0:T(8,128)(2,1)} %wattn_ref.1) | copy-start | bytes 393220
  13.4 11.0 %copy-start.5 = (bf16[128,384]{1,0:T(8,128)(2,1)S(1)}, bf16[128,384]{1,0:T(8,128)(2,1)}, u32[]{:S(2)}) copy-start(bf16[128,384]{1,0:T(8,128)(2,1)} %wagg_ref.1) | copy-start | bytes 294916
  13.4 11.0 %copy-start.6 = (bf16[128,128]{1,0:T(8,128)(2,1)S(1)}, bf16[128,128]{1,0:T(8,128)(2,1)}, u32[]{:S(2)}) copy-start(bf16[128,128]{1,0:T(8,128)(2,1)} %wout_ref.1) | copy-start | bytes 98308
  13.4 11.0 %copy-start.7 = (bf16[16,128]{1,0:T(8,128)(2,1)S(1)}, bf16[16,128]{1,0:T(8,128)(2,1)}, u32[]{:S(2)}) copy-start(bf16[16,128]{1,0:T(8,128)(2,1)} %get-tuple-element.17.tok_ref) | copy-start | bytes 12292
  13.4 11.0 %copy-start.8 = (f32[128]{0:T(128)S(1)}, f32[128]{0:T(128)}, u32[]{:S(2)}) copy-start(f32[128]{0:T(128)} %param.15) | copy-start | bytes 1540
  13.4 40.9 %copy-start = (bf16[128,1024]{1,0:T(8,128)(2,1)S(1)}, bf16[128,1024]{1,0:T(8,128)(2,1)}, u32[]{:S(2)}) copy-start(bf16[128,1024]{1,0:T(8,128)(2,1)} %w_in_ref.3) | copy-start | bytes 786436
  13.4 40.8 %copy-start.1 = (bf16[512,128]{1,0:T(8,128)(2,1)S(1)}, bf16[512,128]{1,0:T(8,128)(2,1)}, u32[]{:S(2)}) copy-start(bf16[512,128]{1,0:T(8,128)(2,1)} %w_out_ref.3) | copy-start | bytes 393220
  13.4 40.8 %copy-start.9 = (s32[128]{0:T(128)S(1)}, s32[128]{0:T(128)}, u32[]{:S(2)}) copy-start(s32[128]{0:T(128)} %constant.4.clone.sender_ref) | copy-start | bytes 1540
  13.5 10.9 %collective-permute-start = (bf16[96,128]{1,0:T(8,128)(2,1)}, bf16[96,128]{1,0:T(8,128)(2,1)S(1)}, u32[]{:S(2)}, u32[]{:S(2)}) collective-permute-start(bf16[96,128]{1,0:T(8,128)(2,1)} %get-tuple-element.15), channel_id=1, source_target_pairs={{15,16},{31,32},{47,48},{63,64},{79,80},{95,96},{111,112},{16,15},... | collective-permute-start | bytes 73736 | tf_op jit(solution)/shard_map/ppermute | solution.py:459
  27.7 1.2 %collective-permute-start.2 = (bf16[16,256]{1,0:T(8,128)(2,1)S(1)}, bf16[16,256]{1,0:T(8,128)(2,1)S(1)}, u32[]{:S(2)}, u32[]{:S(2)}) collective-permute-start(bf16[16,256]{1,0:T(8,128)(2,1)S(1)} %get-tuple-element.21), channel_id=1, source_target_pairs={{0,1},{1,0},{2,3},{3,2},{4,5},{5,4},{6,7},{7,6},{8,9},{9,8},{10,11... | collective-permute-start | bytes 24584 | tf_op jit(solution)/shard_map/ppermute | solution.py:467
  28.9 11.0 %collective-permute-start.3 = (bf16[32,256]{1,0:T(8,128)(2,1)S(1)}, bf16[32,256]{1,0:T(8,128)(2,1)S(1)}, u32[]{:S(2)}, u32[]{:S(2)}) collective-permute-start(bf16[32,256]{1,0:T(8,128)(2,1)S(1)} %get-tuple-element.25), channel_id=1, source_target_pairs={{0,2},{1,3},{2,0},{3,1},{4,6},{5,7},{6,4},{7,5},{8,10},{9,11},{10,... | collective-permute-start | bytes 49160 | tf_op jit(solution)/shard_map/ppermute | solution.py:467
  38.1 6.1 %collective-permute-start.5 = (bf16[32,256]{1,0:T(8,128)(2,1)S(1)}, bf16[32,256]{1,0:T(8,128)(2,1)S(1)}, u32[]{:S(2)}, u32[]{:S(2)}) collective-permute-start(bf16[32,256]{1,0:T(8,128)(2,1)S(1)} %get-tuple-element.25), channel_id=1, source_target_pairs={{0,6},{1,7},{2,4},{3,5},{4,2},{5,3},{6,0},{7,1},{8,14},{9,15},{10,... | collective-permute-start | bytes 49160 | tf_op jit(solution)/shard_map/ppermute | solution.py:467
  38.2 3.7 %collective-permute-start.4 = (bf16[32,256]{1,0:T(8,128)(2,1)S(1)}, bf16[32,256]{1,0:T(8,128)(2,1)S(1)}, u32[]{:S(2)}, u32[]{:S(2)}) collective-permute-start(bf16[32,256]{1,0:T(8,128)(2,1)S(1)} %get-tuple-element.25), channel_id=1, source_target_pairs={{0,4},{1,5},{2,6},{3,7},{4,0},{5,1},{6,2},{7,3},{8,12},{9,13},{10,... | collective-permute-start | bytes 49160 | tf_op jit(solution)/shard_map/ppermute | solution.py:467
  44.3 10.0 %collective-permute-start.7 = (bf16[128,256]{1,0:T(8,128)(2,1)S(1)}, bf16[128,256]{1,0:T(8,128)(2,1)S(1)}, u32[]{:S(2)}, u32[]{:S(2)}) collective-permute-start(bf16[128,256]{1,0:T(8,128)(2,1)S(1)} %constant_dynamic-update-slice_fusion.2.own_ref), channel_id=1, source_target_pairs={{0,16},{1,80},{2,112},{3,96},{4,32},{5,48},{6,0},{7,64},{8,17},{9,... | collective-permute-start | bytes 196616 | tf_op jit(solution)/shard_map/ppermute | solution.py:471
  46.2 8.1 %collective-permute-start.6 = (bf16[128,256]{1,0:T(8,128)(2,1)S(1)}, bf16[128,256]{1,0:T(8,128)(2,1)S(1)}, u32[]{:S(2)}, u32[]{:S(2)}) collective-permute-start(bf16[128,256]{1,0:T(8,128)(2,1)S(1)} %constant_dynamic-update-slice_fusion.2.own_ref), channel_id=1, source_target_pairs={{0,8},{1,9},{2,10},{3,11},{4,12},{5,13},{6,14},{7,15},{8,0},{9,1},... | collective-permute-start | bytes 196616 | tf_op jit(solution)/shard_map/ppermute | solution.py:472
  46.3 33.4 %collective-permute-start.1 = (bf16[128,128]{1,0:T(8,128)(2,1)S(1)}, bf16[128,128]{1,0:T(8,128)(2,1)S(1)}, u32[]{:S(2)}, u32[]{:S(2)}) collective-permute-start(bf16[128,128]{1,0:T(8,128)(2,1)S(1)} %get-tuple-element.20), channel_id=1, source_target_pairs={{0,1},{1,2},{2,3},{3,4},{4,5},{5,6},{6,7},{7,8},{8,9},{9,10},{10,1... | collective-permute-start | bytes 98312 | tf_op jit(solution)/shard_map/ppermute | solution.py:473
